TPU v7x, 256 devices: a whole 4x4x8 slice. The times are simulated.
256 devices in a mesh: tok: 8 (over z), feat: 32 (over x, y, core).
Axes of the slice: x: 4, y: 4, z: 8, core: 2. Of those that a mesh axis runs over, the one named last changes fastest.
Arguments:
- features: float32 [8192, 65536], P('tok', 'feat'), may hold values from -54 to 54
- labels: int32 [8192], P('tok'), may hold values from 0 to 15
- weights: float32 [16, 65536], P(None, 'feat'), may hold values from -0.0234375 to 0.0234375
- right_side: float32 [16, 65536], P(None, 'feat'), may hold values from -6 to 6
Outputs:
- solution: float32 [16, 65536], P(None, 'feat')
- residual: float32 [16, 65536], P(None, 'feat')
All inputs are finite; a program needn't handle non-finite values.
Results may differ from a plain program's by a relative error of at most 0.00035.
Values sent between devices are 32-bit elements; how exact they have to be, the bound alone decides.
No kernel may reach another device: no remote copies, remote signals or barrier semaphores. Data moves between devices by JAX's collectives and lax.ppermute only.
A program may use at most 64 MiB of HBM per device.

v0:
```python
import jax
import jax.numpy as jnp
from jax import lax
from jax.sharding import PartitionSpec as P

ITERS = 2


ridge_strength = 0.25
full_precision = lax.Precision.HIGHEST


def against(left, slab):
    return lax.dot_general(
        left,
        slab,
        (((1,), (1,)), ((), ())),
        precision=full_precision,
        preferred_element_type=jnp.float32,
    )


def on_device(features, labels, weights, right_side):
    classes = weights.shape[0]
    class_ids = jnp.arange(classes, dtype=jnp.int32)
    local_counts = jnp.sum((labels[None, :] == class_ids[:, None]).astype(jnp.float32), axis=1)
    counts = lax.psum(local_counts, "tok")
    picked = (labels[None, :] == class_ids[:, None]).astype(jnp.float32)
    token_scale = 1.0 / (classes * jnp.sum(picked * counts[:, None], axis=0))
    partial_logits = against(weights, features)
    logits = lax.psum(partial_logits, "feat")
    powered = jnp.exp(logits)
    probabilities = powered / jnp.sum(powered, axis=0, keepdims=True)

    def inner_product(left, right):
        return lax.psum(jnp.sum(left * right), "feat")

    residual = right_side
    direction = right_side
    solution = jnp.zeros_like(right_side)
    norm_now = inner_product(residual, residual)
    for iteration in range(ITERS):
        data_projected = lax.psum(against(direction, features), "feat")
        average = jnp.sum(probabilities * data_projected, axis=0, keepdims=True)
        image = (
            lax.psum(
                jnp.dot(
                    token_scale[None, :] * probabilities * (data_projected - average),
                    features,
                    precision=full_precision,
                    preferred_element_type=jnp.float32,
                ),
                "tok",
            )
            + ridge_strength * direction
        )
        step_size = norm_now / inner_product(direction, image)
        solution = solution + step_size * direction
        residual = residual - step_size * image
        if iteration + 1 < ITERS:
            norm_next = inner_product(residual, residual)
            direction = residual + norm_next / norm_now * direction
            norm_now = norm_next
    return (solution, residual)


def solution(mesh):
    placed = (P("tok", "feat"), P("tok"), P(None, "feat"), P(None, "feat"))
    return jax.shard_map(
        on_device,
        mesh=mesh,
        in_specs=placed,
        out_specs=(P(None, "feat"), P(None, "feat")),
        check_vma=False,
    )
```

profile of v0, /device:TPU:32, one launch (start us, length us, event | category | flops | bytes accessed | tf_op | source)
XLA Modules:
  0.0 617.1 jit_solution(17325093910027860707)
XLA Ops:
  7.2 0.0 copy-start
  7.2 0.0 all-reduce.13.cloned.1.call-start
  7.2 0.8 copy-done
  8.1 10.0 %fusion.14 = f32[16,1024]{1,0:T(8,128)} fusion(f32[16,2048]{1,0:T(8,128)S(1)} %copy-done, f32[1024,2048]{1,0:T(8,128)} %param.4), kind=kOutput, calls=%fused_computation.32 | convolution fusion | flops 402653184 | bytes 8585216 | tf_op jit(solution)/shard_map/dot_general | solution.py:14
  18.1 7.6 %fusion.15 = f32[16,1024]{1,0:T(8,128)} fusion(f32[16,2048]{1,0:T(8,128)S(1)} %copy-done.2, f32[1024,2048]{1,0:T(8,128)S(1)} %copy-done.1), kind=kOutput, calls=%fused_computation.33 | convolution fusion | flops 402653184 | bytes 8585216 | tf_op jit(solution)/shard_map/dot_general | solution.py:14
  25.6 0.0 all-reduce.13.cloned.1.call-update
  25.7 0.0 all-reduce.7.cloned.1.call-start
  25.7 0.1 convert_reduce_fusion
  25.8 18.1 %psum.71 = f32[16]{0:T(128)S(1)} all-reduce(f32[16]{0:T(128)S(1)} %convert_reduce_fusion), channel_id=1, replica_groups=mesh['tok'=8,'feat'=32] {'tok'}, use_global_device_ids=true, to_apply=%region_3.0 | all-reduce | flops 16 | bytes 128 | tf_op jit(solution)/shard_map/psum | solution.py:27
  43.9 0.1 select_reduce_fusion
  44.0 94.5 %all-reduce.13.cloned.1.call-done = (f32[16,1024]{1,0:T(8,128)}, f32[16,1024]{1,0:T(8,128)}) async-done(((f32[16,1024]{1,0:T(8,128)}, f32[16,1024]{1,0:T(8,128)}), (f32[16,1024]{1,0:T(8,128)}, f32[16,1024]{1,0:T(8,128)})) %all-reduce.13.cloned.1.call-update) | async-done | bytes 131088 | tf_op jit(solution)/shard_map/psum | solution.py:43
  138.5 0.9 exponential_reduce_fusion
  139.4 0.9 multiply_reduce_fusion.5
  140.3 8.2 %fusion.3 = f32[16,2048]{1,0:T(8,128)} fusion(f32[1024,2048]{1,0:T(8,128)} %param.4, f32[16,1024]{1,0:T(8,128)} %get-tuple-element.6, f32[1024]{0:T(1024)S(1)} %multiply_reduce_fusion.5, f32[1024]{0:T(1024)S(1)} %multiply_divide_fusion, f32[16,1024]{1,0:T(8,128)} %get-tuple-element.7, f32[1024]{0:T(1024)S(1)} %exponential_reduce_fusion), kind=kOutput, calls=%fused_computation.14 | convolution fusion | flops 402718720 | bytes 8663040 | tf_op jit(solution)/shard_map/dot_general | solution.py:47
  148.5 0.0 all-reduce.7.cloned.1.call-update
  148.5 0.0 all-reduce.9.cloned.1.call-start
  148.6 71.2 %all-reduce.7.cloned.1.call-done = f32[16,2048]{1,0:T(8,128)} async-done(((f32[16,2048]{1,0:T(8,128)}), f32[16,2048]{1,0:T(8,128)}) %all-reduce.7.cloned.1.call-update) | async-done | bytes 131088 | tf_op jit(solution)/shard_map/psum | solution.py:46
  219.8 1.5 multiply_reduce_fusion.2
  221.4 63.3 %all-reduce = (f32[]{:T(128)}, f32[]{:T(128)}) all-reduce(f32[]{:T(128)} %get-tuple-element.3, f32[]{:T(128)} %get-tuple-element.2), channel_id=1, replica_groups=mesh['tok'=8,'feat'=32] {'feat'}, use_global_device_ids=true, to_apply=%region_1.0 | all-reduce | flops 2 | bytes 16 | tf_op jit(solution)/shard_map/psum | solution.py:36
  286.0 1.5 multiply_reduce_fusion.1
  287.6 63.4 %psum.76 = f32[]{:T(128)} all-reduce(f32[]{:T(128)} %multiply_reduce_fusion.1), channel_id=1, replica_groups=mesh['tok'=8,'feat'=32] {'feat'}, use_global_device_ids=true, to_apply=%region_13.0 | all-reduce | flops 1 | bytes 8 | tf_op jit(solution)/shard_map/psum | solution.py:36
  352.2 11.0 %fusion.12 = f32[16,1024]{1,0:T(8,128)} fusion(f32[1024,2048]{1,0:T(8,128)} %param.4, f32[16,2048]{1,0:T(8,128)S(1)} %copy-done.2, f32[]{:T(128)S(6)} %div.32, f32[16,2048]{1,0:T(8,128)} %all-reduce.7.cloned.1.call-done, f32[]{:T(128)S(6)} %div.31), kind=kOutput, calls=%fused_computation.29 | convolution fusion | flops 402849792 | bytes 8716296 | tf_op jit(solution)/shard_map/dot_general | solution.py:14
  363.2 0.0 all-reduce.9.cloned.1.call-update
  363.2 0.3 all-reduce.11.cloned.1.call-start
  363.5 99.5 %all-reduce.9.cloned.1.call-done = f32[16,1024]{1,0:T(8,128)} async-done(((f32[16,1024]{1,0:T(8,128)}), f32[16,1024]{1,0:T(8,128)}) %all-reduce.9.cloned.1.call-update) | async-done | bytes 65552 | tf_op jit(solution)/shard_map/psum | solution.py:43
  463.0 0.9 multiply_reduce_fusion.4
  463.8 8.1 %fusion = f32[16,2048]{1,0:T(8,128)} fusion(f32[1024,2048]{1,0:T(8,128)} %param.4, f32[16,1024]{1,0:T(8,128)} %all-reduce.9.cloned.1.call-done, f32[1024]{0:T(1024)S(1)} %multiply_reduce_fusion.4, f32[1024]{0:T(1024)S(1)} %multiply_divide_fusion, f32[16,1024]{1,0:T(8,128)S(1)} %copy-done.4, f32[1024]{0:T(1024)S(1)} %exponential_reduce_fusion), kind=kOutput, calls=%fused_computation.10 | convolution fusion | flops 402718720 | bytes 8663040 | tf_op jit(solution)/shard_map/dot_general | solution.py:47
  472.0 0.0 all-reduce.11.cloned.1.call-update
  472.0 70.7 %all-reduce.11.cloned.1.call-done = f32[16,2048]{1,0:T(8,128)} async-done(((f32[16,2048]{1,0:T(8,128)}), f32[16,2048]{1,0:T(8,128)}) %all-reduce.11.cloned.1.call-update) | async-done | bytes 131088 | tf_op jit(solution)/shard_map/psum | solution.py:46
  542.7 1.6 multiply_reduce_fusion
  544.3 63.3 %psum.79 = f32[]{:T(128)} all-reduce(f32[]{:T(128)} %multiply_reduce_fusion), channel_id=1, replica_groups=mesh['tok'=8,'feat'=32] {'feat'}, use_global_device_ids=true, to_apply=%region_18.0 | all-reduce | flops 1 | bytes 8 | tf_op jit(solution)/shard_map/psum | solution.py:36
  608.9 1.7 multiply_subtract_fusion
  (11 shorter events, 0.0 us)
Async XLA Ops:
  7.2 0.9 copy-start
  7.2 10.9 %copy-start.2 = (f32[16,2048]{1,0:T(8,128)S(1)}, f32[16,2048]{1,0:T(8,128)}, u32[]{:S(2)}) copy-start(f32[16,2048]{1,0:T(8,128)} %param.7) | copy-start | bytes 393220
  7.2 18.5 %copy-start.5 = (s32[1024]{0:T(1024)S(1)}, s32[1024]{0:T(1024)}, u32[]{:S(2)}) copy-start(s32[1024]{0:T(1024)} %param.5) | copy-start | bytes 12292
  7.2 131.3 %all-reduce.13.cloned.1.call-start = ((), (), s32[]{:S(2)}) async-start(), calls=%async_computation.3 | async-start | bytes 262144 | tf_op jit(solution)/shard_map/psum | solution.py:43
  8.1 10.0 %copy-start.1 = (f32[1024,2048]{1,0:T(8,128)S(1)}, f32[1024,2048]{1,0:T(8,128)}, u32[]{:S(2)}) copy-start(f32[1024,2048]{1,0:T(8,128)} %param.4) | copy-start | bytes 25165828
  25.7 194.2 %all-reduce.7.cloned.1.call-start = ((), (), s32[]{:S(2)}) async-start(), calls=%async_computation | async-start | bytes 262144 | tf_op jit(solution)/shard_map/psum | solution.py:46
  140.3 322.6 %copy-start.4 = (f32[16,1024]{1,0:T(8,128)S(1)}, f32[16,1024]{1,0:T(8,128)}, u32[]{:S(2)}) copy-start(f32[16,1024]{1,0:T(8,128)} %get-tuple-element.7) | copy-start | bytes 196612
  148.5 314.4 %all-reduce.9.cloned.1.call-start = ((), (), s32[]{:S(2)}) async-start(), calls=%async_computation.1 | async-start | bytes 131072 | tf_op jit(solution)/shard_map/psum | solution.py:43
  352.2 190.5 %copy-start.3 = (f32[16,2048]{1,0:T(8,128)S(1)}, f32[16,2048]{1,0:T(8,128)}, u32[]{:S(2)}) copy-start(f32[16,2048]{1,0:T(8,128)} %all-reduce.7.cloned.1.call-done) | copy-start | bytes 393220
  363.2 179.5 %all-reduce.11.cloned.1.call-start = ((), (), s32[]{:S(2)}) async-start(), calls=%async_computation.2 | async-start | bytes 262144 | tf_op jit(solution)/shard_map/psum | solution.py:46
Sparse Core Ops, SparseCore 0:
  25.8 112.7 all-reduce.12
  148.7 71.1 all-reduce.6
  363.4 99.5 all-reduce.8
  472.1 70.5 all-reduce.10
where the time goes:
time: 619 us; the launch traced here: 617 us
  waiting for transfers between devices  336 us (54%)
  blocking collectives  208 us (34%)
  matrix products  44.8 us (7%)
  between operations  17.8 us (3%)
  other arithmetic  9.17 us (1%)
    psum x2, waiting for transfers between devices, on_device(): data_projected = lax.psum(against(direction, features), 'feat')  194 us
    psum x3, blocking collectives, inner_product(): return lax.psum(jnp.sum(left * right), 'feat')  190 us
    psum x2, waiting for transfers between devices, on_device(): lax.psum(jnp.dot(token_scale[None, :] * probabilities * (data_projected -...  142 us
    dot_general x3, matrix products, against(): lax.dot_general(left, slab, (((1,), (1,)), ((), ())), precision=full_prec...  28.5 us
    psum x1, blocking collectives, on_device(): counts = lax.psum(local_counts, 'tok')  18.1 us
    dot_general x2, matrix products, on_device(): jnp.dot(token_scale[None, :] * probabilities * (data_projected - average)...  16.3 us
  transfers between devices with their start and end apart: 4, of which 4 were waited for; matrix products, arithmetic and copies ran while one was open for 0% of the time, Pallas kernels for 0%

commit v1 on v0

v1 whole, which is shorter than its diff:
```python
import jax
import jax.numpy as jnp
from jax import lax
from jax.sharding import Mesh, PartitionSpec as P

ridge_strength = 0.25
three_pass = lax.Precision.HIGH


def on_device(features, labels, weights, right_side):
    classes, width = weights.shape
    tokens = features.shape[0]
    half = tokens // 2
    core = lax.axis_index("core")
    toks = lax.axis_size("tok")
    chips = lax.axis_size("chip")
    swap = [(0, 1), (1, 0)]

    def scalars_row(columns, *values):
        row = jnp.stack(values)[None, :]
        return jnp.pad(row, ((0, 7), (0, columns - row.shape[1])))

    def sum_over_feat(part, *values):
        tail = scalars_row(half, *values)
        mine = lax.dynamic_slice_in_dim(part, core * half, half, axis=1)
        other = lax.dynamic_slice_in_dim(part, (1 - core) * half, half, axis=1)
        other = jnp.concatenate([other, tail])
        mine = jnp.concatenate([mine, tail])
        both = mine + lax.ppermute(other, "core", swap)
        spread = jnp.broadcast_to(both[None], (chips,) + both.shape)
        total = jnp.sum(lax.all_to_all(spread, "chip", 0, 0), axis=0)
        rows = part.shape[0]
        return total[:rows], [total[rows, i] for i in range(len(values))]

    def sum_over_tok(part, value):
        step = width // toks
        pieces = part.reshape(classes, toks, step).transpose(1, 0, 2)
        piece = jnp.sum(lax.all_to_all(pieces, "tok", 0, 0), axis=0)
        piece = jnp.concatenate([piece, scalars_row(step, value)])
        spread = jnp.broadcast_to(piece[None], (toks,) + piece.shape)
        pieces = lax.all_to_all(spread, "tok", 0, 0)
        whole = pieces[:, :classes].transpose(1, 0, 2).reshape(classes, width)
        return whole, jnp.sum(pieces[:, classes, 0])

    def product(left, contract):
        return lax.dot_general(
            left, features, (((1,), (contract,)), ((), ())), precision=three_pass, preferred_element_type=jnp.float32
        )

    class_ids = jnp.arange(classes, dtype=jnp.int32)
    onehot = (labels[None, :] == class_ids[:, None]).astype(jnp.float32)
    counts = jnp.sum(onehot, axis=1)
    counts = jnp.broadcast_to(counts[None, :], (8, classes))
    total = counts
    for shift in range(1, toks):
        total = total + lax.ppermute(counts, "tok", [(i, (i + shift) % toks) for i in range(toks)])
    counts = total[0]
    onehot_half = lax.dynamic_slice_in_dim(onehot, core * half, half, axis=1)
    token_scale = 1.0 / (classes * jnp.sum(onehot_half * counts[:, None], axis=0))

    part = product(jnp.concatenate([weights, right_side]), 1)
    total, (norm_now,) = sum_over_feat(part, jnp.sum(right_side * right_side))
    logits, first = total[:classes], total[classes:]
    powered = jnp.exp(logits)
    probabilities = powered / jnp.sum(powered, axis=0, keepdims=True)

    def apply(projected):
        average = jnp.sum(probabilities * projected, axis=0, keepdims=True)
        weighted = token_scale[None, :] * probabilities * (projected - average)
        curve = jnp.sum(projected * weighted)
        packed = jnp.concatenate([weighted, scalars_row(half, curve)])
        other = lax.ppermute(packed, "core", swap)
        low = jnp.where(core == 0, weighted, other[:classes])
        high = jnp.where(core == 0, other[:classes], weighted)
        return sum_over_tok(product(jnp.concatenate([low, high], axis=1), 0), curve + other[classes, 0])

    data, curve = apply(first)
    step_size = norm_now / (curve + ridge_strength * norm_now)
    solution = step_size * right_side
    residual = right_side - step_size * (data + ridge_strength * right_side)

    part = product(residual, 1)
    projected, (norm_next, cross) = sum_over_feat(part, jnp.sum(residual * residual), jnp.sum(residual * right_side))
    ratio = norm_next / norm_now
    direction = residual + ratio * right_side
    data, curve = apply(projected + ratio * first)
    norm_direction = norm_next + ratio * (2.0 * cross + ratio * norm_now)
    step_size = norm_next / (curve + ridge_strength * norm_direction)
    solution = solution + step_size * direction
    residual = residual - step_size * (data + ridge_strength * direction)
    return solution, residual


def solution(mesh):
    toks, feats = mesh.devices.shape
    split = Mesh(mesh.devices.reshape(toks, feats // 2, 2), ("tok", "chip", "core"))
    feat = ("chip", "core")
    return jax.shard_map(
        on_device,
        mesh=split,
        in_specs=(P("tok", feat), P("tok"), P(None, feat), P(None, feat)),
        out_specs=(P(None, feat), P(None, feat)),
        check_vma=False,
    )
```

time: 619 us -> 153 us (0.25)
  waiting for transfers between devices: 336 us -> 34.2 us
  blocking collectives: 208 us -> 18 us
  starting transfers between devices: 0.38 us -> 48 us
  matrix products: 44.8 us -> 25.1 us
  between operations: 17.8 us -> 9.96 us
    psum x4 -> x0, waiting for transfers between devices: 336 us -> none  [the longest x2 194 us: on_device(): data_projected = lax.psum(against(direction, features), 'feat')]
    psum x4 -> x0, blocking collectives: 208 us -> none  [the longest x3 190 us: inner_product(): return lax.psum(jnp.sum(left * right), 'feat')]
    all_to_all x0 -> x5, starting transfers between devices: none -> 29.9 us  [the longest x2 13.3 us: sum_over_tok(): piece = jnp.sum(lax.all_to_all(pieces, 'tok', 0, 0), axis=0)]
    all_to_all x0 -> x5, waiting for transfers between devices: none -> 28 us  [the longest x2 13.7 us: sum_over_tok(): pieces = lax.all_to_all(spread, 'tok', 0, 0)]
    dot_general x5 -> x4, matrix products: 44.8 us -> 25.1 us  [product(): lax.dot_general(left, features, (((1,), (contract,)), ((), ())), precisio...]
    ppermute x0 -> x11, starting transfers between devices: none -> 18.1 us  [the longest x7 17.6 us: on_device(): lax.ppermute(counts, 'tok', [(i, (i + shift) % toks) for i in range(toks)])]
    all_to_all x0 -> x1, blocking collectives: none -> 18 us  [sum_over_feat(): total = jnp.sum(lax.all_to_all(spread, 'chip', 0, 0), axis=0)]
    ppermute x0 -> x11, waiting for transfers between devices: none -> 6.26 us  [the longest x2 2.48 us: sum_over_feat(): both = mine + lax.ppermute(other, 'core', swap)]
  transfers between devices with their start and end apart: 4 -> 16, of which waited for: 4 -> 10; matrix products, arithmetic and copies ran while one was open for 0% -> 1% of each run, Pallas kernels for 0% -> 0%
where the time goes in v1:
time: 153 us; the launch traced here: 152 us
  starting transfers between devices  48 us (31%)
  waiting for transfers between devices  34.2 us (22%)
  matrix products  25.1 us (16%)
  blocking collectives  18 us (12%)
  other arithmetic  10.2 us (7%)
  between operations  9.96 us (7%)
  local copies, waits for them, and re-layouts  6.3 us (4%)
    dot_general x4, matrix products, product(): lax.dot_general(left, features, (((1,), (contract,)), ((), ())), precisio...  25.1 us
    all_to_all x1, blocking collectives, sum_over_feat(): total = jnp.sum(lax.all_to_all(spread, 'chip', 0, 0), axis=0)  18 us
    ppermute x7, starting transfers between devices, on_device(): lax.ppermute(counts, 'tok', [(i, (i + shift) % toks) for i in range(toks)])  17.6 us
    all_to_all x2, waiting for transfers between devices, sum_over_tok(): pieces = lax.all_to_all(spread, 'tok', 0, 0)  13.7 us
    all_to_all x2, starting transfers between devices, sum_over_tok(): piece = jnp.sum(lax.all_to_all(pieces, 'tok', 0, 0), axis=0)  13.3 us
    all_to_all x2, waiting for transfers between devices, sum_over_tok(): piece = jnp.sum(lax.all_to_all(pieces, 'tok', 0, 0), axis=0)  12.4 us
    all_to_all x2, starting transfers between devices, sum_over_tok(): pieces = lax.all_to_all(spread, 'tok', 0, 0)  9.56 us
    all_to_all x1, starting transfers between devices, sum_over_feat(): total = jnp.sum(lax.all_to_all(spread, 'chip', 0, 0), axis=0)  7.04 us
  transfers between devices with their start and end apart: 16, of which 10 were waited for; matrix products, arithmetic and copies ran while one was open for 1% of the time, Pallas kernels for 0%

profile of v1, /device:TPU:32, one launch (start us, length us, event | category | flops | bytes accessed | tf_op | source)
XLA Modules:
  0.0 151.8 jit_solution(5603789701937826536)
XLA Ops:
  0.6 1.5 %multiply_reduce_fusion.2 = f32[]{:T(128)} fusion(f32[16,2048]{1,0:T(8,128)} %param.7), kind=kLoop, calls=%fused_computation.14 | loop fusion | flops 65535 | bytes 131076 | tf_op jit(solution)/shard_map/reduce_sum | solution.py:62
  2.2 7.2 %fusion = f32[32,1024]{1,0:T(8,128)S(1)} fusion(f32[1024,2048]{1,0:T(8,128)} %param.4, f32[16,2048]{1,0:T(8,128)} %param.7, f32[16,2048]{1,0:T(8,128)} %param.6), kind=kOutput, calls=%fused_computation | convolution fusion | flops 402718720 | bytes 8781824 | tf_op jit(solution)/shard_map/dot_general | solution.py:46
  10.3 1.3 collective-permute-done
  12.2 1.2 broadcast_in_dim.12
  13.4 7.0 %all-to-all-start = ((f32[16,40,512]{2,1,0:T(8,128)}), f32[16,40,512]{2,1,0:T(8,128)S(1)}, u32[]{:S(2)}, u32[]{:S(2)}) async-start(f32[16,40,512]{2,1,0:T(8,128)} %broadcast_in_dim.12), calls=%async_computation | async-start | bytes 2621440 | tf_op jit(solution)/shard_map/all_to_all | solution.py:31
  20.6 2.0 %collective-permute-start.1 = (f32[8,16]{1,0:T(8,128)S(1)}, f32[8,16]{1,0:T(8,128)S(1)}, u32[]{:S(2)}, u32[]{:S(2)}) collective-permute-start(f32[8,16]{1,0:T(8,128)S(1)} %broadcast_in_dim.13), channel_id=1, source_target_pairs={{0,32},{32,64},{64,96},{96,128},{128,160},{160,192},{192,224},{224... | collective-permute-start | bytes 1544 | tf_op jit(solution)/shard_map/ppermute | solution.py:56
  22.6 4.5 %collective-permute-start.2 = (f32[8,16]{1,0:T(8,128)S(1)}, f32[8,16]{1,0:T(8,128)S(1)}, u32[]{:S(2)}, u32[]{:S(2)}) collective-permute-start(f32[8,16]{1,0:T(8,128)S(1)} %broadcast_in_dim.13), channel_id=1, source_target_pairs={{0,64},{32,96},{64,128},{96,160},{128,192},{160,224},{192,0},{224,... | collective-permute-start | bytes 1544 | tf_op jit(solution)/shard_map/ppermute | solution.py:56
  27.1 1.9 %collective-permute-start.3 = (f32[8,16]{1,0:T(8,128)S(1)}, f32[8,16]{1,0:T(8,128)S(1)}, u32[]{:S(2)}, u32[]{:S(2)}) collective-permute-start(f32[8,16]{1,0:T(8,128)S(1)} %broadcast_in_dim.13), channel_id=1, source_target_pairs={{0,96},{32,128},{64,160},{96,192},{128,224},{160,0},{192,32},{224,... | collective-permute-start | bytes 1544 | tf_op jit(solution)/shard_map/ppermute | solution.py:56
  29.0 1.4 collective-permute-start.4
  30.4 3.1 %collective-permute-start.5 = (f32[8,16]{1,0:T(8,128)S(1)}, f32[8,16]{1,0:T(8,128)S(1)}, u32[]{:S(2)}, u32[]{:S(2)}) collective-permute-start(f32[8,16]{1,0:T(8,128)S(1)} %broadcast_in_dim.13), channel_id=1, source_target_pairs={{0,160},{32,192},{64,224},{96,0},{128,32},{160,64},{192,96},{224,1... | collective-permute-start | bytes 1544 | tf_op jit(solution)/shard_map/ppermute | solution.py:56
  33.6 2.4 %collective-permute-start.6 = (f32[8,16]{1,0:T(8,128)S(1)}, f32[8,16]{1,0:T(8,128)S(1)}, u32[]{:S(2)}, u32[]{:S(2)}) collective-permute-start(f32[8,16]{1,0:T(8,128)S(1)} %broadcast_in_dim.13), channel_id=1, source_target_pairs={{0,192},{32,224},{64,0},{96,32},{128,64},{160,96},{192,128},{224,1... | collective-permute-start | bytes 1544 | tf_op jit(solution)/shard_map/ppermute | solution.py:56
  35.9 2.2 %collective-permute-start.7 = (f32[8,16]{1,0:T(8,128)S(1)}, f32[8,16]{1,0:T(8,128)S(1)}, u32[]{:S(2)}, u32[]{:S(2)}) collective-permute-start(f32[8,16]{1,0:T(8,128)S(1)} %broadcast_in_dim.13), channel_id=1, source_target_pairs={{0,224},{32,0},{64,32},{96,64},{128,96},{160,128},{192,160},{224,1... | collective-permute-start | bytes 1544 | tf_op jit(solution)/shard_map/ppermute | solution.py:56
  38.2 1.3 collective-permute-done.7
  39.7 1.9 %all-to-all-done = f32[16,40,512]{2,1,0:T(8,128)S(1)} async-done(((f32[16,40,512]{2,1,0:T(8,128)}), f32[16,40,512]{2,1,0:T(8,128)S(1)}, u32[]{:S(2)}, u32[]{:S(2)}) %all-to-all-start) | async-done | bytes 1310752 | tf_op jit(solution)/shard_map/all_to_all | solution.py:31
  43.3 1.2 collective-permute-done.8
  44.5 5.6 %fusion.7 = f32[16,2048]{1,0:T(8,128)S(1)} fusion(f32[1024,2048]{1,0:T(8,128)} %param.4, f32[16,512]{1,0:T(8,128)S(1)} %get-tuple-element.17, f32[16,512]{1,0:T(8,128)S(1)} %get-tuple-element.16), kind=kOutput, calls=%fused_computation.20 | convolution fusion | flops 201342976 | bytes 8585216 | tf_op jit(solution)/shard_map/dot_general | solution.py:46
  50.7 8.6 %all-to-all-start.1 = ((f32[8,16,256]{2,1,0:T(8,128)}), f32[8,16,256]{2,1,0:T(8,128)S(1)}, u32[]{:S(2)}, u32[]{:S(2)}) async-start(f32[8,16,256]{2,1,0:T(8,128)} %bitcast.41), calls=%async_computation.1 | async-start | bytes 262144 | tf_op jit(solution)/shard_map/all_to_all | solution.py:38
  61.2 6.0 %all-to-all-done.1 = f32[8,16,256]{2,1,0:T(8,128)S(1)} async-done(((f32[8,16,256]{2,1,0:T(8,128)}), f32[8,16,256]{2,1,0:T(8,128)S(1)}, u32[]{:S(2)}, u32[]{:S(2)}) %all-to-all-start.1) | async-done | bytes 131104 | tf_op jit(solution)/shard_map/all_to_all | solution.py:38
  68.0 4.8 %all-to-all-start.2 = ((f32[8,24,256]{2,1,0:T(8,128)}), f32[8,24,256]{2,1,0:T(8,128)S(1)}, u32[]{:S(2)}, u32[]{:S(2)}) async-start(f32[8,24,256]{2,1,0:T(8,128)} %broadcast_in_dim.14), calls=%async_computation.2 | async-start | bytes 393216 | tf_op jit(solution)/shard_map/all_to_all | solution.py:41
  73.9 7.2 %all-to-all-done.2 = f32[8,24,256]{2,1,0:T(8,128)S(1)} async-done(((f32[8,24,256]{2,1,0:T(8,128)}), f32[8,24,256]{2,1,0:T(8,128)S(1)}, u32[]{:S(2)}, u32[]{:S(2)}) %all-to-all-start.2) | async-done | bytes 196640 | tf_op jit(solution)/shard_map/all_to_all | solution.py:41
  83.0 6.7 %fusion.25 = f32[16,1024]{1,0:T(8,128)S(1)} fusion(f32[1024,2048]{1,0:T(8,128)} %param.4, f32[16,2048]{1,0:T(8,128)S(1)} %copy-done, f32[16,2048]{1,0:T(8,128)S(1)} %bitcast.42, f32[]{:T(128)S(6)} %div.31), kind=kOutput, calls=%fused_computation.69 | convolution fusion | flops 201457664 | bytes 8716292 | tf_op jit(solution)/shard_map/dot_general | solution.py:46
  89.8 0.8 multiply_reduce_fusion.1
  90.5 1.4 maximum_bitcast_fusion
  92.0 1.2 collective-permute-done.9
  93.3 18.0 %all_to_all.30 = f32[16,24,512]{2,1,0:T(8,128)S(1)} all-to-all(f32[16,24,512]{2,1,0:T(8,128)S(1)} %broadcast_in_dim.16), channel_id=1, replica_groups=mesh['tok'=8,'chip'=16,'core'=2] {'chip'}, dimensions={0} | all-to-all | bytes 1572864 | tf_op jit(solution)/shard_map/all_to_all | solution.py:31
  114.8 1.2 collective-permute-done.10
  116.0 5.6 %fusion.11 = f32[16,2048]{1,0:T(8,128)S(1)} fusion(f32[1024,2048]{1,0:T(8,128)} %param.4, f32[16,512]{1,0:T(8,128)S(1)} %get-tuple-element.15, f32[16,512]{1,0:T(8,128)S(1)} %get-tuple-element.14), kind=kOutput, calls=%fused_computation.24 | convolution fusion | flops 201342976 | bytes 8585216 | tf_op jit(solution)/shard_map/dot_general | solution.py:46
  122.3 4.7 %all-to-all-start.4 = ((f32[8,16,256]{2,1,0:T(8,128)}), f32[8,16,256]{2,1,0:T(8,128)S(1)}, u32[]{:S(2)}, u32[]{:S(2)}) async-start(f32[8,16,256]{2,1,0:T(8,128)} %bitcast.39), calls=%async_computation.4 | async-start | bytes 262144 | tf_op jit(solution)/shard_map/all_to_all | solution.py:38
  128.7 6.4 %all-to-all-done.4 = f32[8,16,256]{2,1,0:T(8,128)S(1)} async-done(((f32[8,16,256]{2,1,0:T(8,128)}), f32[8,16,256]{2,1,0:T(8,128)S(1)}, u32[]{:S(2)}, u32[]{:S(2)}) %all-to-all-start.4) | async-done | bytes 131104 | tf_op jit(solution)/shard_map/all_to_all | solution.py:38
  135.9 4.8 %all-to-all-start.5 = ((f32[8,24,256]{2,1,0:T(8,128)}), f32[8,24,256]{2,1,0:T(8,128)S(1)}, u32[]{:S(2)}, u32[]{:S(2)}) async-start(f32[8,24,256]{2,1,0:T(8,128)} %broadcast_in_dim.17), calls=%async_computation.5 | async-start | bytes 393216 | tf_op jit(solution)/shard_map/all_to_all | solution.py:41
  142.6 6.5 %all-to-all-done.5 = f32[8,24,256]{2,1,0:T(8,128)S(1)} async-done(((f32[8,24,256]{2,1,0:T(8,128)}), f32[8,24,256]{2,1,0:T(8,128)S(1)}, u32[]{:S(2)}, u32[]{:S(2)}) %all-to-all-start.5) | async-done | bytes 196640 | tf_op jit(solution)/shard_map/all_to_all | solution.py:41
  151.0 0.8 multiply_subtract_fusion
  (57 shorter events, 11.4 us)
Async XLA Ops:
  0.6 19.8 %copy-start.1 = (s32[1024]{0:T(1024)S(1)}, s32[1024]{0:T(1024)}, u32[]{:S(2)}) copy-start(s32[1024]{0:T(1024)} %param.5) | copy-start | bytes 12292
  9.5 73.6 %copy-start = (f32[16,2048]{1,0:T(8,128)S(1)}, f32[16,2048]{1,0:T(8,128)}, u32[]{:S(2)}) copy-start(f32[16,2048]{1,0:T(8,128)} %param.7) | copy-start | bytes 393220
  10.2 1.4 collective-permute-start
  13.4 28.2 %all-to-all-start = ((f32[16,40,512]{2,1,0:T(8,128)}), f32[16,40,512]{2,1,0:T(8,128)S(1)}, u32[]{:S(2)}, u32[]{:S(2)}) async-start(f32[16,40,512]{2,1,0:T(8,128)} %broadcast_in_dim.12), calls=%async_computation | async-start | bytes 2621440 | tf_op jit(solution)/shard_map/all_to_all | solution.py:31
  20.6 13.0 %collective-permute-start.1 = (f32[8,16]{1,0:T(8,128)S(1)}, f32[8,16]{1,0:T(8,128)S(1)}, u32[]{:S(2)}, u32[]{:S(2)}) collective-permute-start(f32[8,16]{1,0:T(8,128)S(1)} %broadcast_in_dim.13), channel_id=1, source_target_pairs={{0,32},{32,64},{64,96},{96,128},{128,160},{160,192},{192,224},{224... | collective-permute-start | bytes 1544 | tf_op jit(solution)/shard_map/ppermute | solution.py:56
  22.6 13.4 %collective-permute-start.2 = (f32[8,16]{1,0:T(8,128)S(1)}, f32[8,16]{1,0:T(8,128)S(1)}, u32[]{:S(2)}, u32[]{:S(2)}) collective-permute-start(f32[8,16]{1,0:T(8,128)S(1)} %broadcast_in_dim.13), channel_id=1, source_target_pairs={{0,64},{32,96},{64,128},{96,160},{128,192},{160,224},{192,0},{224,... | collective-permute-start | bytes 1544 | tf_op jit(solution)/shard_map/ppermute | solution.py:56
  27.1 11.1 %collective-permute-start.3 = (f32[8,16]{1,0:T(8,128)S(1)}, f32[8,16]{1,0:T(8,128)S(1)}, u32[]{:S(2)}, u32[]{:S(2)}) collective-permute-start(f32[8,16]{1,0:T(8,128)S(1)} %broadcast_in_dim.13), channel_id=1, source_target_pairs={{0,96},{32,128},{64,160},{96,192},{128,224},{160,0},{192,32},{224,... | collective-permute-start | bytes 1544 | tf_op jit(solution)/shard_map/ppermute | solution.py:56
  29.0 9.2 %collective-permute-start.4 = (f32[8,16]{1,0:T(8,128)S(1)}, f32[8,16]{1,0:T(8,128)S(1)}, u32[]{:S(2)}, u32[]{:S(2)}) collective-permute-start(f32[8,16]{1,0:T(8,128)S(1)} %broadcast_in_dim.13), channel_id=1, source_target_pairs={{0,128},{32,160},{64,192},{96,224},{128,0},{160,32},{192,64},{224,... | collective-permute-start | bytes 1544 | tf_op jit(solution)/shard_map/ppermute | solution.py:56
  30.4 7.8 %collective-permute-start.5 = (f32[8,16]{1,0:T(8,128)S(1)}, f32[8,16]{1,0:T(8,128)S(1)}, u32[]{:S(2)}, u32[]{:S(2)}) collective-permute-start(f32[8,16]{1,0:T(8,128)S(1)} %broadcast_in_dim.13), channel_id=1, source_target_pairs={{0,160},{32,192},{64,224},{96,0},{128,32},{160,64},{192,96},{224,1... | collective-permute-start | bytes 1544 | tf_op jit(solution)/shard_map/ppermute | solution.py:56
  33.6 4.6 %collective-permute-start.6 = (f32[8,16]{1,0:T(8,128)S(1)}, f32[8,16]{1,0:T(8,128)S(1)}, u32[]{:S(2)}, u32[]{:S(2)}) collective-permute-start(f32[8,16]{1,0:T(8,128)S(1)} %broadcast_in_dim.13), channel_id=1, source_target_pairs={{0,192},{32,224},{64,0},{96,32},{128,64},{160,96},{192,128},{224,1... | collective-permute-start | bytes 1544 | tf_op jit(solution)/shard_map/ppermute | solution.py:56
  35.9 3.6 %collective-permute-start.7 = (f32[8,16]{1,0:T(8,128)S(1)}, f32[8,16]{1,0:T(8,128)S(1)}, u32[]{:S(2)}, u32[]{:S(2)}) collective-permute-start(f32[8,16]{1,0:T(8,128)S(1)} %broadcast_in_dim.13), channel_id=1, source_target_pairs={{0,224},{32,0},{64,32},{96,64},{128,96},{160,128},{192,160},{224,1... | collective-permute-start | bytes 1544 | tf_op jit(solution)/shard_map/ppermute | solution.py:56
  43.0 1.5 collective-permute-start.8
  50.7 16.5 %all-to-all-start.1 = ((f32[8,16,256]{2,1,0:T(8,128)}), f32[8,16,256]{2,1,0:T(8,128)S(1)}, u32[]{:S(2)}, u32[]{:S(2)}) async-start(f32[8,16,256]{2,1,0:T(8,128)} %bitcast.41), calls=%async_computation.1 | async-start | bytes 262144 | tf_op jit(solution)/shard_map/all_to_all | solution.py:38
  68.0 13.1 %all-to-all-start.2 = ((f32[8,24,256]{2,1,0:T(8,128)}), f32[8,24,256]{2,1,0:T(8,128)S(1)}, u32[]{:S(2)}, u32[]{:S(2)}) async-start(f32[8,24,256]{2,1,0:T(8,128)} %broadcast_in_dim.14), calls=%async_computation.2 | async-start | bytes 393216 | tf_op jit(solution)/shard_map/all_to_all | solution.py:41
  91.9 1.3 collective-permute-start.9
  114.7 1.3 collective-permute-start.10
  122.3 12.9 %all-to-all-start.4 = ((f32[8,16,256]{2,1,0:T(8,128)}), f32[8,16,256]{2,1,0:T(8,128)S(1)}, u32[]{:S(2)}, u32[]{:S(2)}) async-start(f32[8,16,256]{2,1,0:T(8,128)} %bitcast.39), calls=%async_computation.4 | async-start | bytes 262144 | tf_op jit(solution)/shard_map/all_to_all | solution.py:38
  135.9 13.2 %all-to-all-start.5 = ((f32[8,24,256]{2,1,0:T(8,128)}), f32[8,24,256]{2,1,0:T(8,128)S(1)}, u32[]{:S(2)}, u32[]{:S(2)}) async-start(f32[8,24,256]{2,1,0:T(8,128)} %broadcast_in_dim.17), calls=%async_computation.5 | async-start | bytes 393216 | tf_op jit(solution)/shard_map/all_to_all | solution.py:41

commit v2 on v0

v2 whole, which is shorter than its diff:
```python
import functools
import math

import jax
import jax.numpy as jnp
from jax import lax
from jax.experimental import pallas as pl
from jax.experimental.pallas import tpu as pltpu
from jax.sharding import Mesh, PartitionSpec as P

ridge_strength = 0.25
SUB, LANE = 8, 128
f32, bf16 = jnp.float32, jnp.bfloat16
ROWS_WITH_ROWS = (((1,), (1,)), ((), ()))
ROWS_WITH_COLUMNS = (((1,), (0,)), ((), ()))
ON_CHIP = pl.BlockSpec(memory_space=pltpu.VMEM)
SCALAR = pl.BlockSpec(memory_space=pltpu.SMEM)
IN_HBM = pl.BlockSpec(memory_space=pltpu.HBM)


def call(kernel, name, in_specs, outs, scratch=(), mib=8, cost=None):
    return pl.pallas_call(
        kernel,
        out_shape=outs,
        in_specs=in_specs,
        out_specs=jax.tree.map(lambda _: ON_CHIP, outs),
        scratch_shapes=list(scratch),
        compiler_params=pltpu.CompilerParams(vmem_limit_bytes=mib << 20),
        cost_estimate=cost,
        name=name,
    )


def tiles(*lead):
    return pltpu.VMEM(lead + (SUB, LANE), f32)


def parts(x):
    high = x.astype(bf16)
    return high, (x - high.astype(f32)).astype(bf16)


def total(tile):
    return jnp.sum(tile, axis=(0, 1), keepdims=True)


def class_sum(pair):
    return jnp.sum(pair[0] + pair[1], axis=0, keepdims=True)


def fold(array):
    rows, columns = array.shape
    kept = None
    for r in range(rows // SUB):
        for c in range(columns // LANE):
            tile = array[r * SUB : (r + 1) * SUB, c * LANE : (c + 1) * LANE]
            kept = tile if kept is None else kept + tile
    return kept


def store_half(core_ref, half, value, extra, keep_ref, send_ref):
    rows, columns = value.shape
    across = columns // LANE

    def store(ref):
        for r in range(rows // SUB):
            for c in range(across):
                ref[r * across + c] = value[r * SUB : (r + 1) * SUB, c * LANE : (c + 1) * LANE]
        for i, tile in enumerate(extra):
            ref[(rows // SUB) * across + i] = tile

    @pl.when(core_ref[0] == half)
    def _():
        store(keep_ref)

    @pl.when(core_ref[0] != half)
    def _():
        store(send_ref)


def count_kernel(labels_ref, spread_ref):
    copies, groups = spread_ref.shape[:2]
    ids = lax.broadcasted_iota(jnp.int32, (SUB, LANE), 0)
    for r in range(groups):
        count = jnp.zeros((SUB, LANE), f32)
        for row in range(labels_ref.shape[0]):
            count += (labels_ref[row : row + 1, :] == ids + r * SUB).astype(f32)
        for i in range(copies):
            spread_ref[i, r] = count


def first_kernel(
    step, core_ref, weights_ref, right_ref, features_ref, order_ref, keep_ref, send_ref, left_ref, block_ref, sems
):
    tokens, width = features_ref.shape
    half = tokens // 2
    across = width // step
    copies = []
    for h in range(2):
        for k in range(across):
            i = h * across + k
            copies.append(
                pltpu.make_async_copy(
                    features_ref.at[pl.ds(h * half, half), pl.ds(k * step, step)], block_ref.at[i], sems.at[i]
                )
            )
            copies[-1].start()
    classes = weights_ref.shape[0]
    rows = 2 * classes
    for i, ref in enumerate((weights_ref, right_ref)):
        high, low = parts(ref[...])
        left_ref[i * classes : (i + 1) * classes] = high
        left_ref[rows + i * classes : rows + (i + 1) * classes] = low
    right = right_ref[...]
    norm = fold(right * right)
    for h in range(2):
        both = jnp.zeros((2 * rows, half), f32)
        rest = jnp.zeros((rows, half), f32)
        for k in range(across):
            i = h * across + k
            part = slice(k * step, (k + 1) * step)
            copies[i].wait()
            high, low = parts(block_ref[i])
            both += lax.dot_general(left_ref[:, part], high, ROWS_WITH_ROWS, preferred_element_type=f32)
            rest += lax.dot_general(left_ref[:rows, part], low, ROWS_WITH_ROWS, preferred_element_type=f32)
        store_half(core_ref, h, both[:rows] + both[rows:] + rest, [norm], keep_ref, send_ref)


def spread_kernel(keep_ref, got_ref, spread_ref):
    value = keep_ref[...] + got_ref[...]
    for i in range(spread_ref.shape[0]):
        spread_ref[i] = value


def spread_first_kernel(keep_ref, got_ref, counts_ref, spread_ref, total_ref):
    spread_kernel(keep_ref, got_ref, spread_ref)
    for r in range(total_ref.shape[0]):
        total_ref[r] = jnp.broadcast_to(jnp.sum(summed(counts_ref, r), axis=1, keepdims=True), (SUB, LANE))


def spread_again_kernel(pieces_ref, spread_ref):
    for k in range(pieces_ref.shape[1]):
        tile = summed(pieces_ref, k)
        for i in range(spread_ref.shape[0]):
            spread_ref[i, k] = tile


def gather_kernel(pieces_ref, extra_ref, spread_ref):
    copies, count = pieces_ref.shape[:2]
    for k in range(count):
        tile = pieces_ref[0, k]
        for i in range(1, copies):
            tile += pieces_ref[i, k]
        for i in range(copies):
            spread_ref[i, k] = tile
    for i in range(copies):
        spread_ref[i, count] = extra_ref[...]


def summed(pieces_ref, k):
    tile = pieces_ref[0, k]
    for i in range(1, pieces_ref.shape[0]):
        tile += pieces_ref[i, k]
    return tile


def weigh(c, across, projected, probability, scaled, weighted_ref):
    average = class_sum([projected[r] * probability[r] for r in range(2)])
    curve = jnp.zeros((SUB, LANE), f32)
    for r in range(2):
        value = scaled[r] * (projected[r] - average)
        weighted_ref[r * across + c] = value
        curve += projected[r] * value
    return curve


def softmax_kernel(
    core_ref, labels_ref, counts_ref, pieces_ref, probability_ref, scaled_ref, first_ref, norm_ref, weighted_ref
):
    across = first_ref.shape[0] // 2
    classes = 2 * SUB
    ids = lax.broadcasted_iota(jnp.int32, (SUB, LANE), 0)
    counts = [counts_ref[r] for r in range(2)]
    curve = jnp.zeros((SUB, LANE), f32)
    for c in range(across):
        powered = [jnp.exp(summed(pieces_ref, r * across + c)) for r in range(2)]
        projected = [summed(pieces_ref, (2 + r) * across + c) for r in range(2)]
        whole = class_sum(powered)
        probability = [powered[r] / whole for r in range(2)]
        label = labels_ref[pl.ds(core_ref[0] * across + c, 1), :]
        own = class_sum([jnp.where(label == ids + r * SUB, counts[r], 0.0) for r in range(2)])
        scale = 1.0 / (classes * own)
        scaled = [scale * probability[r] for r in range(2)]
        for r in range(2):
            probability_ref[r * across + c] = probability[r]
            scaled_ref[r * across + c] = scaled[r]
            first_ref[r * across + c] = projected[r]
        curve += weigh(c, across, projected, probability, scaled, weighted_ref)
    weighted_ref[2 * across] = curve
    norm_ref[...] = jnp.broadcast_to(total(summed(pieces_ref, 4 * across)), (SUB, LANE))


def second_kernel(pieces_ref, probability_ref, scaled_ref, first_ref, norm_ref, weighted_ref, numbers_ref):
    across = first_ref.shape[0] // 2
    sums = summed(pieces_ref, 2 * across)
    norm_next, cross = total(sums[:4]), total(sums[4:])
    norm_now = norm_ref[0:1, 0:1]
    ratio = norm_next / norm_now
    curve = jnp.zeros((SUB, LANE), f32)
    for c in range(across):
        projected, probability, scaled = [], [], []
        for r in range(2):
            i = r * across + c
            projected.append(summed(pieces_ref, i) + ratio * first_ref[i])
            probability.append(probability_ref[i])
            scaled.append(scaled_ref[i])
        curve += weigh(c, across, projected, probability, scaled, weighted_ref)
    weighted_ref[2 * across] = curve
    norm_direction = norm_next + ratio * (2.0 * cross + ratio * norm_now)
    for i, value in enumerate((norm_next, ratio, norm_direction)):
        numbers_ref[i] = jnp.broadcast_to(value, (SUB, LANE))


def put_together(core_ref, own_ref, other_ref, curve_ref, left_ref):
    across = (own_ref.shape[0] - 1) // 2
    classes = 2 * SUB
    half = across * LANE
    mine = core_ref[0] == 0
    for r in range(2):
        for c in range(across):
            own, other = own_ref[r * across + c], other_ref[r * across + c]
            for h, value in enumerate((jnp.where(mine, own, other), jnp.where(mine, other, own))):
                high, low = parts(value)
                at = slice(h * half + c * LANE, h * half + (c + 1) * LANE)
                left_ref[r * SUB : (r + 1) * SUB, at] = high.astype(f32)
                left_ref[classes + r * SUB : classes + (r + 1) * SUB, at] = low.astype(f32)
    curve_ref[...] = own_ref[2 * across] + other_ref[2 * across]
    return left_ref[...].astype(bf16)


def image_columns(k, step, left, high_ref, low_ref, pieces_ref):
    classes = left.shape[0] // 2
    share = pieces_ref.shape[1] // 2
    per = share * LANE
    part = slice(k * step, (k + 1) * step)
    both = lax.dot_general(left, high_ref[:, part], ROWS_WITH_COLUMNS, preferred_element_type=f32)
    rest = lax.dot_general(left[:classes], low_ref[:, part], ROWS_WITH_COLUMNS, preferred_element_type=f32)
    value = both[:classes] + both[classes:] + rest
    for z in range(step // per):
        for r in range(2):
            for c in range(share):
                at = z * per + c * LANE
                pieces_ref[k * (step // per) + z, r * share + c] = value[r * SUB : (r + 1) * SUB, at : at + LANE]


def image_kernel(step, core_ref, own_ref, other_ref, high_ref, low_ref, pieces_ref, curve_ref, left_ref):
    left = put_together(core_ref, own_ref, other_ref, curve_ref, left_ref)
    for k in range(high_ref.shape[1] // step):
        image_columns(k, step, left, high_ref, low_ref, pieces_ref)


def image_first_kernel(
    step, core_ref, own_ref, other_ref, features_ref, pieces_ref, curve_ref, high_ref, low_ref, left_ref, block_ref, sems
):
    copies = []
    for k in range(high_ref.shape[1] // step):
        copies.append(
            pltpu.make_async_copy(features_ref.at[:, pl.ds(k * step, step)], block_ref.at[k], sems.at[k])
        )
        copies[-1].start()
    left = put_together(core_ref, own_ref, other_ref, curve_ref, left_ref)
    for k, copy in enumerate(copies):
        part = slice(k * step, (k + 1) * step)
        copy.wait()
        high_ref[:, part], low_ref[:, part] = parts(block_ref[k])
        image_columns(k, step, left, high_ref, low_ref, pieces_ref)


def columns_of(pieces_ref, z, share, classes):
    rows = []
    for r in range(classes // SUB):
        rows.append(jnp.concatenate([pieces_ref[z, r * share + c] for c in range(share)], axis=1))
    return jnp.concatenate(rows, axis=0)


def residual_kernel(
    core_ref, pieces_ref, norm_ref, right_ref, high_ref, low_ref, keep_ref, send_ref, residual_ref, rate_ref, left_ref
):
    classes, width = right_ref.shape
    toks, count = pieces_ref.shape[:2]
    share = (count - 1) // 2
    per = share * LANE
    norm_now = norm_ref[0:1, 0:1]
    curve = total(summed(pieces_ref, count - 1))
    rate = norm_now / (curve + ridge_strength * norm_now)
    rate_ref[...] = jnp.broadcast_to(rate, (SUB, LANE))
    norm = jnp.zeros((SUB, LANE), f32)
    cross = jnp.zeros((SUB, LANE), f32)
    for z in range(toks):
        at = slice(z * per, (z + 1) * per)
        right = right_ref[:, at]
        residual = right - rate * (columns_of(pieces_ref, z, share, classes) + ridge_strength * right)
        residual_ref[:, at] = residual
        norm += fold(residual * residual)
        cross += fold(residual * right)
        high, low = parts(residual)
        left_ref[:classes, at] = high
        left_ref[classes:, at] = low
    half = high_ref.shape[0] // 2
    left = left_ref[...]
    for h in range(2):
        span = slice(h * half, (h + 1) * half)
        both = lax.dot_general(left, high_ref[span], ROWS_WITH_ROWS, preferred_element_type=f32)
        rest = lax.dot_general(left[:classes], low_ref[span], ROWS_WITH_ROWS, preferred_element_type=f32)
        store_half(core_ref, h, both[:classes] + both[classes:] + rest, [jnp.concatenate([norm[:4] + norm[4:], cross[:4] + cross[4:]])], keep_ref, send_ref)


def last_kernel(pieces_ref, numbers_ref, rate_ref, right_ref, old_ref, solution_ref, residual_ref):
    classes, width = right_ref.shape
    toks, count = pieces_ref.shape[:2]
    share = (count - 1) // 2
    per = share * LANE
    norm_next, ratio, norm_direction = [numbers_ref[i, 0:1, 0:1] for i in range(3)]
    curve = total(summed(pieces_ref, count - 1))
    rate = norm_next / (curve + ridge_strength * norm_direction)
    rate_first = rate_ref[0:1, 0:1]
    for z in range(toks):
        at = slice(z * per, (z + 1) * per)
        right, old = right_ref[:, at], old_ref[:, at]
        direction = old + ratio * right
        image = columns_of(pieces_ref, z, share, classes) + ridge_strength * direction
        solution_ref[:, at] = rate_first * right + rate * direction
        residual_ref[:, at] = old - rate * image


def on_device(features, labels, weights, right_side):
    classes, width = weights.shape
    tokens = features.shape[0]
    half = tokens // 2
    across = half // LANE
    groups = classes // SUB
    toks = lax.axis_size("tok")
    across_x, across_y = lax.axis_size("x"), lax.axis_size("y")
    chips = across_x * across_y
    share = width // toks // LANE
    core = lax.axis_index("core").astype(jnp.int32).reshape(1)
    labels = labels.reshape(tokens // LANE, LANE)
    swap = [(0, 1), (1, 0)]
    step = min(512, width)

    spread = call(count_kernel, "count", [ON_CHIP], tiles(toks, groups))(labels)
    counts = lax.all_to_all(spread, "tok", 0, 0)

    def sum_over_feat(keep, send):
        got = lax.ppermute(send, "core", swap)
        spread = call(spread_kernel, "spread", [ON_CHIP] * 2, tiles(chips, *keep.shape[:1]))(keep, got)
        return lax.all_to_all(spread, ("x", "y"), 0, 0)

    def sum_over_tok(pieces, curve):
        pieces = lax.all_to_all(pieces, "tok", 0, 0)
        spread = call(gather_kernel, "gather", [ON_CHIP] * 2, tiles(toks, groups * share + 1))(pieces, curve)
        return lax.all_to_all(spread, "tok", 0, 0)

    image_outs = [tiles(toks, groups * share), tiles()]
    put = pltpu.VMEM((2 * classes, tokens), f32)
    whole = pltpu.VMEM((tokens, width), bf16)

    kept = 2 * groups * across + 1
    blocks = 2 * (width // step)
    keep, send = call(
        functools.partial(first_kernel, step),
        "first",
        [SCALAR, ON_CHIP, ON_CHIP, IN_HBM, ON_CHIP],
        [tiles(kept), tiles(kept)],
        [
            pltpu.VMEM((4 * classes, width), bf16),
            pltpu.VMEM((blocks, half, step), f32),
            pltpu.SemaphoreType.DMA((blocks,)),
        ],
        mib=48,
        cost=pl.CostEstimate(
            flops=12 * classes * tokens * width, bytes_accessed=4 * tokens * width, transcendentals=0
        ),
    )(core, weights, right_side, features, spread)
    got = lax.ppermute(send, "core", swap)
    spread, counts = call(
        spread_first_kernel, "spread_x", [ON_CHIP] * 3, [tiles(across_x, kept), tiles(groups)]
    )(keep, got, counts)
    pieces = lax.all_to_all(spread, "x", 0, 0)
    spread = call(spread_again_kernel, "spread_y", [ON_CHIP], tiles(across_y, kept))(pieces)
    pieces = lax.all_to_all(spread, "y", 0, 0)
    probability, scaled, first, norm_now, weighted = call(
        softmax_kernel,
        "softmax",
        [SCALAR] + [ON_CHIP] * 3,
        [tiles(groups * across)] * 3 + [tiles(), tiles(groups * across + 1)],
    )(core, labels, counts, pieces)
    pieces, curve, high, low = call(
        functools.partial(image_first_kernel, step),
        "image_first",
        [SCALAR] + [ON_CHIP] * 2 + [IN_HBM],
        image_outs + [whole, whole],
        [put, pltpu.VMEM((width // step, tokens, step), f32), pltpu.SemaphoreType.DMA((width // step,))],
        mib=45,
    )(core, weighted, lax.ppermute(weighted, "core", swap), features)
    pieces = sum_over_tok(pieces, curve)

    kept = groups * across + 1
    keep, send, residual, rate = call(
        residual_kernel,
        "residual",
        [SCALAR] + [ON_CHIP] * 5,
        [tiles(kept), tiles(kept), pltpu.VMEM((classes, width), f32), tiles()],
        [pltpu.VMEM((2 * classes, width), bf16)],
    )(core, pieces, norm_now, right_side, high, low)
    pieces = sum_over_feat(keep, send)
    weighted, numbers = call(
        second_kernel, "second", [ON_CHIP] * 5, [tiles(groups * across + 1), tiles(3)]
    )(pieces, probability, scaled, first, norm_now)
    pieces, curve = call(
        functools.partial(image_kernel, step), "image", [SCALAR] + [ON_CHIP] * 4, image_outs, [put]
    )(core, weighted, lax.ppermute(weighted, "core", swap), high, low)
    pieces = sum_over_tok(pieces, curve)
    out = jax.ShapeDtypeStruct((classes, width), f32)
    return tuple(
        call(last_kernel, "last", [ON_CHIP] * 5, [out, out])(pieces, numbers, rate, right_side, residual)
    )


def solution(mesh):
    toks, feats = mesh.devices.shape
    across = math.isqrt(feats // 2)
    split = Mesh(mesh.devices.reshape(toks, across, across, 2), ("tok", "x", "y", "core"))
    feat = ("x", "y", "core")
    return jax.shard_map(
        on_device,
        mesh=split,
        in_specs=(P("tok", feat), P("tok"), P(None, feat), P(None, feat)),
        out_specs=(P(None, feat), P(None, feat)),
        check_vma=False,
    )
```

time: 619 us -> 122 us (0.20)
  waiting for transfers between devices: 336 us -> 4.87 us
  blocking collectives: 208 us -> 88.4 us
  matrix products: 44.8 us -> 0 us
  between operations: 17.8 us -> 0.73 us
  Pallas kernels: 0 us -> 15.3 us
  other arithmetic: 9.17 us -> 0 us
  starting transfers between devices: 0.38 us -> 8.85 us
    psum x4 -> x0, waiting for transfers between devices: 336 us -> none  [the longest x2 194 us: on_device(): data_projected = lax.psum(against(direction, features), 'feat')]
    psum x4 -> x0, blocking collectives: 208 us -> none  [the longest x3 190 us: inner_product(): return lax.psum(jnp.sum(left * right), 'feat')]
    all_to_all x0 -> x7, blocking collectives: none -> 88.4 us  [the longest x2 26.9 us: sum_over_tok(): pieces = lax.all_to_all(pieces, 'tok', 0, 0)]
    dot_general x5 -> x0, matrix products: 44.8 us -> none  [the longest x3 28.5 us: against(): lax.dot_general(left, slab, (((1,), (1,)), ((), ())), precision=full_prec...]
    pallas_call x0 -> x13, Pallas kernels: none -> 15.3 us  [the longest x1 5.4 us: on_device(): call(functools.partial(first_kernel, step), 'first', [SCALAR, ON_CHIP, ON...]
    all_to_all x0 -> x1, starting transfers between devices: none -> 8.57 us  [on_device(): counts = lax.all_to_all(spread, 'tok', 0, 0)]
    reduce_sum x8 -> x0, other arithmetic: 7.5 us -> none  [the longest x3 4.65 us: inner_product(): return lax.psum(jnp.sum(left * right), 'feat')]
  transfers between devices with their start and end apart: 4 -> 5, of which waited for: 4 -> 4; matrix products, arithmetic and copies ran while one was open for 0% -> 0% of each run, Pallas kernels for 0% -> 4%
where the time goes in v2:
time: 122 us; the launch traced here: 121 us
  blocking collectives  88.4 us (72%)
  Pallas kernels  15.3 us (13%)
  starting transfers between devices  8.85 us (7%)
  waiting for transfers between devices  4.87 us (4%)
  local copies, waits for them, and re-layouts  2.5 us (2%)
    all_to_all x2, blocking collectives, sum_over_tok(): pieces = lax.all_to_all(pieces, 'tok', 0, 0)  26.9 us
    all_to_all x2, blocking collectives, sum_over_tok(): return lax.all_to_all(spread, 'tok', 0, 0)  23.7 us
    all_to_all x1, blocking collectives, sum_over_feat(): return lax.all_to_all(spread, ('x', 'y'), 0, 0)  15.5 us
    all_to_all x1, blocking collectives, on_device(): pieces = lax.all_to_all(spread, 'x', 0, 0)  11.2 us
    all_to_all x1, blocking collectives, on_device(): pieces = lax.all_to_all(spread, 'y', 0, 0)  11 us
    all_to_all x1, starting transfers between devices, on_device(): counts = lax.all_to_all(spread, 'tok', 0, 0)  8.57 us
    pallas_call x1, Pallas kernels, on_device(): call(functools.partial(first_kernel, step), 'first', [SCALAR, ON_CHIP, ON...  5.4 us
    pallas_call x1, Pallas kernels, on_device(): call(functools.partial(image_first_kernel, step), 'image_first', [SCALAR]...  4.01 us
  transfers between devices with their start and end apart: 5, of which 4 were waited for; matrix products, arithmetic and copies ran while one was open for 0% of the time, Pallas kernels for 4%

profile of v2, /device:TPU:32, one launch (start us, length us, event | category | flops | bytes accessed | tf_op | source)
XLA Modules:
  0.0 120.7 jit_solution(10248892088335502333)
XLA Ops:
  0.6 0.0 copy-start.3
  0.6 0.7 copy-done.3
  1.3 0.6 count.1.order_ref
  2.0 8.6 %all-to-all-start = ((f32[8,2,8,128]{3,2,1,0:T(8,128)}), f32[8,2,8,128]{3,2,1,0:T(8,128)S(1)}, u32[]{:S(2)}, u32[]{:S(2)}) async-start(f32[8,2,8,128]{3,2,1,0:T(8,128)} %count.1.order_ref), calls=%async_computation | async-start | bytes 131072 | tf_op jit(solution)/shard_map/all_to_all | solution.py:352
  10.5 0.9 copy-done
  11.4 0.9 copy-done.2
  12.3 5.4 %first.1 = (f32[17,8,128]{2,1,0:T(8,128)S(1)}, f32[17,8,128]{2,1,0:T(8,128)S(1)}) custom-call(s32[1]{0:T(128)} %bitcast.core_ref, f32[16,2048]{1,0:T(8,128)S(1)} %copy-done.2, f32[16,2048]{1,0:T(8,128)S(1)} %copy-done, f32[1024,2048]{1,0:T(8,128)} %features_ref.3, f32[8,2,8,128]{3,2,1,0:T(8,128)} %count.1.order_ref), custom_call_target="tpu_custom_call" | custom-call | flops 402653184 | bytes 8388608 | tf_op jit(solution)/shard_map/first/pallas_call | solution.py:370
  17.7 0.1 collective-permute-start
  17.8 1.2 %collective-permute-done.got_ref = f32[17,8,128]{2,1,0:T(8,128)S(1)} collective-permute-done((f32[17,8,128]{2,1,0:T(8,128)S(1)}, f32[17,8,128]{2,1,0:T(8,128)S(1)}, u32[]{:S(2)}, u32[]{:S(2)}) %collective-permute-start) | collective-permute-done | bytes 69664 | tf_op jit(solution)/shard_map/ppermute | solution.py:385
  19.1 0.0 all-to-all-done.counts_ref
  19.1 0.1 spread_x.1
  19.2 11.2 %all_to_all.40.pieces_ref = f32[4,17,8,128]{3,2,1,0:T(8,128)S(1)} all-to-all(f32[4,17,8,128]{3,2,1,0:T(8,128)S(1)} %get-tuple-element.26), channel_id=1, replica_groups=mesh['tok'=8,'x'=4,'y'=4,'core'=2] {'x'}, dimensions={0} | all-to-all | bytes 557056 | tf_op jit(solution)/shard_map/all_to_all | solution.py:389
  30.5 11.0 %all_to_all.41.pieces_ref = f32[4,17,8,128]{3,2,1,0:T(8,128)S(1)} all-to-all(f32[4,17,8,128]{3,2,1,0:T(8,128)S(1)} %spread_y.1), channel_id=1, replica_groups=mesh['tok'=8,'x'=4,'y'=4,'core'=2] {'y'}, dimensions={0} | all-to-all | bytes 557056 | tf_op jit(solution)/shard_map/all_to_all | solution.py:391
  41.5 0.0 copy-done.4
  41.5 0.1 softmax.1
  41.6 0.0 copy-start.1
  41.7 0.1 collective-permute-start.1
  41.8 1.2 collective-permute-done.1.other_ref
  43.0 4.0 %image_first.1 = (f32[8,4,8,128]{3,2,1,0:T(8,128)S(1)}, f32[8,128]{1,0:T(8,128)S(1)}, bf16[1024,2048]{1,0:T(8,128)(2,1)S(1)}, bf16[1024,2048]{1,0:T(8,128)(2,1)S(1)}) custom-call(s32[1]{0:T(128)} %bitcast.core_ref, f32[9,8,128]{2,1,0:T(8,128)S(1)} %get-tuple-element.27.own_ref, f32[9,8,128]{2,1,0:T(8,128)S(1)} %collective-permute-done.1.other_ref, ...), custom_call_target="tpu_custom_call" | custom-call | tf_op jit(solution)/shard_map/image_first/pallas_call | solution.py:398
  47.0 14.9 %all_to_all.42.pieces_ref = f32[8,4,8,128]{3,2,1,0:T(8,128)S(1)} all-to-all(f32[8,4,8,128]{3,2,1,0:T(8,128)S(1)} %get-tuple-element.28), channel_id=1, replica_groups=mesh['tok'=8,'x'=4,'y'=4,'core'=2] {'tok'}, dimensions={0} | all-to-all | bytes 262144 | tf_op jit(solution)/shard_map/all_to_all | solution.py:360
  61.9 11.8 %all_to_all.43.pieces_ref = f32[8,5,8,128]{3,2,1,0:T(8,128)S(1)} all-to-all(f32[8,5,8,128]{3,2,1,0:T(8,128)S(1)} %gather.2), channel_id=1, replica_groups=mesh['tok'=8,'x'=4,'y'=4,'core'=2] {'tok'}, dimensions={0} | all-to-all | bytes 327680 | tf_op jit(solution)/shard_map/all_to_all | solution.py:362
  73.8 2.6 %residual.1 = (f32[9,8,128]{2,1,0:T(8,128)S(1)}, f32[9,8,128]{2,1,0:T(8,128)S(1)}, f32[16,2048]{1,0:T(8,128)S(1)}, f32[8,128]{1,0:T(8,128)S(1)}) custom-call(s32[1]{0:T(128)} %bitcast.core_ref, f32[8,5,8,128]{3,2,1,0:T(8,128)S(1)} %all_to_all.43.pieces_ref, f32[8,128]{1,0:T(8,128)S(1)} %get-tuple-element.30.norm_ref, f32[16,2048]{1,0:T(8,128)S(1)} %copy-done.1, ...), custom_call_target="tpu_custom_call" | custom-call | tf_op jit(solution)/shard_map/residual/pallas_call | solution.py:409
  76.4 0.0 collective-permute-start.2
  76.4 1.2 %collective-permute-done.2.got_ref = f32[9,8,128]{2,1,0:T(8,128)S(1)} collective-permute-done((f32[9,8,128]{2,1,0:T(8,128)S(1)}, f32[9,8,128]{2,1,0:T(8,128)S(1)}, u32[]{:S(2)}, u32[]{:S(2)}) %collective-permute-start.2) | collective-permute-done | bytes 36896 | tf_op jit(solution)/shard_map/ppermute | solution.py:355
  77.6 15.5 %all_to_all.44.pieces_ref = f32[16,9,8,128]{3,2,1,0:T(8,128)S(1)} all-to-all(f32[16,9,8,128]{3,2,1,0:T(8,128)S(1)} %spread.1), channel_id=1, replica_groups=mesh['tok'=8,'x'=4,'y'=4,'core'=2] {'x','y'}, dimensions={0} | all-to-all | bytes 1179648 | tf_op jit(solution)/shard_map/all_to_all | solution.py:357
  93.1 0.2 second.1
  93.3 0.1 collective-permute-start.3
  93.4 1.2 collective-permute-done.3.other_ref
  94.6 1.3 %image.1 = (f32[8,4,8,128]{3,2,1,0:T(8,128)S(1)}, f32[8,128]{1,0:T(8,128)S(1)}) custom-call(s32[1]{0:T(128)} %bitcast.core_ref, f32[9,8,128]{2,1,0:T(8,128)S(1)} %get-tuple-element.38.own_ref, f32[9,8,128]{2,1,0:T(8,128)S(1)} %collective-permute-done.3.other_ref, bf16[1024,2048]{1,0:T(8,128)(2,1)S(1)} %get-tuple-element.31.high_ref, ...), custom_call_target="tpu_custom_call" | custom-call | tf_op jit(solution)/shard_map/image/pallas_call | solution.py:420
  95.9 12.0 %all_to_all.45.pieces_ref = f32[8,4,8,128]{3,2,1,0:T(8,128)S(1)} all-to-all(f32[8,4,8,128]{3,2,1,0:T(8,128)S(1)} %get-tuple-element.39), channel_id=1, replica_groups=mesh['tok'=8,'x'=4,'y'=4,'core'=2] {'tok'}, dimensions={0} | all-to-all | bytes 262144 | tf_op jit(solution)/shard_map/all_to_all | solution.py:360
  108.0 11.9 %all_to_all.46.pieces_ref = f32[8,5,8,128]{3,2,1,0:T(8,128)S(1)} all-to-all(f32[8,5,8,128]{3,2,1,0:T(8,128)S(1)} %gather.3), channel_id=1, replica_groups=mesh['tok'=8,'x'=4,'y'=4,'core'=2] {'tok'}, dimensions={0} | all-to-all | bytes 327680 | tf_op jit(solution)/shard_map/all_to_all | solution.py:362
  119.8 0.9 last.1
  (8 shorter events, 0.1 us)
Async XLA Ops:
  0.6 0.7 copy-start.3
  2.0 17.1 %all-to-all-start = ((f32[8,2,8,128]{3,2,1,0:T(8,128)}), f32[8,2,8,128]{3,2,1,0:T(8,128)S(1)}, u32[]{:S(2)}, u32[]{:S(2)}) async-start(f32[8,2,8,128]{3,2,1,0:T(8,128)} %count.1.order_ref), calls=%async_computation | async-start | bytes 131072 | tf_op jit(solution)/shard_map/all_to_all | solution.py:352
  10.5 0.9 copy-start
  11.4 0.9 copy-start.2
  12.3 29.2 %copy-start.4 = (s32[1024]{0:T(1024)S(1)}, s32[1024]{0:T(1024)}, u32[]{:S(2)}) copy-start(s32[1024]{0:T(1024)} %param.5) | copy-start | bytes 12292
  17.7 1.3 %collective-permute-start = (f32[17,8,128]{2,1,0:T(8,128)S(1)}, f32[17,8,128]{2,1,0:T(8,128)S(1)}, u32[]{:S(2)}, u32[]{:S(2)}) collective-permute-start(f32[17,8,128]{2,1,0:T(8,128)S(1)} %get-tuple-element.24), channel_id=1, source_target_pairs={{0,1},{1,0},{2,3},{3,2},{4,5},{5,4},{6,7},{7,6},{8,9},{9,8},{10,11... | collective-permute-start | bytes 208904 | tf_op jit(solution)/shard_map/ppermute | solution.py:385
  41.6 32.1 %copy-start.1 = (f32[16,2048]{1,0:T(8,128)S(1)}, f32[16,2048]{1,0:T(8,128)}, u32[]{:S(2)}) copy-start(f32[16,2048]{1,0:T(8,128)} %right_ref.5) | copy-start | bytes 393220
  41.7 1.3 %collective-permute-start.1 = (f32[9,8,128]{2,1,0:T(8,128)S(1)}, f32[9,8,128]{2,1,0:T(8,128)S(1)}, u32[]{:S(2)}, u32[]{:S(2)}) collective-permute-start(f32[9,8,128]{2,1,0:T(8,128)S(1)} %get-tuple-element.27.own_ref), channel_id=1, source_target_pairs={{0,1},{1,0},{2,3},{3,2},{4,5},{5,4},{6,7},{7,6},{8,9},{9,8},{10,11... | collective-permute-start | bytes 110600 | tf_op jit(solution)/shard_map/ppermute | solution.py:405
  76.4 1.2 %collective-permute-start.2 = (f32[9,8,128]{2,1,0:T(8,128)S(1)}, f32[9,8,128]{2,1,0:T(8,128)S(1)}, u32[]{:S(2)}, u32[]{:S(2)}) collective-permute-start(f32[9,8,128]{2,1,0:T(8,128)S(1)} %get-tuple-element.34), channel_id=1, source_target_pairs={{0,1},{1,0},{2,3},{3,2},{4,5},{5,4},{6,7},{7,6},{8,9},{9,8},{10,11... | collective-permute-start | bytes 110600 | tf_op jit(solution)/shard_map/ppermute | solution.py:355
  93.3 1.3 %collective-permute-start.3 = (f32[9,8,128]{2,1,0:T(8,128)S(1)}, f32[9,8,128]{2,1,0:T(8,128)S(1)}, u32[]{:S(2)}, u32[]{:S(2)}) collective-permute-start(f32[9,8,128]{2,1,0:T(8,128)S(1)} %get-tuple-element.38.own_ref), channel_id=1, source_target_pairs={{0,1},{1,0},{2,3},{3,2},{4,5},{5,4},{6,7},{7,6},{8,9},{9,8},{10,11... | collective-permute-start | bytes 110600 | tf_op jit(solution)/shard_map/ppermute | solution.py:422

commit v3 on v2

v3 whole, which is shorter than its diff:
```python
import functools
import math

import jax
import jax.numpy as jnp
from jax import lax
from jax.experimental import pallas as pl
from jax.experimental.pallas import tpu as pltpu
from jax.sharding import Mesh, PartitionSpec as P

ridge_strength = 0.25
SUB, LANE = 8, 128
f32, bf16 = jnp.float32, jnp.bfloat16
ROWS_WITH_ROWS = (((1,), (1,)), ((), ()))
ROWS_WITH_COLUMNS = (((1,), (0,)), ((), ()))
ON_CHIP = pl.BlockSpec(memory_space=pltpu.VMEM)
SCALAR = pl.BlockSpec(memory_space=pltpu.SMEM)
IN_HBM = pl.BlockSpec(memory_space=pltpu.HBM)


def call(kernel, name, in_specs, outs, scratch=(), mib=8, kib=0, cost=None):
    return pl.pallas_call(
        kernel,
        out_shape=outs,
        in_specs=in_specs,
        out_specs=jax.tree.map(lambda _: ON_CHIP, outs),
        scratch_shapes=list(scratch),
        compiler_params=pltpu.CompilerParams(vmem_limit_bytes=kib << 10 if kib else mib << 20),
        cost_estimate=cost,
        name=name,
    )


def tiles(*lead):
    return pltpu.VMEM(lead + (SUB, LANE), f32)


def parts(x):
    high = x.astype(bf16)
    return high, (x - high.astype(f32)).astype(bf16)


def total(tile):
    return jnp.sum(tile, axis=(0, 1), keepdims=True)


def class_sum(pair):
    return jnp.sum(pair[0] + pair[1], axis=0, keepdims=True)


def fold(array):
    rows, columns = array.shape
    kept = None
    for r in range(rows // SUB):
        for c in range(columns // LANE):
            tile = array[r * SUB : (r + 1) * SUB, c * LANE : (c + 1) * LANE]
            kept = tile if kept is None else kept + tile
    return kept


def store_tiles(ref, value, extra):
    rows, columns = value.shape
    across = columns // LANE
    for r in range(rows // SUB):
        for c in range(across):
            ref[r * across + c] = value[r * SUB : (r + 1) * SUB, c * LANE : (c + 1) * LANE]
    ref[(rows // SUB) * across] = extra


def summed(pieces_ref, k):
    tile = pieces_ref[0, k]
    for i in range(1, pieces_ref.shape[0]):
        tile += pieces_ref[i, k]
    return tile


def prepare_kernel(
    labels_hbm, weights_hbm, right_hbm, count_ref, norm_ref, left_ref, labels_ref, weights_ref, right_ref, sems
):
    pairs = ((labels_hbm, labels_ref), (weights_hbm, weights_ref), (right_hbm, right_ref))
    copies = [pltpu.make_async_copy(*pair, sems.at[i]) for i, pair in enumerate(pairs)]
    for copy in copies:
        copy.start()
    copies[0].wait()
    ids = lax.broadcasted_iota(jnp.int32, (SUB, LANE), 0)
    for r in range(count_ref.shape[0]):
        count = jnp.zeros((SUB, LANE), f32)
        for row in range(labels_ref.shape[0]):
            count += (labels_ref[row : row + 1, :] == ids + r * SUB).astype(f32)
        count_ref[r] = count
    classes = weights_ref.shape[0]
    rows = 2 * classes
    for i, ref in enumerate((weights_ref, right_ref)):
        copies[i + 1].wait()
        high, low = parts(ref[...])
        left_ref[i * classes : (i + 1) * classes] = high
        left_ref[rows + i * classes : rows + (i + 1) * classes] = low
    right = right_ref[...]
    norm_ref[...] = fold(right * right)


def read_half(row, step, features_ref, block_ref, sems):
    half, width = features_ref.shape[0] // 2, features_ref.shape[1]
    rows = pl.ds(pl.multiple_of(row, half), half)
    copies = []
    for k in range(width // step):
        copies.append(
            pltpu.make_async_copy(features_ref.at[rows, pl.ds(k * step, step)], block_ref.at[k], sems.at[k])
        )
        copies[-1].start()
    return copies


def project_half(copies, step, left_ref, block_ref):
    rows, half = left_ref.shape[0] // 2, block_ref.shape[1]
    both = jnp.zeros((2 * rows, half), f32)
    rest = jnp.zeros((rows, half), f32)
    for k, copy in enumerate(copies):
        part = slice(k * step, (k + 1) * step)
        copy.wait()
        high, low = parts(block_ref[k])
        both += lax.dot_general(left_ref[:, part], high, ROWS_WITH_ROWS, preferred_element_type=f32)
        rest += lax.dot_general(left_ref[:rows, part], low, ROWS_WITH_ROWS, preferred_element_type=f32)
    return both[:rows] + both[rows:] + rest


def first_kernel(step, own, core_ref, left_ref, norm_ref, features_ref, out_ref, block_ref, sems):
    half = features_ref.shape[0] // 2
    which = core_ref[0] if own else 1 - core_ref[0]
    copies = read_half(which * half, step, features_ref, block_ref, sems)
    store_tiles(out_ref, project_half(copies, step, left_ref, block_ref), norm_ref[...])


def spread_kernel(keep_ref, got_ref, spread_ref):
    value = keep_ref[...] + got_ref[...]
    for i in range(spread_ref.shape[0]):
        spread_ref[i] = value


def spread_first_kernel(keep_ref, got_ref, count_ref, other_ref, spread_ref, counts_ref):
    spread_kernel(keep_ref, got_ref, spread_ref)
    for r in range(counts_ref.shape[0]):
        counts_ref[r] = count_ref[r] + other_ref[r]


def middle_kernel(pieces_ref, other_ref, sum_ref):
    count = pieces_ref.shape[1]
    for k in range(count):
        sum_ref[k] = summed(pieces_ref, k)
    for r in range(other_ref.shape[0]):
        sum_ref[count + r] = other_ref[r]


def keep_kernel(
    step,
    core_ref,
    features_ref,
    order_ref,
    high_own_ref,
    low_own_ref,
    high_other_ref,
    low_other_ref,
    done_ref,
    own_block_ref,
    other_block_ref,
    own_sems,
    other_sems,
):
    half = features_ref.shape[0] // 2
    core = core_ref[0]
    own = read_half(core * half, step, features_ref, own_block_ref, own_sems)
    other = read_half((1 - core) * half, step, features_ref, other_block_ref, other_sems)
    for copies, block_ref, high_ref, low_ref in (
        (own, own_block_ref, high_own_ref, low_own_ref),
        (other, other_block_ref, high_other_ref, low_other_ref),
    ):
        for k, copy in enumerate(copies):
            part = slice(k * step, (k + 1) * step)
            copy.wait()
            high_ref[:, part], low_ref[:, part] = parts(block_ref[k])
    done_ref[...] = order_ref[0]


def gather_kernel(pieces_ref, extra_ref, spread_ref):
    copies, count = pieces_ref.shape[:2]
    for k in range(count):
        tile = summed(pieces_ref, k)
        for i in range(copies):
            spread_ref[i, k] = tile
    for i in range(copies):
        spread_ref[i, count] = extra_ref[...]


def weigh(c, across, projected, probability, scaled, weighted_ref):
    average = class_sum([projected[r] * probability[r] for r in range(2)])
    curve = jnp.zeros((SUB, LANE), f32)
    for r in range(2):
        value = scaled[r] * (projected[r] - average)
        weighted_ref[r * across + c] = value
        curve += projected[r] * value
    return curve


def softmax_kernel(
    core_ref,
    labels_ref,
    order_ref,
    own_ref,
    one_ref,
    two_ref,
    three_ref,
    probability_ref,
    scaled_ref,
    first_ref,
    norm_ref,
    weighted_ref,
):
    def whole_sum(k):
        return own_ref[k] + one_ref[k] + two_ref[k] + three_ref[k]

    across = first_ref.shape[0] // 2
    classes = 2 * SUB
    ids = lax.broadcasted_iota(jnp.int32, (SUB, LANE), 0)
    counts = [jnp.sum(whole_sum(4 * across + 1 + r), axis=1, keepdims=True) for r in range(2)]
    curve = jnp.zeros((SUB, LANE), f32)
    for c in range(across):
        powered = [jnp.exp(whole_sum(r * across + c)) for r in range(2)]
        projected = [whole_sum((2 + r) * across + c) for r in range(2)]
        whole = class_sum(powered)
        probability = [powered[r] / whole for r in range(2)]
        label = labels_ref[pl.ds(core_ref[0] * across + c, 1), :]
        own = class_sum([jnp.where(label == ids + r * SUB, counts[r], 0.0) for r in range(2)])
        scale = 1.0 / (classes * own)
        scaled = [scale * probability[r] for r in range(2)]
        for r in range(2):
            probability_ref[r * across + c] = probability[r]
            scaled_ref[r * across + c] = scaled[r]
            first_ref[r * across + c] = projected[r]
        curve += weigh(c, across, projected, probability, scaled, weighted_ref)
    weighted_ref[2 * across] = curve
    norm_ref[...] = jnp.broadcast_to(total(whole_sum(4 * across)), (SUB, LANE))


def second_kernel(pieces_ref, probability_ref, scaled_ref, first_ref, norm_ref, weighted_ref, numbers_ref):
    across = first_ref.shape[0] // 2
    sums = summed(pieces_ref, 2 * across)
    norm_next, cross = total(sums[:4]), total(sums[4:])
    norm_now = norm_ref[0:1, 0:1]
    ratio = norm_next / norm_now
    curve = jnp.zeros((SUB, LANE), f32)
    for c in range(across):
        projected, probability, scaled = [], [], []
        for r in range(2):
            i = r * across + c
            projected.append(summed(pieces_ref, i) + ratio * first_ref[i])
            probability.append(probability_ref[i])
            scaled.append(scaled_ref[i])
        curve += weigh(c, across, projected, probability, scaled, weighted_ref)
    weighted_ref[2 * across] = curve
    norm_direction = norm_next + ratio * (2.0 * cross + ratio * norm_now)
    for i, value in enumerate((norm_next, ratio, norm_direction)):
        numbers_ref[i] = jnp.broadcast_to(value, (SUB, LANE))


def put_together(weighted_ref, left_ref):
    across = (weighted_ref.shape[0] - 1) // 2
    classes = 2 * SUB
    for r in range(2):
        for c in range(across):
            high, low = parts(weighted_ref[r * across + c])
            at = slice(c * LANE, (c + 1) * LANE)
            left_ref[r * SUB : (r + 1) * SUB, at] = high.astype(f32)
            left_ref[classes + r * SUB : classes + (r + 1) * SUB, at] = low.astype(f32)
    return left_ref[...].astype(bf16)


def image_columns(k, step, left, high_ref, low_ref, before_ref, pieces_ref):
    classes = left.shape[0] // 2
    share = pieces_ref.shape[1] // 2
    per = share * LANE
    part = slice(k * step, (k + 1) * step)
    both = lax.dot_general(left, high_ref[:, part], ROWS_WITH_COLUMNS, preferred_element_type=f32)
    rest = lax.dot_general(left[:classes], low_ref[:, part], ROWS_WITH_COLUMNS, preferred_element_type=f32)
    value = both[:classes] + both[classes:] + rest
    for z in range(step // per):
        for r in range(2):
            for c in range(share):
                at = z * per + c * LANE
                tile = value[r * SUB : (r + 1) * SUB, at : at + LANE]
                to = k * (step // per) + z
                if before_ref is not None:
                    tile = tile + before_ref[to, r * share + c]
                pieces_ref[to, r * share + c] = tile


def image_kernel(step, weighted_ref, high_ref, low_ref, before_ref, pieces_ref, left_ref):
    left = put_together(weighted_ref, left_ref)
    for k in range(high_ref.shape[1] // step):
        image_columns(k, step, left, high_ref, low_ref, before_ref, pieces_ref)


def image_own_kernel(step, weighted_ref, high_ref, low_ref, pieces_ref, left_ref):
    image_kernel(step, weighted_ref, high_ref, low_ref, None, pieces_ref, left_ref)


def image_other_kernel(
    step, other_ref, own_ref, high_ref, low_ref, before_ref, pieces_ref, curve_ref, left_ref
):
    last = own_ref.shape[0] - 1
    curve_ref[...] = own_ref[last] + other_ref[last]
    image_kernel(step, other_ref, high_ref, low_ref, before_ref, pieces_ref, left_ref)


def columns_of(pieces_ref, z, share, classes):
    rows = []
    for r in range(classes // SUB):
        rows.append(jnp.concatenate([pieces_ref[z, r * share + c] for c in range(share)], axis=1))
    return jnp.concatenate(rows, axis=0)


def project_kept(left_ref, high_ref, low_ref):
    classes = left_ref.shape[0] // 2
    left = left_ref[...]
    both = lax.dot_general(left, high_ref[...], ROWS_WITH_ROWS, preferred_element_type=f32)
    rest = lax.dot_general(left[:classes], low_ref[...], ROWS_WITH_ROWS, preferred_element_type=f32)
    return both[:classes] + both[classes:] + rest


def residual_other_kernel(
    pieces_ref, norm_ref, right_ref, high_ref, low_ref, send_ref, residual_ref, rate_ref, left_ref
):
    classes, width = right_ref.shape
    toks, count = pieces_ref.shape[:2]
    share = (count - 1) // 2
    per = share * LANE
    norm_now = norm_ref[0:1, 0:1]
    curve = total(summed(pieces_ref, count - 1))
    rate = norm_now / (curve + ridge_strength * norm_now)
    rate_ref[...] = jnp.broadcast_to(rate, (SUB, LANE))
    norm = jnp.zeros((SUB, LANE), f32)
    cross = jnp.zeros((SUB, LANE), f32)
    for z in range(toks):
        at = slice(z * per, (z + 1) * per)
        right = right_ref[:, at]
        residual = right - rate * (columns_of(pieces_ref, z, share, classes) + ridge_strength * right)
        residual_ref[:, at] = residual
        norm += fold(residual * residual)
        cross += fold(residual * right)
        high, low = parts(residual)
        left_ref[:classes, at] = high
        left_ref[classes:, at] = low
    sums = jnp.concatenate([norm[:4] + norm[4:], cross[:4] + cross[4:]])
    store_tiles(send_ref, project_kept(left_ref, high_ref, low_ref), sums)


def residual_own_kernel(left_ref, high_ref, low_ref, send_ref, keep_ref):
    store_tiles(keep_ref, project_kept(left_ref, high_ref, low_ref), send_ref[send_ref.shape[0] - 1])


def last_kernel(pieces_ref, numbers_ref, rate_ref, right_ref, old_ref, solution_ref, residual_ref):
    classes, width = right_ref.shape
    toks, count = pieces_ref.shape[:2]
    share = (count - 1) // 2
    per = share * LANE
    norm_next, ratio, norm_direction = [numbers_ref[i, 0:1, 0:1] for i in range(3)]
    curve = total(summed(pieces_ref, count - 1))
    rate = norm_next / (curve + ridge_strength * norm_direction)
    rate_first = rate_ref[0:1, 0:1]
    for z in range(toks):
        at = slice(z * per, (z + 1) * per)
        right, old = right_ref[:, at], old_ref[:, at]
        direction = old + ratio * right
        image = columns_of(pieces_ref, z, share, classes) + ridge_strength * direction
        solution_ref[:, at] = rate_first * right + rate * direction
        residual_ref[:, at] = old - rate * image


def on_device(features, labels, weights, right_side):
    classes, width = weights.shape
    tokens = features.shape[0]
    half = tokens // 2
    across = half // LANE
    groups = classes // SUB
    toks = lax.axis_size("tok")
    across_x, across_y = lax.axis_size("x"), lax.axis_size("y")
    share = width // toks // LANE
    core = lax.axis_index("core").astype(jnp.int32).reshape(1)
    labels = labels.reshape(tokens // LANE, LANE)
    step = min(512, width)
    swap = [(0, 1), (1, 0)]
    half_product = pl.CostEstimate(
        flops=12 * classes * half * width, bytes_accessed=4 * half * width, transcendentals=0
    )
    reading = [pltpu.VMEM((width // step, half, step), f32), pltpu.SemaphoreType.DMA((width // step,))]
    short = pl.CostEstimate(flops=0, bytes_accessed=1024, transcendentals=0)
    kept_half = pltpu.VMEM((half, width), bf16)
    image_outs = tiles(toks, groups * share)
    put = pltpu.VMEM((2 * classes, half), f32)

    def with_step(kernel):
        return functools.partial(kernel, step)

    def swapped(value):
        return lax.ppermute(value, "core", swap)

    def from_tok(value, distances):
        pairs = [
            ((z + distances[y]) % toks * across_y + y, z * across_y + y)
            for z in range(toks)
            for y in range(across_y)
        ]
        return lax.ppermute(value, ("tok", "y"), pairs)

    def sum_over_tok(pieces, curve):
        pieces = lax.all_to_all(pieces, "tok", 0, 0)
        spread = call(gather_kernel, "gather", [ON_CHIP] * 2, tiles(toks, groups * share + 1))(pieces, curve)
        return lax.all_to_all(spread, "tok", 0, 0)

    near, far = (-1, 2, 2, -1), (0, 1, 2, -2)
    count, norm, left = call(
        prepare_kernel,
        "prepare",
        [IN_HBM] * 3,
        [tiles(groups), tiles(), pltpu.VMEM((4 * classes, width), bf16)],
        [
            pltpu.VMEM(labels.shape, labels.dtype),
            pltpu.VMEM((classes, width), f32),
            pltpu.VMEM((classes, width), f32),
            pltpu.SemaphoreType.DMA((3,)),
        ],
        kib=61700,
    )(labels, weights, right_side)
    other = from_tok(count, near)
    kept = 2 * groups * across + 1

    def first_half(own, name):
        return call(
            functools.partial(first_kernel, step, own),
            name,
            [SCALAR, ON_CHIP, ON_CHIP, IN_HBM],
            tiles(kept),
            reading,
            mib=53,
            cost=short,
        )(core, left, norm, features)

    got = swapped(first_half(False, "first_other"))
    keep = first_half(True, "first_own")
    spread, count = call(
        spread_first_kernel, "spread_x", [ON_CHIP] * 4, [tiles(across_x, kept), tiles(groups)]
    )(keep, got, count, other)
    other = from_tok(count, far)
    pieces = lax.all_to_all(spread, "x", 0, 0)
    own = call(middle_kernel, "middle", [ON_CHIP] * 2, tiles(kept + groups))(pieces, other)
    others = [
        lax.ppermute(own, "y", [(i, (i + d) % across_y) for i in range(across_y)]) for d in range(1, across_y)
    ]
    high_own, low_own, high_other, low_other, done = call(
        with_step(keep_kernel),
        "keep",
        [SCALAR, IN_HBM, ON_CHIP],
        [kept_half] * 4 + [tiles()],
        reading[:1] * 2 + reading[1:] * 2,
        mib=45,
        cost=pl.CostEstimate(flops=0, bytes_accessed=20 * half * width, transcendentals=0),
    )(core, features, own)
    probability, scaled, first, norm_now, weighted = call(
        softmax_kernel,
        "softmax",
        [SCALAR] + [ON_CHIP] * 6,
        [tiles(groups * across)] * 3 + [tiles(), tiles(groups * across + 1)],
    )(core, labels, done, own, *others)

    def image(weighted):
        other = swapped(weighted)
        pieces = call(
            with_step(image_own_kernel), "image_own", [ON_CHIP] * 3, image_outs, [put], cost=half_product
        )(weighted, high_own, low_own)
        return call(
            with_step(image_other_kernel), "image_other", [ON_CHIP] * 5, [image_outs, tiles()], [put]
        )(other, weighted, high_other, low_other, pieces)

    pieces = sum_over_tok(*image(weighted))

    kept = groups * across + 1
    send, residual, rate, left = call(
        residual_other_kernel,
        "residual_other",
        [ON_CHIP] * 5,
        [tiles(kept), pltpu.VMEM((classes, width), f32), tiles(), pltpu.VMEM((2 * classes, width), bf16)],
    )(pieces, norm_now, right_side, high_other, low_other)
    got = swapped(send)
    keep = call(residual_own_kernel, "residual_own", [ON_CHIP] * 4, tiles(kept), cost=half_product)(
        left, high_own, low_own, send
    )
    spread = call(spread_kernel, "spread", [ON_CHIP] * 2, tiles(across_x * across_y, kept))(keep, got)
    pieces = lax.all_to_all(spread, ("x", "y"), 0, 0)
    weighted, numbers = call(second_kernel, "second", [ON_CHIP] * 5, [tiles(kept), tiles(3)])(
        pieces, probability, scaled, first, norm_now
    )

    pieces = sum_over_tok(*image(weighted))
    out = jax.ShapeDtypeStruct((classes, width), f32)
    return tuple(
        call(last_kernel, "last", [ON_CHIP] * 5, [out, out])(pieces, numbers, rate, right_side, residual)
    )


def solution(mesh):
    toks, feats = mesh.devices.shape
    across = math.isqrt(feats // 2)
    split = Mesh(mesh.devices.reshape(toks, across, across, 2), ("tok", "x", "y", "core"))
    feat = ("x", "y", "core")
    return jax.shard_map(
        on_device,
        mesh=split,
        in_specs=(P("tok", feat), P("tok"), P(None, feat), P(None, feat)),
        out_specs=(P(None, feat), P(None, feat)),
        check_vma=False,
    )
```

time: 122 us -> 111 us (0.910)
  blocking collectives: 88.4 us -> 67.7 us
  starting transfers between devices: 8.85 us -> 15.4 us
  waiting for transfers between devices: 4.87 us -> 8.2 us
  Pallas kernels: 15.3 us -> 18.3 us
  local copies, waits for them, and re-layouts: 2.5 us -> 0.01 us
    all_to_all x3 -> x1, blocking collectives: 37.8 us -> 18.5 us  [on_device(): pieces = lax.all_to_all(spread, ('x', 'y'), 0, 0)]
    ppermute x4 -> x9, starting transfers between devices: 0.28 us -> 11.1 us  [the longest x3 8.17 us: on_device(): lax.ppermute(own, 'y', [(i, (i + d) % across_y) for i in range(across_y)])]
    all_to_all x1, waiting for transfers between devices: 0.01 us -> 6.49 us  [on_device(): pieces = lax.all_to_all(spread, 'x', 0, 0)]
    all_to_all x1, starting transfers between devices: 8.57 us -> 4.29 us  [on_device(): pieces = lax.all_to_all(spread, 'x', 0, 0)]
    ppermute x4 -> x9, waiting for transfers between devices: 4.87 us -> 1.71 us  [the longest x4 1 us: swapped(): return lax.ppermute(value, 'core', swap)]
    pallas_call x10 -> x15, Pallas kernels: 14.4 us -> 17.4 us  [the longest x2 5.93 us: first_half(): call(functools.partial(first_kernel, step, own), name, [SCALAR, ON_CHIP,...]
    unnamed x10 -> x4, local copies, waits for them, and re-layouts: 2.5 us -> 0.01 us
    all_to_all x2, blocking collectives: 26.9 us -> 25.5 us  [sum_over_tok(): pieces = lax.all_to_all(pieces, 'tok', 0, 0)]
  transfers between devices with their start and end apart: 5 -> 10, of which waited for: 4 -> 4; matrix products, arithmetic and copies ran while one was open for 0% -> 0% of each run, Pallas kernels for 4% -> 9%
where the time goes in v3:
time: 111 us; the launch traced here: 110 us
  blocking collectives  67.7 us (61%)
  Pallas kernels  18.3 us (16%)
  starting transfers between devices  15.4 us (14%)
  waiting for transfers between devices  8.2 us (7%)
    all_to_all x2, blocking collectives, sum_over_tok(): pieces = lax.all_to_all(pieces, 'tok', 0, 0)  25.5 us
    all_to_all x2, blocking collectives, sum_over_tok(): return lax.all_to_all(spread, 'tok', 0, 0)  23.7 us
    all_to_all x1, blocking collectives, on_device(): pieces = lax.all_to_all(spread, ('x', 'y'), 0, 0)  18.5 us
    ppermute x3, starting transfers between devices, on_device(): lax.ppermute(own, 'y', [(i, (i + d) % across_y) for i in range(across_y)])  8.17 us
    all_to_all x1, waiting for transfers between devices, on_device(): pieces = lax.all_to_all(spread, 'x', 0, 0)  6.49 us
    pallas_call x2, Pallas kernels, first_half(): call(functools.partial(first_kernel, step, own), name, [SCALAR, ON_CHIP,...  5.93 us
    all_to_all x1, starting transfers between devices, on_device(): pieces = lax.all_to_all(spread, 'x', 0, 0)  4.29 us
    pallas_call x1, Pallas kernels, on_device(): call(with_step(keep_kernel), 'keep', [SCALAR, IN_HBM, ON_CHIP], [kept_hal...  3.91 us
  transfers between devices with their start and end apart: 10, of which 4 were waited for; matrix products, arithmetic and copies ran while one was open for 0% of the time, Pallas kernels for 9%

profile of v3, /device:TPU:32, one launch (start us, length us, event | category | flops | bytes accessed | tf_op | source)
XLA Modules:
  0.0 110.4 jit_solution(7817199393683919670)
XLA Ops:
  0.6 1.1 prepare.1
  1.7 3.0 %first_other.1 = f32[17,8,128]{2,1,0:T(8,128)S(1)} custom-call(s32[1]{0:T(128)} %bitcast.core_ref, bf16[64,2048]{1,0:T(8,128)(2,1)S(1)} %get-tuple-element.27.left_ref, f32[8,128]{1,0:T(8,128)S(1)} %get-tuple-element.28.norm_ref, f32[1024,2048]{1,0:T(8,128)} %features_ref.5), custom_call_target="tpu_custom_call" | custom-call | bytes 1024 | tf_op jit(solution)/shard_map/first_other/pallas_call | solution.py:437
  4.7 0.1 collective-permute-start
  4.8 2.0 %collective-permute-start.1 = (f32[2,8,128]{2,1,0:T(8,128)S(1)}, f32[2,8,128]{2,1,0:T(8,128)S(1)}, u32[]{:S(2)}, u32[]{:S(2)}) collective-permute-start(f32[2,8,128]{2,1,0:T(8,128)S(1)} %get-tuple-element.29.count_ref), channel_id=1, source_target_pairs={{224,0},{66,2},{68,4},{230,6},{0,32},{98,34},{100,36},{6,38},{32,6... | collective-permute-start | bytes 24584 | tf_op jit(solution)/shard_map/ppermute | solution.py:412
  6.8 3.0 %first_own.1.keep_ref = f32[17,8,128]{2,1,0:T(8,128)S(1)} custom-call(s32[1]{0:T(128)} %bitcast.core_ref, bf16[64,2048]{1,0:T(8,128)(2,1)S(1)} %get-tuple-element.27.left_ref, f32[8,128]{1,0:T(8,128)S(1)} %get-tuple-element.28.norm_ref, f32[1024,2048]{1,0:T(8,128)} %features_ref.5), custom_call_target="tpu_custom_call" | custom-call | bytes 1024 | tf_op jit(solution)/shard_map/first_own/pallas_call | solution.py:437
  9.8 0.7 spread_x.1
  10.5 4.3 %all-to-all-start = ((f32[4,17,8,128]{3,2,1,0:T(8,128)}), f32[4,17,8,128]{3,2,1,0:T(8,128)S(1)}, u32[]{:S(2)}, u32[]{:S(2)}) async-start(f32[4,17,8,128]{3,2,1,0:T(8,128)} %get-tuple-element.30), calls=%async_computation | async-start | bytes 557056 | tf_op jit(solution)/shard_map/all_to_all | solution.py:453
  14.8 0.6 collective-permute-start.2
  15.5 6.5 %all-to-all-done.pieces_ref = f32[4,17,8,128]{3,2,1,0:T(8,128)S(1)} async-done(((f32[4,17,8,128]{3,2,1,0:T(8,128)}), f32[4,17,8,128]{3,2,1,0:T(8,128)S(1)}, u32[]{:S(2)}, u32[]{:S(2)}) %all-to-all-start) | async-done | bytes 278560 | tf_op jit(solution)/shard_map/all_to_all | solution.py:453
  22.0 3.7 %collective-permute-start.5 = (f32[19,8,128]{2,1,0:T(8,128)S(1)}, f32[19,8,128]{2,1,0:T(8,128)S(1)}, u32[]{:S(2)}, u32[]{:S(2)}) collective-permute-start(f32[19,8,128]{2,1,0:T(8,128)S(1)} %middle.1.order_ref.own_ref), channel_id=1, source_target_pairs={{0,6},{2,0},{4,2},{6,4},{1,7},{3,1},{5,3},{7,5},{8,14},{10,8},{12,... | collective-permute-start | bytes 233480 | tf_op jit(solution)/shard_map/ppermute | solution.py:456
  25.6 3.5 %collective-permute-start.4 = (f32[19,8,128]{2,1,0:T(8,128)S(1)}, f32[19,8,128]{2,1,0:T(8,128)S(1)}, u32[]{:S(2)}, u32[]{:S(2)}) collective-permute-start(f32[19,8,128]{2,1,0:T(8,128)S(1)} %middle.1.order_ref.own_ref), channel_id=1, source_target_pairs={{0,4},{2,6},{4,0},{6,2},{1,5},{3,7},{5,1},{7,3},{8,12},{10,14},{12... | collective-permute-start | bytes 233480 | tf_op jit(solution)/shard_map/ppermute | solution.py:456
  29.2 1.0 collective-permute-start.3
  30.2 3.9 %keep.1 = (bf16[512,2048]{1,0:T(8,128)(2,1)S(1)}, bf16[512,2048]{1,0:T(8,128)(2,1)S(1)}, bf16[512,2048]{1,0:T(8,128)(2,1)S(1)}, bf16[512,2048]{1,0:T(8,128)(2,1)S(1)}, f32[8,128]{1,0:T(8,128)S(1)}) custom-call(s32[1]{0:T(128)} %bitcast.core_ref, f32[1024,2048]{1,0:T(8,128)} %features_ref.5, f32[19,8,128]{2,1,0:T(8,128)S(1)} %middle.1.order_ref.own_ref), custom_call_target="tpu_custom_call" | custom-call | bytes 20971520 | tf_op jit(solution)/shard_map/keep/pallas_call | solution.py:458
  34.1 0.7 collective-permute-done.3.one_ref
  34.8 0.1 softmax.1
  34.9 0.1 collective-permute-start.6
  35.0 0.7 image_own.2.before_ref
  35.7 0.5 collective-permute-done.6.other_ref
  36.2 0.7 image_other.2
  36.9 13.5 %all_to_all.30.pieces_ref = f32[8,4,8,128]{3,2,1,0:T(8,128)S(1)} all-to-all(f32[8,4,8,128]{3,2,1,0:T(8,128)S(1)} %get-tuple-element.38), channel_id=1, replica_groups=mesh['tok'=8,'x'=4,'y'=4,'core'=2] {'tok'}, dimensions={0} | all-to-all | bytes 262144 | tf_op jit(solution)/shard_map/all_to_all | solution.py:415
  50.4 11.8 %all_to_all.31.pieces_ref = f32[8,5,8,128]{3,2,1,0:T(8,128)S(1)} all-to-all(f32[8,5,8,128]{3,2,1,0:T(8,128)S(1)} %gather.2), channel_id=1, replica_groups=mesh['tok'=8,'x'=4,'y'=4,'core'=2] {'tok'}, dimensions={0} | all-to-all | bytes 327680 | tf_op jit(solution)/shard_map/all_to_all | solution.py:417
  62.2 1.3 %residual_other.1 = (f32[9,8,128]{2,1,0:T(8,128)S(1)}, f32[16,2048]{1,0:T(8,128)S(1)}, f32[8,128]{1,0:T(8,128)S(1)}, bf16[32,2048]{1,0:T(8,128)(2,1)S(1)}) custom-call(f32[8,5,8,128]{3,2,1,0:T(8,128)S(1)} %all_to_all.31.pieces_ref, f32[8,128]{1,0:T(8,128)S(1)} %get-tuple-element.40.norm_ref, f32[16,2048]{1,0:T(8,128)S(1)} %copy-done, ...), custom_call_target="tpu_custom_call" | custom-call | tf_op jit(solution)/shard_map/residual_other/pallas_call | solution.py:486
  63.6 1.3 %residual_own.1.keep_ref = f32[9,8,128]{2,1,0:T(8,128)S(1)} custom-call(bf16[32,2048]{1,0:T(8,128)(2,1)S(1)} %get-tuple-element.41.left_ref, bf16[512,2048]{1,0:T(8,128)(2,1)S(1)} %get-tuple-element.36.high_ref, bf16[512,2048]{1,0:T(8,128)(2,1)S(1)} %get-tuple-element.37.low_ref, f32[9,8,128]{2,1,0:T(8,128)S(1)} %get-tuple-element.42.send_ref), custom_call_target="tpu_custom_call" | custom-call | flops 201326592 | bytes 4194304 | tf_op jit(solution)/shard_map/residual_own/pallas_call | solution.py:493
  64.9 18.5 %all_to_all.32.pieces_ref = f32[16,9,8,128]{3,2,1,0:T(8,128)S(1)} all-to-all(f32[16,9,8,128]{3,2,1,0:T(8,128)S(1)} %spread.1), channel_id=1, replica_groups=mesh['tok'=8,'x'=4,'y'=4,'core'=2] {'x','y'}, dimensions={0} | all-to-all | bytes 1179648 | tf_op jit(solution)/shard_map/all_to_all | solution.py:497
  83.4 0.2 second.1
  83.6 0.1 collective-permute-start.8
  83.7 0.7 image_own.3.before_ref
  84.4 0.5 collective-permute-done.8.other_ref
  84.9 0.7 image_other.3
  85.6 12.0 %all_to_all.33.pieces_ref = f32[8,4,8,128]{3,2,1,0:T(8,128)S(1)} all-to-all(f32[8,4,8,128]{3,2,1,0:T(8,128)S(1)} %get-tuple-element.47), channel_id=1, replica_groups=mesh['tok'=8,'x'=4,'y'=4,'core'=2] {'tok'}, dimensions={0} | all-to-all | bytes 262144 | tf_op jit(solution)/shard_map/all_to_all | solution.py:415
  97.7 11.9 %all_to_all.34.pieces_ref = f32[8,5,8,128]{3,2,1,0:T(8,128)S(1)} all-to-all(f32[8,5,8,128]{3,2,1,0:T(8,128)S(1)} %gather.3), channel_id=1, replica_groups=mesh['tok'=8,'x'=4,'y'=4,'core'=2] {'tok'}, dimensions={0} | all-to-all | bytes 327680 | tf_op jit(solution)/shard_map/all_to_all | solution.py:417
  109.5 0.9 last.1
  (15 shorter events, 0.1 us)
Async XLA Ops:
  4.7 5.1 %collective-permute-start = (f32[17,8,128]{2,1,0:T(8,128)S(1)}, f32[17,8,128]{2,1,0:T(8,128)S(1)}, u32[]{:S(2)}, u32[]{:S(2)}) collective-permute-start(f32[17,8,128]{2,1,0:T(8,128)S(1)} %first_other.1), channel_id=1, source_target_pairs={{0,1},{1,0},{2,3},{3,2},{4,5},{5,4},{6,7},{7,6},{8,9},{9,8},{10,11... | collective-permute-start | bytes 208904 | tf_op jit(solution)/shard_map/ppermute | solution.py:404
  4.8 5.0 %collective-permute-start.1 = (f32[2,8,128]{2,1,0:T(8,128)S(1)}, f32[2,8,128]{2,1,0:T(8,128)S(1)}, u32[]{:S(2)}, u32[]{:S(2)}) collective-permute-start(f32[2,8,128]{2,1,0:T(8,128)S(1)} %get-tuple-element.29.count_ref), channel_id=1, source_target_pairs={{224,0},{66,2},{68,4},{230,6},{0,32},{98,34},{100,36},{6,38},{32,6... | collective-permute-start | bytes 24584 | tf_op jit(solution)/shard_map/ppermute | solution.py:412
  10.5 11.5 %all-to-all-start = ((f32[4,17,8,128]{3,2,1,0:T(8,128)}), f32[4,17,8,128]{3,2,1,0:T(8,128)S(1)}, u32[]{:S(2)}, u32[]{:S(2)}) async-start(f32[4,17,8,128]{3,2,1,0:T(8,128)} %get-tuple-element.30), calls=%async_computation | async-start | bytes 557056 | tf_op jit(solution)/shard_map/all_to_all | solution.py:453
  14.8 0.7 collective-permute-start.2
  22.0 12.8 %copy-start.1 = (s32[1024]{0:T(1024)S(1)}, s32[1024]{0:T(1024)}, u32[]{:S(2)}) copy-start(s32[1024]{0:T(1024)} %param.5) | copy-start | bytes 12292
  22.0 12.1 %collective-permute-start.5 = (f32[19,8,128]{2,1,0:T(8,128)S(1)}, f32[19,8,128]{2,1,0:T(8,128)S(1)}, u32[]{:S(2)}, u32[]{:S(2)}) collective-permute-start(f32[19,8,128]{2,1,0:T(8,128)S(1)} %middle.1.order_ref.own_ref), channel_id=1, source_target_pairs={{0,6},{2,0},{4,2},{6,4},{1,7},{3,1},{5,3},{7,5},{8,14},{10,8},{12,... | collective-permute-start | bytes 233480 | tf_op jit(solution)/shard_map/ppermute | solution.py:456
  25.6 8.4 %collective-permute-start.4 = (f32[19,8,128]{2,1,0:T(8,128)S(1)}, f32[19,8,128]{2,1,0:T(8,128)S(1)}, u32[]{:S(2)}, u32[]{:S(2)}) collective-permute-start(f32[19,8,128]{2,1,0:T(8,128)S(1)} %middle.1.order_ref.own_ref), channel_id=1, source_target_pairs={{0,4},{2,6},{4,0},{6,2},{1,5},{3,7},{5,1},{7,3},{8,12},{10,14},{12... | collective-permute-start | bytes 233480 | tf_op jit(solution)/shard_map/ppermute | solution.py:456
  29.2 5.6 %collective-permute-start.3 = (f32[19,8,128]{2,1,0:T(8,128)S(1)}, f32[19,8,128]{2,1,0:T(8,128)S(1)}, u32[]{:S(2)}, u32[]{:S(2)}) collective-permute-start(f32[19,8,128]{2,1,0:T(8,128)S(1)} %middle.1.order_ref.own_ref), channel_id=1, source_target_pairs={{0,2},{2,4},{4,6},{6,0},{1,3},{3,5},{5,7},{7,1},{8,10},{10,12},{12... | collective-permute-start | bytes 233480 | tf_op jit(solution)/shard_map/ppermute | solution.py:456
  34.9 1.3 %collective-permute-start.6 = (f32[9,8,128]{2,1,0:T(8,128)S(1)}, f32[9,8,128]{2,1,0:T(8,128)S(1)}, u32[]{:S(2)}, u32[]{:S(2)}) collective-permute-start(f32[9,8,128]{2,1,0:T(8,128)S(1)} %get-tuple-element.33.weighted_ref.own_ref), channel_id=1, source_target_pairs={{0,1},{1,0},{2,3},{3,2},{4,5},{5,4},{6,7},{7,6},{8,9},{9,8},{10,11... | collective-permute-start | bytes 110600 | tf_op jit(solution)/shard_map/ppermute | solution.py:404
  36.2 26.0 %copy-start = (f32[16,2048]{1,0:T(8,128)S(1)}, f32[16,2048]{1,0:T(8,128)}, u32[]{:S(2)}) copy-start(f32[16,2048]{1,0:T(8,128)} %right_ref.3) | copy-start | bytes 393220
  63.6 1.3 %collective-permute-start.7 = (f32[9,8,128]{2,1,0:T(8,128)S(1)}, f32[9,8,128]{2,1,0:T(8,128)S(1)}, u32[]{:S(2)}, u32[]{:S(2)}) collective-permute-start(f32[9,8,128]{2,1,0:T(8,128)S(1)} %get-tuple-element.42.send_ref), channel_id=1, source_target_pairs={{0,1},{1,0},{2,3},{3,2},{4,5},{5,4},{6,7},{7,6},{8,9},{9,8},{10,11... | collective-permute-start | bytes 110600 | tf_op jit(solution)/shard_map/ppermute | solution.py:404
  83.6 1.3 %collective-permute-start.8 = (f32[9,8,128]{2,1,0:T(8,128)S(1)}, f32[9,8,128]{2,1,0:T(8,128)S(1)}, u32[]{:S(2)}, u32[]{:S(2)}) collective-permute-start(f32[9,8,128]{2,1,0:T(8,128)S(1)} %get-tuple-element.46.weighted_ref.own_ref), channel_id=1, source_target_pairs={{0,1},{1,0},{2,3},{3,2},{4,5},{5,4},{6,7},{7,6},{8,9},{9,8},{10,11... | collective-permute-start | bytes 110600 | tf_op jit(solution)/shard_map/ppermute | solution.py:404

commit v4 on v3

--- a/solution.py
+++ b/solution.py
@@ -74,31 +74,6 @@
     return tile
 
 
-def prepare_kernel(
-    labels_hbm, weights_hbm, right_hbm, count_ref, norm_ref, left_ref, labels_ref, weights_ref, right_ref, sems
-):
-    pairs = ((labels_hbm, labels_ref), (weights_hbm, weights_ref), (right_hbm, right_ref))
-    copies = [pltpu.make_async_copy(*pair, sems.at[i]) for i, pair in enumerate(pairs)]
-    for copy in copies:
-        copy.start()
-    copies[0].wait()
-    ids = lax.broadcasted_iota(jnp.int32, (SUB, LANE), 0)
-    for r in range(count_ref.shape[0]):
-        count = jnp.zeros((SUB, LANE), f32)
-        for row in range(labels_ref.shape[0]):
-            count += (labels_ref[row : row + 1, :] == ids + r * SUB).astype(f32)
-        count_ref[r] = count
-    classes = weights_ref.shape[0]
-    rows = 2 * classes
-    for i, ref in enumerate((weights_ref, right_ref)):
-        copies[i + 1].wait()
-        high, low = parts(ref[...])
-        left_ref[i * classes : (i + 1) * classes] = high
-        left_ref[rows + i * classes : rows + (i + 1) * classes] = low
-    right = right_ref[...]
-    norm_ref[...] = fold(right * right)
-
-
 def read_half(row, step, features_ref, block_ref, sems):
     half, width = features_ref.shape[0] // 2, features_ref.shape[1]
     rows = pl.ds(pl.multiple_of(row, half), half)
@@ -111,74 +86,89 @@
     return copies
 
 
-def project_half(copies, step, left_ref, block_ref):
+def project_half(copies, step, left_ref, block_ref, high_ref, low_ref):
     rows, half = left_ref.shape[0] // 2, block_ref.shape[1]
     both = jnp.zeros((2 * rows, half), f32)
     rest = jnp.zeros((rows, half), f32)
     for k, copy in enumerate(copies):
         part = slice(k * step, (k + 1) * step)
         copy.wait()
-        high, low = parts(block_ref[k])
-        both += lax.dot_general(left_ref[:, part], high, ROWS_WITH_ROWS, preferred_element_type=f32)
-        rest += lax.dot_general(left_ref[:rows, part], low, ROWS_WITH_ROWS, preferred_element_type=f32)
+        high_ref[:, part], low_ref[:, part] = parts(block_ref[k])
+        both += lax.dot_general(left_ref[:, part], high_ref[:, part], ROWS_WITH_ROWS, preferred_element_type=f32)
+        rest += lax.dot_general(left_ref[:rows, part], low_ref[:, part], ROWS_WITH_ROWS, preferred_element_type=f32)
     return both[:rows] + both[rows:] + rest
 
 
-def first_kernel(step, own, core_ref, left_ref, norm_ref, features_ref, out_ref, block_ref, sems):
+def first_other_kernel(
+    step,
+    core_ref,
+    labels_hbm,
+    weights_hbm,
+    right_hbm,
+    features_ref,
+    send_ref,
+    count_ref,
+    left_ref,
+    high_ref,
+    low_ref,
+    labels_ref,
+    weights_ref,
+    right_ref,
+    block_ref,
+    sems,
+    block_sems,
+):
+    pairs = ((weights_hbm, weights_ref), (right_hbm, right_ref), (labels_hbm, labels_ref))
+    loads = [pltpu.make_async_copy(*pair, sems.at[i]) for i, pair in enumerate(pairs)]
+    for load in loads:
+        load.start()
     half = features_ref.shape[0] // 2
-    which = core_ref[0] if own else 1 - core_ref[0]
-    copies = read_half(which * half, step, features_ref, block_ref, sems)
-    store_tiles(out_ref, project_half(copies, step, left_ref, block_ref), norm_ref[...])
-
-
-def spread_kernel(keep_ref, got_ref, spread_ref):
-    value = keep_ref[...] + got_ref[...]
-    for i in range(spread_ref.shape[0]):
-        spread_ref[i] = value
-
-
-def spread_first_kernel(keep_ref, got_ref, count_ref, other_ref, spread_ref, counts_ref):
-    spread_kernel(keep_ref, got_ref, spread_ref)
-    for r in range(counts_ref.shape[0]):
-        counts_ref[r] = count_ref[r] + other_ref[r]
-
-
-def middle_kernel(pieces_ref, other_ref, sum_ref):
-    count = pieces_ref.shape[1]
+    copies = read_half((1 - core_ref[0]) * half, step, features_ref, block_ref, block_sems)
+    classes = weights_ref.shape[0]
+    rows = 2 * classes
+    for i, ref in enumerate((weights_ref, right_ref)):
+        loads[i].wait()
+        high, low = parts(ref[...])
+        left_ref[i * classes : (i + 1) * classes] = high
+        left_ref[rows + i * classes : rows + (i + 1) * classes] = low
+    right = right_ref[...]
+    norm = fold(right * right)
+    loads[2].wait()
+    ids = lax.broadcasted_iota(jnp.int32, (SUB, LANE), 0)
+    for r in range(count_ref.shape[0]):
+        count = jnp.zeros((SUB, LANE), f32)
+        for row in range(labels_ref.shape[0]):
+            count += (labels_ref[row : row + 1, :] == ids + r * SUB).astype(f32)
+        count_ref[r] = count
+    store_tiles(send_ref, project_half(copies, step, left_ref, block_ref, high_ref, low_ref), norm)
+
+
+def first_own_kernel(
+    step, core_ref, left_ref, send_ref, features_ref, keep_ref, high_ref, low_ref, block_ref, sems
+):
+    half = features_ref.shape[0] // 2
+    copies = read_half(core_ref[0] * half, step, features_ref, block_ref, sems)
+    store_tiles(keep_ref, project_half(copies, step, left_ref, block_ref, high_ref, low_ref), send_ref[send_ref.shape[0] - 1])
+
+
+def add_kernel(*refs):
+    value = refs[0][...]
+    for ref in refs[1:-1]:
+        value += ref[...]
+    refs[-1][...] = value
+
+
+def join_kernel(keep_ref, got_ref, count_ref, other_ref, sum_ref, counts_ref):
+    sum_ref[...] = keep_ref[...] + got_ref[...]
+    counts_ref[...] = count_ref[...] + other_ref[...]
+
+
+def middle_kernel(own_ref, one_ref, two_ref, three_ref, other_ref, sum_ref):
+    count = own_ref.shape[0]
     for k in range(count):
-        sum_ref[k] = summed(pieces_ref, k)
+        sum_ref[k] = own_ref[k] + one_ref[k] + two_ref[k] + three_ref[k]
     for r in range(other_ref.shape[0]):
         sum_ref[count + r] = other_ref[r]
-
-
-def keep_kernel(
-    step,
-    core_ref,
-    features_ref,
-    order_ref,
-    high_own_ref,
-    low_own_ref,
-    high_other_ref,
-    low_other_ref,
-    done_ref,
-    own_block_ref,
-    other_block_ref,
-    own_sems,
-    other_sems,
-):
-    half = features_ref.shape[0] // 2
-    core = core_ref[0]
-    own = read_half(core * half, step, features_ref, own_block_ref, own_sems)
-    other = read_half((1 - core) * half, step, features_ref, other_block_ref, other_sems)
-    for copies, block_ref, high_ref, low_ref in (
-        (own, own_block_ref, high_own_ref, low_own_ref),
-        (other, other_block_ref, high_other_ref, low_other_ref),
-    ):
-        for k, copy in enumerate(copies):
-            part = slice(k * step, (k + 1) * step)
-            copy.wait()
-            high_ref[:, part], low_ref[:, part] = parts(block_ref[k])
-    done_ref[...] = order_ref[0]
 
 
 def gather_kernel(pieces_ref, extra_ref, spread_ref):
@@ -204,7 +194,6 @@
 def softmax_kernel(
     core_ref,
     labels_ref,
-    order_ref,
     own_ref,
     one_ref,
     two_ref,
@@ -392,7 +381,6 @@
         flops=12 * classes * half * width, bytes_accessed=4 * half * width, transcendentals=0
     )
     reading = [pltpu.VMEM((width // step, half, step), f32), pltpu.SemaphoreType.DMA((width // step,))]
-    short = pl.CostEstimate(flops=0, bytes_accessed=1024, transcendentals=0)
     kept_half = pltpu.VMEM((half, width), bf16)
     image_outs = tiles(toks, groups * share)
     put = pltpu.VMEM((2 * classes, half), f32)
@@ -417,59 +405,50 @@
         return lax.all_to_all(spread, "tok", 0, 0)
 
     near, far = (-1, 2, 2, -1), (0, 1, 2, -2)
-    count, norm, left = call(
-        prepare_kernel,
-        "prepare",
-        [IN_HBM] * 3,
-        [tiles(groups), tiles(), pltpu.VMEM((4 * classes, width), bf16)],
+    kept = 2 * groups * across + 1
+    send, count, left, high_other, low_other = call(
+        with_step(first_other_kernel),
+        "first_other",
+        [SCALAR] + [IN_HBM] * 4,
+        [tiles(kept), tiles(groups), pltpu.VMEM((4 * classes, width), bf16), kept_half, kept_half],
         [
             pltpu.VMEM(labels.shape, labels.dtype),
             pltpu.VMEM((classes, width), f32),
             pltpu.VMEM((classes, width), f32),
+            reading[0],
             pltpu.SemaphoreType.DMA((3,)),
+            reading[1],
         ],
-        kib=61700,
-    )(labels, weights, right_side)
+        kib=61560 - 4096,
+    )(core, labels, weights, right_side, features)
+    got = swapped(send)
     other = from_tok(count, near)
-    kept = 2 * groups * across + 1
-
-    def first_half(own, name):
-        return call(
-            functools.partial(first_kernel, step, own),
-            name,
-            [SCALAR, ON_CHIP, ON_CHIP, IN_HBM],
-            tiles(kept),
-            reading,
-            mib=53,
-            cost=short,
-        )(core, left, norm, features)
-
-    got = swapped(first_half(False, "first_other"))
-    keep = first_half(True, "first_own")
-    spread, count = call(
-        spread_first_kernel, "spread_x", [ON_CHIP] * 4, [tiles(across_x, kept), tiles(groups)]
-    )(keep, got, count, other)
+    keep, high_own, low_own = call(
+        with_step(first_own_kernel),
+        "first_own",
+        [SCALAR, ON_CHIP, ON_CHIP, IN_HBM],
+        [tiles(kept), kept_half, kept_half],
+        reading,
+        mib=45,
+        cost=half_product,
+    )(core, left, send, features)
+
+    def from_others(value, axis, count):
+        return [
+            lax.ppermute(value, axis, [(i, (i + d) % count) for i in range(count)]) for d in range(1, count)
+        ]
+
+    own, count = call(join_kernel, "join", [ON_CHIP] * 4, [tiles(kept), tiles(groups)])(keep, got, count, other)
+    others = from_others(own, "x", across_x)
     other = from_tok(count, far)
-    pieces = lax.all_to_all(spread, "x", 0, 0)
-    own = call(middle_kernel, "middle", [ON_CHIP] * 2, tiles(kept + groups))(pieces, other)
-    others = [
-        lax.ppermute(own, "y", [(i, (i + d) % across_y) for i in range(across_y)]) for d in range(1, across_y)
-    ]
-    high_own, low_own, high_other, low_other, done = call(
-        with_step(keep_kernel),
-        "keep",
-        [SCALAR, IN_HBM, ON_CHIP],
-        [kept_half] * 4 + [tiles()],
-        reading[:1] * 2 + reading[1:] * 2,
-        mib=45,
-        cost=pl.CostEstimate(flops=0, bytes_accessed=20 * half * width, transcendentals=0),
-    )(core, features, own)
+    own = call(middle_kernel, "middle", [ON_CHIP] * 5, tiles(kept + groups))(own, *others, other)
+    others = from_others(own, "y", across_y)
     probability, scaled, first, norm_now, weighted = call(
         softmax_kernel,
         "softmax",
-        [SCALAR] + [ON_CHIP] * 6,
+        [SCALAR] + [ON_CHIP] * 5,
         [tiles(groups * across)] * 3 + [tiles(), tiles(groups * across + 1)],
-    )(core, labels, done, own, *others)
+    )(core, labels, own, *others)
 
     def image(weighted):
         other = swapped(weighted)
@@ -493,12 +472,12 @@
     keep = call(residual_own_kernel, "residual_own", [ON_CHIP] * 4, tiles(kept), cost=half_product)(
         left, high_own, low_own, send
     )
-    spread = call(spread_kernel, "spread", [ON_CHIP] * 2, tiles(across_x * across_y, kept))(keep, got)
-    pieces = lax.all_to_all(spread, ("x", "y"), 0, 0)
+    own = call(add_kernel, "add", [ON_CHIP] * 2, tiles(kept))(keep, got)
+    own = call(add_kernel, "add_x", [ON_CHIP] * 4, tiles(kept))(own, *from_others(own, "x", across_x))
+    own = call(add_kernel, "add_y", [ON_CHIP] * 4, tiles(kept))(own, *from_others(own, "y", across_y))
     weighted, numbers = call(second_kernel, "second", [ON_CHIP] * 5, [tiles(kept), tiles(3)])(
-        pieces, probability, scaled, first, norm_now
-    )
-
+        own[None], probability, scaled, first, norm_now
+    )
     pieces = sum_over_tok(*image(weighted))
     out = jax.ShapeDtypeStruct((classes, width), f32)
     return tuple(

time: 111 us -> 108 us (0.973)
  blocking collectives: 67.7 us -> 50.1 us
  waiting for transfers between devices: 8.2 us -> 18.9 us
  starting transfers between devices: 15.4 us -> 23.9 us
  Pallas kernels: 18.3 us -> 13.5 us
    all_to_all x1 -> x0, blocking collectives: 18.5 us -> none  [on_device(): pieces = lax.all_to_all(spread, ('x', 'y'), 0, 0)]
    ppermute x3 -> x12, waiting for transfers between devices: 0.7 us -> 17.9 us  [from_others(): lax.ppermute(value, axis, [(i, (i + d) % count) for i in range(count)])]
    ppermute x3 -> x12, starting transfers between devices: 8.17 us -> 20.8 us  [from_others(): lax.ppermute(value, axis, [(i, (i + d) % count) for i in range(count)])]
    all_to_all x1 -> x0, waiting for transfers between devices: 6.49 us -> none  [on_device(): pieces = lax.all_to_all(spread, 'x', 0, 0)]
    pallas_call x8, Pallas kernels: 11.8 us -> 6.96 us  [the longest x1 3.62 us: on_device(): call(with_step(first_other_kernel), 'first_other', [SCALAR] + [IN_HBM] *...]
    all_to_all x1 -> x0, starting transfers between devices: 4.29 us -> none  [on_device(): pieces = lax.all_to_all(spread, 'x', 0, 0)]
  transfers between devices with their start and end apart: 10 -> 18, of which waited for: 4 -> 13; matrix products, arithmetic and copies ran while one was open for 0% -> 0% of each run, Pallas kernels for 9% -> 5%
where the time goes in v4:
time: 108 us; the launch traced here: 107 us
  blocking collectives  50.1 us (46%)
  starting transfers between devices  23.9 us (22%)
  waiting for transfers between devices  18.9 us (17%)
  Pallas kernels  13.5 us (12%)
    all_to_all x2, blocking collectives, sum_over_tok(): pieces = lax.all_to_all(pieces, 'tok', 0, 0)  26.4 us
    all_to_all x2, blocking collectives, sum_over_tok(): return lax.all_to_all(spread, 'tok', 0, 0)  23.7 us
    ppermute x12, starting transfers between devices, from_others(): lax.ppermute(value, axis, [(i, (i + d) % count) for i in range(count)])  20.8 us
    ppermute x12, waiting for transfers between devices, from_others(): lax.ppermute(value, axis, [(i, (i + d) % count) for i in range(count)])  17.9 us
    pallas_call x1, Pallas kernels, on_device(): call(with_step(first_other_kernel), 'first_other', [SCALAR] + [IN_HBM] *...  3.62 us
    pallas_call x1, Pallas kernels, on_device(): call(with_step(first_own_kernel), 'first_own', [SCALAR, ON_CHIP, ON_CHIP,...  3.13 us
    ppermute x2, starting transfers between devices, from_tok(): return lax.ppermute(value, ('tok', 'y'), pairs)  2.64 us
  transfers between devices with their start and end apart: 18, of which 13 were waited for; matrix products, arithmetic and copies ran while one was open for 0% of the time, Pallas kernels for 5%

profile of v4, /device:TPU:32, one launch (start us, length us, event | category | flops | bytes accessed | tf_op | source)
XLA Modules:
  0.0 107.1 jit_solution(2136616536453933519)
XLA Ops:
  0.6 3.6 %first_other.1 = (f32[17,8,128]{2,1,0:T(8,128)S(1)}, f32[2,8,128]{2,1,0:T(8,128)S(1)}, bf16[64,2048]{1,0:T(8,128)(2,1)S(1)}, bf16[512,2048]{1,0:T(8,128)(2,1)S(1)}, bf16[512,2048]{1,0:T(8,128)(2,1)S(1)}) custom-call(s32[1]{0:T(128)} %bitcast.core_ref, s32[8,128]{1,0:T(8,128)} %bitcast.4, f32[16,2048]{1,0:T(8,128)} %weights_hbm.1, f32[16,2048]{1,0:T(8,128)} %right_ref.3, ...), custom_call_target="tpu_custom_call" | custom-call | tf_op jit(solution)/shard_map/first_other/pallas_call | solution.py:409
  4.4 2.0 %collective-permute-start.1 = (f32[2,8,128]{2,1,0:T(8,128)S(1)}, f32[2,8,128]{2,1,0:T(8,128)S(1)}, u32[]{:S(2)}, u32[]{:S(2)}) collective-permute-start(f32[2,8,128]{2,1,0:T(8,128)S(1)} %get-tuple-element.30.count_ref), channel_id=1, source_target_pairs={{224,0},{66,2},{68,4},{230,6},{0,32},{98,34},{100,36},{6,38},{32,6... | collective-permute-start | bytes 24584 | tf_op jit(solution)/shard_map/ppermute | solution.py:400
  6.4 3.1 %first_own.1 = (f32[17,8,128]{2,1,0:T(8,128)S(1)}, bf16[512,2048]{1,0:T(8,128)(2,1)S(1)}, bf16[512,2048]{1,0:T(8,128)(2,1)S(1)}) custom-call(s32[1]{0:T(128)} %bitcast.core_ref, bf16[64,2048]{1,0:T(8,128)(2,1)S(1)} %get-tuple-element.27.left_ref, f32[17,8,128]{2,1,0:T(8,128)S(1)} %get-tuple-element.28.send_ref, f32[1024,2048]{1,0:T(8,128)} %features_ref.3), custom_call_target="tpu_custom_call" | custom-call | flops 201326592 | bytes 4194304 | tf_op jit(solution)/shard_map/first_own/pallas_call | solution.py:426
  9.5 2.8 %collective-permute-start.4 = (f32[17,8,128]{2,1,0:T(8,128)S(1)}, f32[17,8,128]{2,1,0:T(8,128)S(1)}, u32[]{:S(2)}, u32[]{:S(2)}) collective-permute-start(f32[17,8,128]{2,1,0:T(8,128)S(1)} %get-tuple-element.31.own_ref), channel_id=1, source_target_pairs={{0,24},{8,0},{16,8},{24,16},{1,25},{9,1},{17,9},{25,17},{2,26},{10... | collective-permute-start | bytes 208904 | tf_op jit(solution)/shard_map/ppermute | solution.py:438
  12.4 0.8 collective-permute-start.3
  13.2 0.9 collective-permute-start.2
  14.7 1.0 collective-permute-done.4.three_ref
  15.7 2.9 %collective-permute-done.3.two_ref = f32[17,8,128]{2,1,0:T(8,128)S(1)} collective-permute-done((f32[17,8,128]{2,1,0:T(8,128)S(1)}, f32[17,8,128]{2,1,0:T(8,128)S(1)}, u32[]{:S(2)}, u32[]{:S(2)}) %collective-permute-start.3) | collective-permute-done | bytes 69664 | tf_op jit(solution)/shard_map/ppermute | solution.py:438
  18.6 0.7 collective-permute-done.2.one_ref
  19.4 5.6 %collective-permute-start.8 = (f32[19,8,128]{2,1,0:T(8,128)S(1)}, f32[19,8,128]{2,1,0:T(8,128)S(1)}, u32[]{:S(2)}, u32[]{:S(2)}) collective-permute-start(f32[19,8,128]{2,1,0:T(8,128)S(1)} %middle.1.own_ref), channel_id=1, source_target_pairs={{0,6},{2,0},{4,2},{6,4},{1,7},{3,1},{5,3},{7,5},{8,14},{10,8},{12,... | collective-permute-start | bytes 233480 | tf_op jit(solution)/shard_map/ppermute | solution.py:438
  24.9 2.5 %collective-permute-start.7 = (f32[19,8,128]{2,1,0:T(8,128)S(1)}, f32[19,8,128]{2,1,0:T(8,128)S(1)}, u32[]{:S(2)}, u32[]{:S(2)}) collective-permute-start(f32[19,8,128]{2,1,0:T(8,128)S(1)} %middle.1.own_ref), channel_id=1, source_target_pairs={{0,4},{2,6},{4,0},{6,2},{1,5},{3,7},{5,1},{7,3},{8,12},{10,14},{12... | collective-permute-start | bytes 233480 | tf_op jit(solution)/shard_map/ppermute | solution.py:438
  27.4 1.3 %collective-permute-start.6 = (f32[19,8,128]{2,1,0:T(8,128)S(1)}, f32[19,8,128]{2,1,0:T(8,128)S(1)}, u32[]{:S(2)}, u32[]{:S(2)}) collective-permute-start(f32[19,8,128]{2,1,0:T(8,128)S(1)} %middle.1.own_ref), channel_id=1, source_target_pairs={{0,2},{2,4},{4,6},{6,0},{1,3},{3,5},{5,7},{7,1},{8,10},{10,12},{12... | collective-permute-start | bytes 233480 | tf_op jit(solution)/shard_map/ppermute | solution.py:438
  28.7 2.2 %collective-permute-done.7.two_ref = f32[19,8,128]{2,1,0:T(8,128)S(1)} collective-permute-done((f32[19,8,128]{2,1,0:T(8,128)S(1)}, f32[19,8,128]{2,1,0:T(8,128)S(1)}, u32[]{:S(2)}, u32[]{:S(2)}) %collective-permute-start.7) | collective-permute-done | bytes 77856 | tf_op jit(solution)/shard_map/ppermute | solution.py:438
  30.9 2.1 %collective-permute-done.6.one_ref = f32[19,8,128]{2,1,0:T(8,128)S(1)} collective-permute-done((f32[19,8,128]{2,1,0:T(8,128)S(1)}, f32[19,8,128]{2,1,0:T(8,128)S(1)}, u32[]{:S(2)}, u32[]{:S(2)}) %collective-permute-start.6) | collective-permute-done | bytes 77856 | tf_op jit(solution)/shard_map/ppermute | solution.py:438
  33.2 0.7 image_own.2.before_ref
  35.1 14.4 %all_to_all.20.pieces_ref = f32[8,4,8,128]{3,2,1,0:T(8,128)S(1)} all-to-all(f32[8,4,8,128]{3,2,1,0:T(8,128)S(1)} %get-tuple-element.38), channel_id=1, replica_groups=mesh['tok'=8,'x'=4,'y'=4,'core'=2] {'tok'}, dimensions={0} | all-to-all | bytes 262144 | tf_op jit(solution)/shard_map/all_to_all | solution.py:403
  49.5 11.8 %all_to_all.21.pieces_ref = f32[8,5,8,128]{3,2,1,0:T(8,128)S(1)} all-to-all(f32[8,5,8,128]{3,2,1,0:T(8,128)S(1)} %gather.2), channel_id=1, replica_groups=mesh['tok'=8,'x'=4,'y'=4,'core'=2] {'tok'}, dimensions={0} | all-to-all | bytes 327680 | tf_op jit(solution)/shard_map/all_to_all | solution.py:405
  61.4 1.4 %residual_other.1 = (f32[9,8,128]{2,1,0:T(8,128)S(1)}, f32[16,2048]{1,0:T(8,128)S(1)}, f32[8,128]{1,0:T(8,128)S(1)}, bf16[32,2048]{1,0:T(8,128)(2,1)S(1)}) custom-call(f32[8,5,8,128]{3,2,1,0:T(8,128)S(1)} %all_to_all.21.pieces_ref, f32[8,128]{1,0:T(8,128)S(1)} %get-tuple-element.40.norm_ref, f32[16,2048]{1,0:T(8,128)S(1)} %copy-done, ...), custom_call_target="tpu_custom_call" | custom-call | tf_op jit(solution)/shard_map/residual_other/pallas_call | solution.py:465
  62.9 1.2 %residual_own.1.refs_0_ = f32[9,8,128]{2,1,0:T(8,128)S(1)} custom-call(bf16[32,2048]{1,0:T(8,128)(2,1)S(1)} %get-tuple-element.41.left_ref, bf16[512,2048]{1,0:T(8,128)(2,1)S(1)} %get-tuple-element.36.high_ref, bf16[512,2048]{1,0:T(8,128)(2,1)S(1)} %get-tuple-element.37.low_ref, f32[9,8,128]{2,1,0:T(8,128)S(1)} %get-tuple-element.42.send_ref), custom_call_target="tpu_custom_call" | custom-call | flops 201326592 | bytes 4194304 | tf_op jit(solution)/shard_map/residual_own/pallas_call | solution.py:472
  64.2 2.4 %collective-permute-start.13 = (f32[9,8,128]{2,1,0:T(8,128)S(1)}, f32[9,8,128]{2,1,0:T(8,128)S(1)}, u32[]{:S(2)}, u32[]{:S(2)}) collective-permute-start(f32[9,8,128]{2,1,0:T(8,128)S(1)} %add.1.refs_0_), channel_id=1, source_target_pairs={{0,24},{8,0},{16,8},{24,16},{1,25},{9,1},{17,9},{25,17},{2,26},{10... | collective-permute-start | bytes 110600 | tf_op jit(solution)/shard_map/ppermute | solution.py:438
  66.6 1.5 %collective-permute-start.12 = (f32[9,8,128]{2,1,0:T(8,128)S(1)}, f32[9,8,128]{2,1,0:T(8,128)S(1)}, u32[]{:S(2)}, u32[]{:S(2)}) collective-permute-start(f32[9,8,128]{2,1,0:T(8,128)S(1)} %add.1.refs_0_), channel_id=1, source_target_pairs={{0,16},{8,24},{16,0},{24,8},{1,17},{9,25},{17,1},{25,9},{2,18},{10... | collective-permute-start | bytes 110600 | tf_op jit(solution)/shard_map/ppermute | solution.py:438
  68.8 3.3 %collective-permute-done.12.refs_2_ = f32[9,8,128]{2,1,0:T(8,128)S(1)} collective-permute-done((f32[9,8,128]{2,1,0:T(8,128)S(1)}, f32[9,8,128]{2,1,0:T(8,128)S(1)}, u32[]{:S(2)}, u32[]{:S(2)}) %collective-permute-start.12) | collective-permute-done | bytes 36896 | tf_op jit(solution)/shard_map/ppermute | solution.py:438
  72.1 1.2 %collective-permute-done.11.refs_1_ = f32[9,8,128]{2,1,0:T(8,128)S(1)} collective-permute-done((f32[9,8,128]{2,1,0:T(8,128)S(1)}, f32[9,8,128]{2,1,0:T(8,128)S(1)}, u32[]{:S(2)}, u32[]{:S(2)}) %collective-permute-start.11) | collective-permute-done | bytes 36896 | tf_op jit(solution)/shard_map/ppermute | solution.py:438
  73.3 0.9 collective-permute-start.16
  74.2 0.8 collective-permute-start.15
  75.0 1.3 %collective-permute-start.14 = (f32[9,8,128]{2,1,0:T(8,128)S(1)}, f32[9,8,128]{2,1,0:T(8,128)S(1)}, u32[]{:S(2)}, u32[]{:S(2)}) collective-permute-start(f32[9,8,128]{2,1,0:T(8,128)S(1)} %add_x.1.refs_0_), channel_id=1, source_target_pairs={{0,2},{2,4},{4,6},{6,0},{1,3},{3,5},{5,7},{7,1},{8,10},{10,12},{12... | collective-permute-start | bytes 110600 | tf_op jit(solution)/shard_map/ppermute | solution.py:438
  76.3 1.1 collective-permute-done.16.refs_3_
  77.3 2.4 %collective-permute-done.15.refs_2_ = f32[9,8,128]{2,1,0:T(8,128)S(1)} collective-permute-done((f32[9,8,128]{2,1,0:T(8,128)S(1)}, f32[9,8,128]{2,1,0:T(8,128)S(1)}, u32[]{:S(2)}, u32[]{:S(2)}) %collective-permute-start.15) | collective-permute-done | bytes 36896 | tf_op jit(solution)/shard_map/ppermute | solution.py:438
  80.5 0.7 image_own.3.before_ref
  82.4 12.0 %all_to_all.22.pieces_ref = f32[8,4,8,128]{3,2,1,0:T(8,128)S(1)} all-to-all(f32[8,4,8,128]{3,2,1,0:T(8,128)S(1)} %get-tuple-element.47), channel_id=1, replica_groups=mesh['tok'=8,'x'=4,'y'=4,'core'=2] {'tok'}, dimensions={0} | all-to-all | bytes 262144 | tf_op jit(solution)/shard_map/all_to_all | solution.py:403
  94.4 11.9 %all_to_all.23.pieces_ref = f32[8,5,8,128]{3,2,1,0:T(8,128)S(1)} all-to-all(f32[8,5,8,128]{3,2,1,0:T(8,128)S(1)} %gather.3), channel_id=1, replica_groups=mesh['tok'=8,'x'=4,'y'=4,'core'=2] {'tok'}, dimensions={0} | all-to-all | bytes 327680 | tf_op jit(solution)/shard_map/all_to_all | solution.py:405
  106.3 0.9 last.1
  (30 shorter events, 5.1 us)
Async XLA Ops:
  4.3 5.3 %collective-permute-start = (f32[17,8,128]{2,1,0:T(8,128)S(1)}, f32[17,8,128]{2,1,0:T(8,128)S(1)}, u32[]{:S(2)}, u32[]{:S(2)}) collective-permute-start(f32[17,8,128]{2,1,0:T(8,128)S(1)} %get-tuple-element.28.send_ref), channel_id=1, source_target_pairs={{0,1},{1,0},{2,3},{3,2},{4,5},{5,4},{6,7},{7,6},{8,9},{9,8},{10,11... | collective-permute-start | bytes 208904 | tf_op jit(solution)/shard_map/ppermute | solution.py:392
  4.4 5.1 %collective-permute-start.1 = (f32[2,8,128]{2,1,0:T(8,128)S(1)}, f32[2,8,128]{2,1,0:T(8,128)S(1)}, u32[]{:S(2)}, u32[]{:S(2)}) collective-permute-start(f32[2,8,128]{2,1,0:T(8,128)S(1)} %get-tuple-element.30.count_ref), channel_id=1, source_target_pairs={{224,0},{66,2},{68,4},{230,6},{0,32},{98,34},{100,36},{6,38},{32,6... | collective-permute-start | bytes 24584 | tf_op jit(solution)/shard_map/ppermute | solution.py:400
  6.4 26.6 %copy-start.1 = (s32[1024]{0:T(1024)S(1)}, s32[1024]{0:T(1024)}, u32[]{:S(2)}) copy-start(s32[1024]{0:T(1024)} %param.5) | copy-start | bytes 12292
  9.5 6.2 %collective-permute-start.4 = (f32[17,8,128]{2,1,0:T(8,128)S(1)}, f32[17,8,128]{2,1,0:T(8,128)S(1)}, u32[]{:S(2)}, u32[]{:S(2)}) collective-permute-start(f32[17,8,128]{2,1,0:T(8,128)S(1)} %get-tuple-element.31.own_ref), channel_id=1, source_target_pairs={{0,24},{8,0},{16,8},{24,16},{1,25},{9,1},{17,9},{25,17},{2,26},{10... | collective-permute-start | bytes 208904 | tf_op jit(solution)/shard_map/ppermute | solution.py:438
  12.4 6.2 %collective-permute-start.3 = (f32[17,8,128]{2,1,0:T(8,128)S(1)}, f32[17,8,128]{2,1,0:T(8,128)S(1)}, u32[]{:S(2)}, u32[]{:S(2)}) collective-permute-start(f32[17,8,128]{2,1,0:T(8,128)S(1)} %get-tuple-element.31.own_ref), channel_id=1, source_target_pairs={{0,16},{8,24},{16,0},{24,8},{1,17},{9,25},{17,1},{25,9},{2,18},{10... | collective-permute-start | bytes 208904 | tf_op jit(solution)/shard_map/ppermute | solution.py:438
  13.2 6.2 %collective-permute-start.2 = (f32[17,8,128]{2,1,0:T(8,128)S(1)}, f32[17,8,128]{2,1,0:T(8,128)S(1)}, u32[]{:S(2)}, u32[]{:S(2)}) collective-permute-start(f32[17,8,128]{2,1,0:T(8,128)S(1)} %get-tuple-element.31.own_ref), channel_id=1, source_target_pairs={{0,8},{8,16},{16,24},{24,0},{1,9},{9,17},{17,25},{25,1},{2,10},{10... | collective-permute-start | bytes 208904 | tf_op jit(solution)/shard_map/ppermute | solution.py:438
  14.1 0.7 collective-permute-start.5
  19.4 9.4 %collective-permute-start.8 = (f32[19,8,128]{2,1,0:T(8,128)S(1)}, f32[19,8,128]{2,1,0:T(8,128)S(1)}, u32[]{:S(2)}, u32[]{:S(2)}) collective-permute-start(f32[19,8,128]{2,1,0:T(8,128)S(1)} %middle.1.own_ref), channel_id=1, source_target_pairs={{0,6},{2,0},{4,2},{6,4},{1,7},{3,1},{5,3},{7,5},{8,14},{10,8},{12,... | collective-permute-start | bytes 233480 | tf_op jit(solution)/shard_map/ppermute | solution.py:438
  24.9 6.0 %collective-permute-start.7 = (f32[19,8,128]{2,1,0:T(8,128)S(1)}, f32[19,8,128]{2,1,0:T(8,128)S(1)}, u32[]{:S(2)}, u32[]{:S(2)}) collective-permute-start(f32[19,8,128]{2,1,0:T(8,128)S(1)} %middle.1.own_ref), channel_id=1, source_target_pairs={{0,4},{2,6},{4,0},{6,2},{1,5},{3,7},{5,1},{7,3},{8,12},{10,14},{12... | collective-permute-start | bytes 233480 | tf_op jit(solution)/shard_map/ppermute | solution.py:438
  27.4 5.6 %collective-permute-start.6 = (f32[19,8,128]{2,1,0:T(8,128)S(1)}, f32[19,8,128]{2,1,0:T(8,128)S(1)}, u32[]{:S(2)}, u32[]{:S(2)}) collective-permute-start(f32[19,8,128]{2,1,0:T(8,128)S(1)} %middle.1.own_ref), channel_id=1, source_target_pairs={{0,2},{2,4},{4,6},{6,0},{1,3},{3,5},{5,7},{7,1},{8,10},{10,12},{12... | collective-permute-start | bytes 233480 | tf_op jit(solution)/shard_map/ppermute | solution.py:438
  33.1 1.3 %collective-permute-start.9 = (f32[9,8,128]{2,1,0:T(8,128)S(1)}, f32[9,8,128]{2,1,0:T(8,128)S(1)}, u32[]{:S(2)}, u32[]{:S(2)}) collective-permute-start(f32[9,8,128]{2,1,0:T(8,128)S(1)} %get-tuple-element.33.weighted_ref.own_ref), channel_id=1, source_target_pairs={{0,1},{1,0},{2,3},{3,2},{4,5},{5,4},{6,7},{7,6},{8,9},{9,8},{10,11... | collective-permute-start | bytes 110600 | tf_op jit(solution)/shard_map/ppermute | solution.py:392
  34.4 26.9 %copy-start = (f32[16,2048]{1,0:T(8,128)S(1)}, f32[16,2048]{1,0:T(8,128)}, u32[]{:S(2)}) copy-start(f32[16,2048]{1,0:T(8,128)} %right_ref.3) | copy-start | bytes 393220
  62.7 1.4 %collective-permute-start.10 = (f32[9,8,128]{2,1,0:T(8,128)S(1)}, f32[9,8,128]{2,1,0:T(8,128)S(1)}, u32[]{:S(2)}, u32[]{:S(2)}) collective-permute-start(f32[9,8,128]{2,1,0:T(8,128)S(1)} %get-tuple-element.42.send_ref), channel_id=1, source_target_pairs={{0,1},{1,0},{2,3},{3,2},{4,5},{5,4},{6,7},{7,6},{8,9},{9,8},{10,11... | collective-permute-start | bytes 110600 | tf_op jit(solution)/shard_map/ppermute | solution.py:392
  64.2 4.6 %collective-permute-start.13 = (f32[9,8,128]{2,1,0:T(8,128)S(1)}, f32[9,8,128]{2,1,0:T(8,128)S(1)}, u32[]{:S(2)}, u32[]{:S(2)}) collective-permute-start(f32[9,8,128]{2,1,0:T(8,128)S(1)} %add.1.refs_0_), channel_id=1, source_target_pairs={{0,24},{8,0},{16,8},{24,16},{1,25},{9,1},{17,9},{25,17},{2,26},{10... | collective-permute-start | bytes 110600 | tf_op jit(solution)/shard_map/ppermute | solution.py:438
  66.6 5.5 %collective-permute-start.12 = (f32[9,8,128]{2,1,0:T(8,128)S(1)}, f32[9,8,128]{2,1,0:T(8,128)S(1)}, u32[]{:S(2)}, u32[]{:S(2)}) collective-permute-start(f32[9,8,128]{2,1,0:T(8,128)S(1)} %add.1.refs_0_), channel_id=1, source_target_pairs={{0,16},{8,24},{16,0},{24,8},{1,17},{9,25},{17,1},{25,9},{2,18},{10... | collective-permute-start | bytes 110600 | tf_op jit(solution)/shard_map/ppermute | solution.py:438
  68.1 5.2 %collective-permute-start.11 = (f32[9,8,128]{2,1,0:T(8,128)S(1)}, f32[9,8,128]{2,1,0:T(8,128)S(1)}, u32[]{:S(2)}, u32[]{:S(2)}) collective-permute-start(f32[9,8,128]{2,1,0:T(8,128)S(1)} %add.1.refs_0_), channel_id=1, source_target_pairs={{0,8},{8,16},{16,24},{24,0},{1,9},{9,17},{17,25},{25,1},{2,10},{10... | collective-permute-start | bytes 110600 | tf_op jit(solution)/shard_map/ppermute | solution.py:438
  73.3 4.0 %collective-permute-start.16 = (f32[9,8,128]{2,1,0:T(8,128)S(1)}, f32[9,8,128]{2,1,0:T(8,128)S(1)}, u32[]{:S(2)}, u32[]{:S(2)}) collective-permute-start(f32[9,8,128]{2,1,0:T(8,128)S(1)} %add_x.1.refs_0_), channel_id=1, source_target_pairs={{0,6},{2,0},{4,2},{6,4},{1,7},{3,1},{5,3},{7,5},{8,14},{10,8},{12,... | collective-permute-start | bytes 110600 | tf_op jit(solution)/shard_map/ppermute | solution.py:438
  74.2 5.5 %collective-permute-start.15 = (f32[9,8,128]{2,1,0:T(8,128)S(1)}, f32[9,8,128]{2,1,0:T(8,128)S(1)}, u32[]{:S(2)}, u32[]{:S(2)}) collective-permute-start(f32[9,8,128]{2,1,0:T(8,128)S(1)} %add_x.1.refs_0_), channel_id=1, source_target_pairs={{0,4},{2,6},{4,0},{6,2},{1,5},{3,7},{5,1},{7,3},{8,12},{10,14},{12... | collective-permute-start | bytes 110600 | tf_op jit(solution)/shard_map/ppermute | solution.py:438
  75.0 5.2 %collective-permute-start.14 = (f32[9,8,128]{2,1,0:T(8,128)S(1)}, f32[9,8,128]{2,1,0:T(8,128)S(1)}, u32[]{:S(2)}, u32[]{:S(2)}) collective-permute-start(f32[9,8,128]{2,1,0:T(8,128)S(1)} %add_x.1.refs_0_), channel_id=1, source_target_pairs={{0,2},{2,4},{4,6},{6,0},{1,3},{3,5},{5,7},{7,1},{8,10},{10,12},{12... | collective-permute-start | bytes 110600 | tf_op jit(solution)/shard_map/ppermute | solution.py:438
  80.4 1.3 %collective-permute-start.17 = (f32[9,8,128]{2,1,0:T(8,128)S(1)}, f32[9,8,128]{2,1,0:T(8,128)S(1)}, u32[]{:S(2)}, u32[]{:S(2)}) collective-permute-start(f32[9,8,128]{2,1,0:T(8,128)S(1)} %get-tuple-element.46.weighted_ref.own_ref), channel_id=1, source_target_pairs={{0,1},{1,0},{2,3},{3,2},{4,5},{5,4},{6,7},{7,6},{8,9},{9,8},{10,11... | collective-permute-start | bytes 110600 | tf_op jit(solution)/shard_map/ppermute | solution.py:392

commit v5 on v4

--- a/solution.py
+++ b/solution.py
@@ -101,7 +101,7 @@
 
 def first_other_kernel(
     step,
-    core_ref,
+    place_ref,
     labels_hbm,
     weights_hbm,
     right_hbm,
@@ -123,7 +123,7 @@
     for load in loads:
         load.start()
     half = features_ref.shape[0] // 2
-    copies = read_half((1 - core_ref[0]) * half, step, features_ref, block_ref, block_sems)
+    copies = read_half((1 - (place_ref[0] & 1)) * half, step, features_ref, block_ref, block_sems)
     classes = weights_ref.shape[0]
     rows = 2 * classes
     for i, ref in enumerate((weights_ref, right_ref)):
@@ -144,18 +144,21 @@
 
 
 def first_own_kernel(
-    step, core_ref, left_ref, send_ref, features_ref, keep_ref, high_ref, low_ref, block_ref, sems
+    step, place_ref, left_ref, send_ref, features_ref, keep_ref, high_ref, low_ref, block_ref, sems
 ):
     half = features_ref.shape[0] // 2
-    copies = read_half(core_ref[0] * half, step, features_ref, block_ref, sems)
+    copies = read_half((place_ref[0] & 1) * half, step, features_ref, block_ref, sems)
     store_tiles(keep_ref, project_half(copies, step, left_ref, block_ref, high_ref, low_ref), send_ref[send_ref.shape[0] - 1])
 
 
+def tree(values):
+    while len(values) > 1:
+        values = [values[i] + values[i + 1] for i in range(0, len(values), 2)]
+    return values[0]
+
+
 def add_kernel(*refs):
-    value = refs[0][...]
-    for ref in refs[1:-1]:
-        value += ref[...]
-    refs[-1][...] = value
+    refs[-1][...] = tree([ref[...] for ref in refs[:-1]])
 
 
 def join_kernel(keep_ref, got_ref, count_ref, other_ref, sum_ref, counts_ref):
@@ -166,19 +169,9 @@
 def middle_kernel(own_ref, one_ref, two_ref, three_ref, other_ref, sum_ref):
     count = own_ref.shape[0]
     for k in range(count):
-        sum_ref[k] = own_ref[k] + one_ref[k] + two_ref[k] + three_ref[k]
+        sum_ref[k] = tree([own_ref[k], one_ref[k], two_ref[k], three_ref[k]])
     for r in range(other_ref.shape[0]):
         sum_ref[count + r] = other_ref[r]
-
-
-def gather_kernel(pieces_ref, extra_ref, spread_ref):
-    copies, count = pieces_ref.shape[:2]
-    for k in range(count):
-        tile = summed(pieces_ref, k)
-        for i in range(copies):
-            spread_ref[i, k] = tile
-    for i in range(copies):
-        spread_ref[i, count] = extra_ref[...]
 
 
 def weigh(c, across, projected, probability, scaled, weighted_ref):
@@ -192,7 +185,7 @@
 
 
 def softmax_kernel(
-    core_ref,
+    place_ref,
     labels_ref,
     own_ref,
     one_ref,
@@ -205,7 +198,7 @@
     weighted_ref,
 ):
     def whole_sum(k):
-        return own_ref[k] + one_ref[k] + two_ref[k] + three_ref[k]
+        return tree([own_ref[k], one_ref[k], two_ref[k], three_ref[k]])
 
     across = first_ref.shape[0] // 2
     classes = 2 * SUB
@@ -217,7 +210,7 @@
         projected = [whole_sum((2 + r) * across + c) for r in range(2)]
         whole = class_sum(powered)
         probability = [powered[r] / whole for r in range(2)]
-        label = labels_ref[pl.ds(core_ref[0] * across + c, 1), :]
+        label = labels_ref[pl.ds((place_ref[0] & 1) * across + c, 1), :]
         own = class_sum([jnp.where(label == ids + r * SUB, counts[r], 0.0) for r in range(2)])
         scale = 1.0 / (classes * own)
         scaled = [scale * probability[r] for r in range(2)]
@@ -263,47 +256,38 @@
     return left_ref[...].astype(bf16)
 
 
-def image_columns(k, step, left, high_ref, low_ref, before_ref, pieces_ref):
+def image_columns(at, step, left, high_ref, low_ref):
     classes = left.shape[0] // 2
-    share = pieces_ref.shape[1] // 2
-    per = share * LANE
-    part = slice(k * step, (k + 1) * step)
+    part = pl.ds(at, step)
     both = lax.dot_general(left, high_ref[:, part], ROWS_WITH_COLUMNS, preferred_element_type=f32)
     rest = lax.dot_general(left[:classes], low_ref[:, part], ROWS_WITH_COLUMNS, preferred_element_type=f32)
-    value = both[:classes] + both[classes:] + rest
-    for z in range(step // per):
-        for r in range(2):
-            for c in range(share):
-                at = z * per + c * LANE
-                tile = value[r * SUB : (r + 1) * SUB, at : at + LANE]
-                to = k * (step // per) + z
-                if before_ref is not None:
-                    tile = tile + before_ref[to, r * share + c]
-                pieces_ref[to, r * share + c] = tile
-
-
-def image_kernel(step, weighted_ref, high_ref, low_ref, before_ref, pieces_ref, left_ref):
+    return both[:classes] + both[classes:] + rest
+
+
+def image_own_kernel(step, weighted_ref, high_ref, low_ref, image_ref, left_ref):
     left = put_together(weighted_ref, left_ref)
     for k in range(high_ref.shape[1] // step):
-        image_columns(k, step, left, high_ref, low_ref, before_ref, pieces_ref)
-
-
-def image_own_kernel(step, weighted_ref, high_ref, low_ref, pieces_ref, left_ref):
-    image_kernel(step, weighted_ref, high_ref, low_ref, None, pieces_ref, left_ref)
+        image_ref[k] = image_columns(k * step, step, left, high_ref, low_ref)
 
 
 def image_other_kernel(
-    step, other_ref, own_ref, high_ref, low_ref, before_ref, pieces_ref, curve_ref, left_ref
+    step, place_ref, other_ref, own_ref, high_ref, low_ref, before_ref, *piece_refs_and_left
 ):
+    *piece_refs, left_ref = piece_refs_and_left
     last = own_ref.shape[0] - 1
-    curve_ref[...] = own_ref[last] + other_ref[last]
-    image_kernel(step, other_ref, high_ref, low_ref, before_ref, pieces_ref, left_ref)
-
-
-def columns_of(pieces_ref, z, share, classes):
+    curve = own_ref[last] + other_ref[last]
+    left = put_together(other_ref, left_ref)
+    for d, piece_ref in enumerate(piece_refs):
+        block = (place_ref[0] >> 1) ^ d
+        at = pl.multiple_of(block * step, step)
+        store_tiles(piece_ref, before_ref[block] + image_columns(at, step, left, high_ref, low_ref), curve)
+
+
+def columns_of(piece_ref, classes):
+    across = (piece_ref.shape[0] - 1) // (classes // SUB)
     rows = []
     for r in range(classes // SUB):
-        rows.append(jnp.concatenate([pieces_ref[z, r * share + c] for c in range(share)], axis=1))
+        rows.append(jnp.concatenate([piece_ref[r * across + c] for c in range(across)], axis=1))
     return jnp.concatenate(rows, axis=0)
 
 
@@ -316,28 +300,36 @@
 
 
 def residual_other_kernel(
-    pieces_ref, norm_ref, right_ref, high_ref, low_ref, send_ref, residual_ref, rate_ref, left_ref
+    step,
+    place_ref,
+    own_ref,
+    one_ref,
+    two_ref,
+    three_ref,
+    norm_ref,
+    right_ref,
+    high_ref,
+    low_ref,
+    send_ref,
+    residual_ref,
+    rate_ref,
+    left_ref,
 ):
-    classes, width = right_ref.shape
-    toks, count = pieces_ref.shape[:2]
-    share = (count - 1) // 2
-    per = share * LANE
+    classes = right_ref.shape[0]
     norm_now = norm_ref[0:1, 0:1]
-    curve = total(summed(pieces_ref, count - 1))
+    curve = total(own_ref[own_ref.shape[0] - 1])
     rate = norm_now / (curve + ridge_strength * norm_now)
     rate_ref[...] = jnp.broadcast_to(rate, (SUB, LANE))
-    norm = jnp.zeros((SUB, LANE), f32)
-    cross = jnp.zeros((SUB, LANE), f32)
-    for z in range(toks):
-        at = slice(z * per, (z + 1) * per)
+    for d, piece_ref in enumerate((own_ref, one_ref, two_ref, three_ref)):
+        at = pl.ds(pl.multiple_of(((place_ref[0] >> 1) ^ d) * step, step), step)
         right = right_ref[:, at]
-        residual = right - rate * (columns_of(pieces_ref, z, share, classes) + ridge_strength * right)
+        residual = right - rate * (columns_of(piece_ref, classes) + ridge_strength * right)
         residual_ref[:, at] = residual
-        norm += fold(residual * residual)
-        cross += fold(residual * right)
         high, low = parts(residual)
         left_ref[:classes, at] = high
         left_ref[classes:, at] = low
+    right, residual = right_ref[...], residual_ref[...]
+    norm, cross = fold(residual * residual), fold(residual * right)
     sums = jnp.concatenate([norm[:4] + norm[4:], cross[:4] + cross[4:]])
     store_tiles(send_ref, project_kept(left_ref, high_ref, low_ref), sums)
 
@@ -346,20 +338,30 @@
     store_tiles(keep_ref, project_kept(left_ref, high_ref, low_ref), send_ref[send_ref.shape[0] - 1])
 
 
-def last_kernel(pieces_ref, numbers_ref, rate_ref, right_ref, old_ref, solution_ref, residual_ref):
-    classes, width = right_ref.shape
-    toks, count = pieces_ref.shape[:2]
-    share = (count - 1) // 2
-    per = share * LANE
+def last_kernel(
+    step,
+    place_ref,
+    own_ref,
+    one_ref,
+    two_ref,
+    three_ref,
+    numbers_ref,
+    rate_ref,
+    right_ref,
+    old_ref,
+    solution_ref,
+    residual_ref,
+):
+    classes = right_ref.shape[0]
     norm_next, ratio, norm_direction = [numbers_ref[i, 0:1, 0:1] for i in range(3)]
-    curve = total(summed(pieces_ref, count - 1))
+    curve = total(own_ref[own_ref.shape[0] - 1])
     rate = norm_next / (curve + ridge_strength * norm_direction)
     rate_first = rate_ref[0:1, 0:1]
-    for z in range(toks):
-        at = slice(z * per, (z + 1) * per)
+    for d, piece_ref in enumerate((own_ref, one_ref, two_ref, three_ref)):
+        at = pl.ds(pl.multiple_of(((place_ref[0] >> 1) ^ d) * step, step), step)
         right, old = right_ref[:, at], old_ref[:, at]
         direction = old + ratio * right
-        image = columns_of(pieces_ref, z, share, classes) + ridge_strength * direction
+        image = columns_of(piece_ref, classes) + ridge_strength * direction
         solution_ref[:, at] = rate_first * right + rate * direction
         residual_ref[:, at] = old - rate * image
 
@@ -372,17 +374,18 @@
     groups = classes // SUB
     toks = lax.axis_size("tok")
     across_x, across_y = lax.axis_size("x"), lax.axis_size("y")
-    share = width // toks // LANE
-    core = lax.axis_index("core").astype(jnp.int32).reshape(1)
     labels = labels.reshape(tokens // LANE, LANE)
-    step = min(512, width)
+    step = width // 4
+    tok = lax.axis_index("tok").astype(jnp.int32)
+    role = jnp.minimum(tok, toks - 1 - tok)
+    place = (2 * role + lax.axis_index("core").astype(jnp.int32)).reshape(1)
     swap = [(0, 1), (1, 0)]
     half_product = pl.CostEstimate(
         flops=12 * classes * half * width, bytes_accessed=4 * half * width, transcendentals=0
     )
     reading = [pltpu.VMEM((width // step, half, step), f32), pltpu.SemaphoreType.DMA((width // step,))]
     kept_half = pltpu.VMEM((half, width), bf16)
-    image_outs = tiles(toks, groups * share)
+    piece = tiles(groups * step // LANE + 1)
     put = pltpu.VMEM((2 * classes, half), f32)
 
     def with_step(kernel):
@@ -399,10 +402,18 @@
         ]
         return lax.ppermute(value, ("tok", "y"), pairs)
 
-    def sum_over_tok(pieces, curve):
-        pieces = lax.all_to_all(pieces, "tok", 0, 0)
-        spread = call(gather_kernel, "gather", [ON_CHIP] * 2, tiles(toks, groups * share + 1))(pieces, curve)
-        return lax.all_to_all(spread, "tok", 0, 0)
+    def from_others(value, axis):
+        values = value if isinstance(value, list) else [value] * 3
+        count = lax.axis_size(axis)
+        return [lax.ppermute(v, axis, [(i, i ^ (d + 1)) for i in range(count)]) for d, v in enumerate(values)]
+
+    def add(name, *values):
+        return call(add_kernel, name, [ON_CHIP] * len(values), tiles(values[0].shape[0]))(*values)
+
+    def sum_over_tok(own, *rest):
+        own = add("add_half", own, *from_others(list(rest), "tok"))
+        own = add("add_tok", own, lax.ppermute(own, "tok", [(i, toks - 1 - i) for i in range(toks)]))
+        return [own] + from_others(own, "tok")
 
     near, far = (-1, 2, 2, -1), (0, 1, 2, -2)
     kept = 2 * groups * across + 1
@@ -420,7 +431,7 @@
             reading[1],
         ],
         kib=61560 - 4096,
-    )(core, labels, weights, right_side, features)
+    )(place, labels, weights, right_side, features)
     got = swapped(send)
     other = from_tok(count, near)
     keep, high_own, low_own = call(
@@ -431,57 +442,59 @@
         reading,
         mib=45,
         cost=half_product,
-    )(core, left, send, features)
-
-    def from_others(value, axis, count):
-        return [
-            lax.ppermute(value, axis, [(i, (i + d) % count) for i in range(count)]) for d in range(1, count)
-        ]
+    )(place, left, send, features)
 
     own, count = call(join_kernel, "join", [ON_CHIP] * 4, [tiles(kept), tiles(groups)])(keep, got, count, other)
-    others = from_others(own, "x", across_x)
+    others = from_others(own, "x")
     other = from_tok(count, far)
     own = call(middle_kernel, "middle", [ON_CHIP] * 5, tiles(kept + groups))(own, *others, other)
-    others = from_others(own, "y", across_y)
+    others = from_others(own, "y")
     probability, scaled, first, norm_now, weighted = call(
         softmax_kernel,
         "softmax",
         [SCALAR] + [ON_CHIP] * 5,
         [tiles(groups * across)] * 3 + [tiles(), tiles(groups * across + 1)],
-    )(core, labels, own, *others)
+    )(place, labels, own, *others)
 
     def image(weighted):
         other = swapped(weighted)
-        pieces = call(
-            with_step(image_own_kernel), "image_own", [ON_CHIP] * 3, image_outs, [put], cost=half_product
+        before = call(
+            with_step(image_own_kernel),
+            "image_own",
+            [ON_CHIP] * 3,
+            pltpu.VMEM((4, classes, step), f32),
+            [put],
+            cost=half_product,
         )(weighted, high_own, low_own)
         return call(
-            with_step(image_other_kernel), "image_other", [ON_CHIP] * 5, [image_outs, tiles()], [put]
-        )(other, weighted, high_other, low_other, pieces)
+            with_step(image_other_kernel), "image_other", [SCALAR] + [ON_CHIP] * 5, [piece] * 4, [put]
+        )(place, other, weighted, high_other, low_other, before)
 
     pieces = sum_over_tok(*image(weighted))
 
     kept = groups * across + 1
     send, residual, rate, left = call(
-        residual_other_kernel,
+        with_step(residual_other_kernel),
         "residual_other",
-        [ON_CHIP] * 5,
+        [SCALAR] + [ON_CHIP] * 8,
         [tiles(kept), pltpu.VMEM((classes, width), f32), tiles(), pltpu.VMEM((2 * classes, width), bf16)],
-    )(pieces, norm_now, right_side, high_other, low_other)
+    )(place, *pieces, norm_now, right_side, high_other, low_other)
     got = swapped(send)
     keep = call(residual_own_kernel, "residual_own", [ON_CHIP] * 4, tiles(kept), cost=half_product)(
         left, high_own, low_own, send
     )
-    own = call(add_kernel, "add", [ON_CHIP] * 2, tiles(kept))(keep, got)
-    own = call(add_kernel, "add_x", [ON_CHIP] * 4, tiles(kept))(own, *from_others(own, "x", across_x))
-    own = call(add_kernel, "add_y", [ON_CHIP] * 4, tiles(kept))(own, *from_others(own, "y", across_y))
+    own = add("add_core", keep, got)
+    own = add("add_x", own, *from_others(own, "x"))
+    own = add("add_y", own, *from_others(own, "y"))
     weighted, numbers = call(second_kernel, "second", [ON_CHIP] * 5, [tiles(kept), tiles(3)])(
         own[None], probability, scaled, first, norm_now
     )
     pieces = sum_over_tok(*image(weighted))
     out = jax.ShapeDtypeStruct((classes, width), f32)
     return tuple(
-        call(last_kernel, "last", [ON_CHIP] * 5, [out, out])(pieces, numbers, rate, right_side, residual)
+        call(with_step(last_kernel), "last", [SCALAR] + [ON_CHIP] * 8, [out, out])(
+            place, *pieces, numbers, rate, right_side, residual
+        )
     )
 
 

time: 108 us -> 98.2 us (0.909)
  blocking collectives: 50.1 us -> 0 us
  starting transfers between devices: 23.9 us -> 46.2 us
  waiting for transfers between devices: 18.9 us -> 37.7 us
    all_to_all x4 -> x0, blocking collectives: 50.1 us -> none  [the longest x2 26.4 us: sum_over_tok(): pieces = lax.all_to_all(pieces, 'tok', 0, 0)]
    ppermute x12 -> x26, starting transfers between devices: 20.8 us -> 43.2 us  [the longest x24 35.3 us: from_others(): lax.ppermute(v, axis, [(i, i ^ d + 1) for i in range(count)])]
    ppermute x12 -> x26, waiting for transfers between devices: 17.9 us -> 36.7 us  [the longest x24 30.4 us: from_others(): lax.ppermute(v, axis, [(i, i ^ d + 1) for i in range(count)])]
    pallas_call x11 -> x13, Pallas kernels: 5.13 us -> 5.13 us  [the longest x2 1.41 us: image(): call(with_step(image_other_kernel), 'image_other', [SCALAR] + [ON_CHIP] *...]
  transfers between devices with their start and end apart: 18 -> 32, of which waited for: 13 -> 25; matrix products, arithmetic and copies ran while one was open for 0% -> 0% of each run, Pallas kernels for 5% -> 6%
where the time goes in v5:
time: 98.2 us; the launch traced here: 98.1 us
  starting transfers between devices  46.2 us (47%)
  waiting for transfers between devices  37.7 us (38%)
  Pallas kernels  13.5 us (14%)
    ppermute x24, starting transfers between devices, from_others(): lax.ppermute(v, axis, [(i, i ^ d + 1) for i in range(count)])  35.3 us
    ppermute x24, waiting for transfers between devices, from_others(): lax.ppermute(v, axis, [(i, i ^ d + 1) for i in range(count)])  30.4 us
    ppermute x2, starting transfers between devices, sum_over_tok(): lax.ppermute(own, 'tok', [(i, toks - 1 - i) for i in range(toks)])  7.94 us
    ppermute x2, waiting for transfers between devices, sum_over_tok(): lax.ppermute(own, 'tok', [(i, toks - 1 - i) for i in range(toks)])  6.27 us
    pallas_call x1, Pallas kernels, on_device(): call(with_step(first_other_kernel), 'first_other', [SCALAR] + [IN_HBM] *...  3.62 us
    pallas_call x1, Pallas kernels, on_device(): call(with_step(first_own_kernel), 'first_own', [SCALAR, ON_CHIP, ON_CHIP,...  3.13 us
    ppermute x2, starting transfers between devices, from_tok(): return lax.ppermute(value, ('tok', 'y'), pairs)  2.65 us
  transfers between devices with their start and end apart: 32, of which 25 were waited for; matrix products, arithmetic and copies ran while one was open for 0% of the time, Pallas kernels for 6%

profile of v5, /device:TPU:32, one launch (start us, length us, event | category | flops | bytes accessed | tf_op | source)
XLA Modules:
  0.0 98.1 jit_solution(11235131265207013158)
XLA Ops:
  0.6 3.6 %first_other.1 = (f32[17,8,128]{2,1,0:T(8,128)S(1)}, f32[2,8,128]{2,1,0:T(8,128)S(1)}, bf16[64,2048]{1,0:T(8,128)(2,1)S(1)}, bf16[512,2048]{1,0:T(8,128)(2,1)S(1)}, bf16[512,2048]{1,0:T(8,128)(2,1)S(1)}) custom-call(s32[1]{0:T(128)} %bitcast.place_ref, s32[8,128]{1,0:T(8,128)} %bitcast.4, f32[16,2048]{1,0:T(8,128)} %weights_hbm.1, f32[16,2048]{1,0:T(8,128)} %right_ref.3, ...), custom_call_target="tpu_custom_call" | custom-call | tf_op jit(solution)/shard_map/first_other/pallas_call | solution.py:420
  4.4 2.0 %collective-permute-start.1 = (f32[2,8,128]{2,1,0:T(8,128)S(1)}, f32[2,8,128]{2,1,0:T(8,128)S(1)}, u32[]{:S(2)}, u32[]{:S(2)}) collective-permute-start(f32[2,8,128]{2,1,0:T(8,128)S(1)} %get-tuple-element.34.count_ref), channel_id=1, source_target_pairs={{224,0},{66,2},{68,4},{230,6},{0,32},{98,34},{100,36},{6,38},{32,6... | collective-permute-start | bytes 24584 | tf_op jit(solution)/shard_map/ppermute | solution.py:403
  6.4 3.1 %first_own.1 = (f32[17,8,128]{2,1,0:T(8,128)S(1)}, bf16[512,2048]{1,0:T(8,128)(2,1)S(1)}, bf16[512,2048]{1,0:T(8,128)(2,1)S(1)}) custom-call(s32[1]{0:T(128)} %bitcast.place_ref, bf16[64,2048]{1,0:T(8,128)(2,1)S(1)} %get-tuple-element.31.left_ref, f32[17,8,128]{2,1,0:T(8,128)S(1)} %get-tuple-element.32.send_ref, f32[1024,2048]{1,0:T(8,128)} %features_ref.3), custom_call_target="tpu_custom_call" | custom-call | flops 201326592 | bytes 4194304 | tf_op jit(solution)/shard_map/first_own/pallas_call | solution.py:437
  9.6 2.8 %collective-permute-start.4 = (f32[17,8,128]{2,1,0:T(8,128)S(1)}, f32[17,8,128]{2,1,0:T(8,128)S(1)}, u32[]{:S(2)}, u32[]{:S(2)}) collective-permute-start(f32[17,8,128]{2,1,0:T(8,128)S(1)} %get-tuple-element.35.own_ref), channel_id=1, source_target_pairs={{0,24},{8,16},{16,8},{24,0},{1,25},{9,17},{17,9},{25,1},{2,26},{10... | collective-permute-start | bytes 208904 | tf_op jit(solution)/shard_map/ppermute | solution.py:408
  15.5 3.1 %collective-permute-done.3.two_ref = f32[17,8,128]{2,1,0:T(8,128)S(1)} collective-permute-done((f32[17,8,128]{2,1,0:T(8,128)S(1)}, f32[17,8,128]{2,1,0:T(8,128)S(1)}, u32[]{:S(2)}, u32[]{:S(2)}) %collective-permute-start.3) | collective-permute-done | bytes 69664 | tf_op jit(solution)/shard_map/ppermute | solution.py:408
  18.6 6.0 %collective-permute-start.8 = (f32[19,8,128]{2,1,0:T(8,128)S(1)}, f32[19,8,128]{2,1,0:T(8,128)S(1)}, u32[]{:S(2)}, u32[]{:S(2)}) collective-permute-start(f32[19,8,128]{2,1,0:T(8,128)S(1)} %middle.1.own_ref), channel_id=1, source_target_pairs={{0,6},{2,4},{4,2},{6,0},{1,7},{3,5},{5,3},{7,1},{8,14},{10,12},{12... | collective-permute-start | bytes 233480 | tf_op jit(solution)/shard_map/ppermute | solution.py:408
  24.6 2.5 %collective-permute-start.7 = (f32[19,8,128]{2,1,0:T(8,128)S(1)}, f32[19,8,128]{2,1,0:T(8,128)S(1)}, u32[]{:S(2)}, u32[]{:S(2)}) collective-permute-start(f32[19,8,128]{2,1,0:T(8,128)S(1)} %middle.1.own_ref), channel_id=1, source_target_pairs={{0,4},{2,6},{4,0},{6,2},{1,5},{3,7},{5,1},{7,3},{8,12},{10,14},{12... | collective-permute-start | bytes 233480 | tf_op jit(solution)/shard_map/ppermute | solution.py:408
  27.8 3.4 %collective-permute-done.7.two_ref = f32[19,8,128]{2,1,0:T(8,128)S(1)} collective-permute-done((f32[19,8,128]{2,1,0:T(8,128)S(1)}, f32[19,8,128]{2,1,0:T(8,128)S(1)}, u32[]{:S(2)}, u32[]{:S(2)}) %collective-permute-start.7) | collective-permute-done | bytes 77856 | tf_op jit(solution)/shard_map/ppermute | solution.py:408
  33.6 1.5 %collective-permute-start.10 = (f32[9,8,128]{2,1,0:T(8,128)S(1)}, f32[9,8,128]{2,1,0:T(8,128)S(1)}, u32[]{:S(2)}, u32[]{:S(2)}) collective-permute-start(f32[9,8,128]{2,1,0:T(8,128)S(1)} %get-tuple-element.43), channel_id=1, source_target_pairs={{0,32},{32,0},{64,96},{96,64},{128,160},{160,128},{192,224},{224,1... | collective-permute-start | bytes 110600 | tf_op jit(solution)/shard_map/ppermute | solution.py:408
  35.9 1.2 %collective-permute-start.12 = (f32[9,8,128]{2,1,0:T(8,128)S(1)}, f32[9,8,128]{2,1,0:T(8,128)S(1)}, u32[]{:S(2)}, u32[]{:S(2)}) collective-permute-start(f32[9,8,128]{2,1,0:T(8,128)S(1)} %get-tuple-element.45), channel_id=1, source_target_pairs={{0,96},{32,64},{64,32},{96,0},{128,224},{160,192},{192,160},{224,1... | collective-permute-start | bytes 110600 | tf_op jit(solution)/shard_map/ppermute | solution.py:408
  37.6 2.5 %collective-permute-done.11.refs_2_ = f32[9,8,128]{2,1,0:T(8,128)S(1)} collective-permute-done((f32[9,8,128]{2,1,0:T(8,128)S(1)}, f32[9,8,128]{2,1,0:T(8,128)S(1)}, u32[]{:S(2)}, u32[]{:S(2)}) %collective-permute-start.11) | collective-permute-done | bytes 36896 | tf_op jit(solution)/shard_map/ppermute | solution.py:408
  40.4 3.9 %collective-permute-start.13 = (f32[9,8,128]{2,1,0:T(8,128)S(1)}, f32[9,8,128]{2,1,0:T(8,128)S(1)}, u32[]{:S(2)}, u32[]{:S(2)}) collective-permute-start(f32[9,8,128]{2,1,0:T(8,128)S(1)} %add_half.2.refs_0_), channel_id=1, source_target_pairs={{0,224},{32,192},{64,160},{96,128},{128,96},{160,64},{192,32},{224... | collective-permute-start | bytes 110600 | tf_op jit(solution)/shard_map/ppermute | solution.py:415
  44.3 3.2 %collective-permute-done.13.refs_1_ = f32[9,8,128]{2,1,0:T(8,128)S(1)} collective-permute-done((f32[9,8,128]{2,1,0:T(8,128)S(1)}, f32[9,8,128]{2,1,0:T(8,128)S(1)}, u32[]{:S(2)}, u32[]{:S(2)}) %collective-permute-start.13) | collective-permute-done | bytes 36896 | tf_op jit(solution)/shard_map/ppermute | solution.py:415
  47.4 1.5 %collective-permute-start.16 = (f32[9,8,128]{2,1,0:T(8,128)S(1)}, f32[9,8,128]{2,1,0:T(8,128)S(1)}, u32[]{:S(2)}, u32[]{:S(2)}) collective-permute-start(f32[9,8,128]{2,1,0:T(8,128)S(1)} %add_tok.2.own_ref), channel_id=1, source_target_pairs={{0,96},{32,64},{64,32},{96,0},{128,224},{160,192},{192,160},{224,1... | collective-permute-start | bytes 110600 | tf_op jit(solution)/shard_map/ppermute | solution.py:408
  49.0 2.3 %collective-permute-start.15 = (f32[9,8,128]{2,1,0:T(8,128)S(1)}, f32[9,8,128]{2,1,0:T(8,128)S(1)}, u32[]{:S(2)}, u32[]{:S(2)}) collective-permute-start(f32[9,8,128]{2,1,0:T(8,128)S(1)} %add_tok.2.own_ref), channel_id=1, source_target_pairs={{0,64},{32,96},{64,0},{96,32},{128,192},{160,224},{192,128},{224,1... | collective-permute-start | bytes 110600 | tf_op jit(solution)/shard_map/ppermute | solution.py:408
  51.4 2.4 %collective-permute-done.15.two_ref = f32[9,8,128]{2,1,0:T(8,128)S(1)} collective-permute-done((f32[9,8,128]{2,1,0:T(8,128)S(1)}, f32[9,8,128]{2,1,0:T(8,128)S(1)}, u32[]{:S(2)}, u32[]{:S(2)}) %collective-permute-start.15) | collective-permute-done | bytes 36896 | tf_op jit(solution)/shard_map/ppermute | solution.py:408
  53.8 1.4 %collective-permute-done.14.one_ref = f32[9,8,128]{2,1,0:T(8,128)S(1)} collective-permute-done((f32[9,8,128]{2,1,0:T(8,128)S(1)}, f32[9,8,128]{2,1,0:T(8,128)S(1)}, u32[]{:S(2)}, u32[]{:S(2)}) %collective-permute-start.14) | collective-permute-done | bytes 36896 | tf_op jit(solution)/shard_map/ppermute | solution.py:408
  55.2 1.4 %residual_other.1 = (f32[9,8,128]{2,1,0:T(8,128)S(1)}, f32[16,2048]{1,0:T(8,128)S(1)}, f32[8,128]{1,0:T(8,128)S(1)}, bf16[32,2048]{1,0:T(8,128)(2,1)S(1)}) custom-call(s32[1]{0:T(128)} %bitcast.place_ref, f32[9,8,128]{2,1,0:T(8,128)S(1)} %add_tok.2.own_ref, f32[9,8,128]{2,1,0:T(8,128)S(1)} %collective-permute-done.14.one_ref, ...), custom_call_target="tpu_custom_call" | custom-call | tf_op jit(solution)/shard_map/residual_other/pallas_call | solution.py:476
  56.6 1.3 %residual_own.1.refs_0_ = f32[9,8,128]{2,1,0:T(8,128)S(1)} custom-call(bf16[32,2048]{1,0:T(8,128)(2,1)S(1)} %get-tuple-element.47.left_ref, bf16[512,2048]{1,0:T(8,128)(2,1)S(1)} %get-tuple-element.40.high_ref, bf16[512,2048]{1,0:T(8,128)(2,1)S(1)} %get-tuple-element.41.low_ref, f32[9,8,128]{2,1,0:T(8,128)S(1)} %get-tuple-element.48.send_ref), custom_call_target="tpu_custom_call" | custom-call | flops 201326592 | bytes 4194304 | tf_op jit(solution)/shard_map/residual_own/pallas_call | solution.py:483
  57.9 2.8 %collective-permute-start.20 = (f32[9,8,128]{2,1,0:T(8,128)S(1)}, f32[9,8,128]{2,1,0:T(8,128)S(1)}, u32[]{:S(2)}, u32[]{:S(2)}) collective-permute-start(f32[9,8,128]{2,1,0:T(8,128)S(1)} %add_core.1.refs_0_), channel_id=1, source_target_pairs={{0,24},{8,16},{16,8},{24,0},{1,25},{9,17},{17,9},{25,1},{2,26},{10... | collective-permute-start | bytes 110600 | tf_op jit(solution)/shard_map/ppermute | solution.py:408
  63.1 3.2 %collective-permute-done.19.refs_2_ = f32[9,8,128]{2,1,0:T(8,128)S(1)} collective-permute-done((f32[9,8,128]{2,1,0:T(8,128)S(1)}, f32[9,8,128]{2,1,0:T(8,128)S(1)}, u32[]{:S(2)}, u32[]{:S(2)}) %collective-permute-start.19) | collective-permute-done | bytes 36896 | tf_op jit(solution)/shard_map/ppermute | solution.py:408
  66.4 2.1 %collective-permute-start.23 = (f32[9,8,128]{2,1,0:T(8,128)S(1)}, f32[9,8,128]{2,1,0:T(8,128)S(1)}, u32[]{:S(2)}, u32[]{:S(2)}) collective-permute-start(f32[9,8,128]{2,1,0:T(8,128)S(1)} %add_x.1.refs_0_), channel_id=1, source_target_pairs={{0,6},{2,4},{4,2},{6,0},{1,7},{3,5},{5,3},{7,1},{8,14},{10,12},{12... | collective-permute-start | bytes 110600 | tf_op jit(solution)/shard_map/ppermute | solution.py:408
  69.4 1.2 %collective-permute-start.21 = (f32[9,8,128]{2,1,0:T(8,128)S(1)}, f32[9,8,128]{2,1,0:T(8,128)S(1)}, u32[]{:S(2)}, u32[]{:S(2)}) collective-permute-start(f32[9,8,128]{2,1,0:T(8,128)S(1)} %add_x.1.refs_0_), channel_id=1, source_target_pairs={{0,2},{2,0},{4,6},{6,4},{1,3},{3,1},{5,7},{7,5},{8,10},{10,8},{12,... | collective-permute-start | bytes 110600 | tf_op jit(solution)/shard_map/ppermute | solution.py:408
  70.6 1.4 %collective-permute-done.23.refs_3_ = f32[9,8,128]{2,1,0:T(8,128)S(1)} collective-permute-done((f32[9,8,128]{2,1,0:T(8,128)S(1)}, f32[9,8,128]{2,1,0:T(8,128)S(1)}, u32[]{:S(2)}, u32[]{:S(2)}) %collective-permute-start.23) | collective-permute-done | bytes 36896 | tf_op jit(solution)/shard_map/ppermute | solution.py:408
  72.0 2.0 %collective-permute-done.22.refs_2_ = f32[9,8,128]{2,1,0:T(8,128)S(1)} collective-permute-done((f32[9,8,128]{2,1,0:T(8,128)S(1)}, f32[9,8,128]{2,1,0:T(8,128)S(1)}, u32[]{:S(2)}, u32[]{:S(2)}) %collective-permute-start.22) | collective-permute-done | bytes 36896 | tf_op jit(solution)/shard_map/ppermute | solution.py:408
  76.9 2.0 %collective-permute-start.26 = (f32[9,8,128]{2,1,0:T(8,128)S(1)}, f32[9,8,128]{2,1,0:T(8,128)S(1)}, u32[]{:S(2)}, u32[]{:S(2)}) collective-permute-start(f32[9,8,128]{2,1,0:T(8,128)S(1)} %get-tuple-element.55), channel_id=1, source_target_pairs={{0,64},{32,96},{64,0},{96,32},{128,192},{160,224},{192,128},{224,1... | collective-permute-start | bytes 110600 | tf_op jit(solution)/shard_map/ppermute | solution.py:408
  80.3 1.6 %collective-permute-done.26.refs_2_ = f32[9,8,128]{2,1,0:T(8,128)S(1)} collective-permute-done((f32[9,8,128]{2,1,0:T(8,128)S(1)}, f32[9,8,128]{2,1,0:T(8,128)S(1)}, u32[]{:S(2)}, u32[]{:S(2)}) %collective-permute-start.26) | collective-permute-done | bytes 36896 | tf_op jit(solution)/shard_map/ppermute | solution.py:408
  81.9 1.2 %collective-permute-done.27.refs_3_ = f32[9,8,128]{2,1,0:T(8,128)S(1)} collective-permute-done((f32[9,8,128]{2,1,0:T(8,128)S(1)}, f32[9,8,128]{2,1,0:T(8,128)S(1)}, u32[]{:S(2)}, u32[]{:S(2)}) %collective-permute-start.27) | collective-permute-done | bytes 36896 | tf_op jit(solution)/shard_map/ppermute | solution.py:408
  83.1 4.0 %collective-permute-start.28 = (f32[9,8,128]{2,1,0:T(8,128)S(1)}, f32[9,8,128]{2,1,0:T(8,128)S(1)}, u32[]{:S(2)}, u32[]{:S(2)}) collective-permute-start(f32[9,8,128]{2,1,0:T(8,128)S(1)} %add_half.3.refs_0_), channel_id=1, source_target_pairs={{0,224},{32,192},{64,160},{96,128},{128,96},{160,64},{192,32},{224... | collective-permute-start | bytes 110600 | tf_op jit(solution)/shard_map/ppermute | solution.py:415
  87.1 3.1 %collective-permute-done.28.refs_1_ = f32[9,8,128]{2,1,0:T(8,128)S(1)} collective-permute-done((f32[9,8,128]{2,1,0:T(8,128)S(1)}, f32[9,8,128]{2,1,0:T(8,128)S(1)}, u32[]{:S(2)}, u32[]{:S(2)}) %collective-permute-start.28) | collective-permute-done | bytes 36896 | tf_op jit(solution)/shard_map/ppermute | solution.py:415
  91.3 2.0 %collective-permute-start.30 = (f32[9,8,128]{2,1,0:T(8,128)S(1)}, f32[9,8,128]{2,1,0:T(8,128)S(1)}, u32[]{:S(2)}, u32[]{:S(2)}) collective-permute-start(f32[9,8,128]{2,1,0:T(8,128)S(1)} %add_tok.3.own_ref), channel_id=1, source_target_pairs={{0,64},{32,96},{64,0},{96,32},{128,192},{160,224},{192,128},{224,1... | collective-permute-start | bytes 110600 | tf_op jit(solution)/shard_map/ppermute | solution.py:408
  94.2 2.0 %collective-permute-done.30.two_ref = f32[9,8,128]{2,1,0:T(8,128)S(1)} collective-permute-done((f32[9,8,128]{2,1,0:T(8,128)S(1)}, f32[9,8,128]{2,1,0:T(8,128)S(1)}, u32[]{:S(2)}, u32[]{:S(2)}) %collective-permute-start.30) | collective-permute-done | bytes 36896 | tf_op jit(solution)/shard_map/ppermute | solution.py:408
  (56 shorter events, 19.7 us)
Async XLA Ops:
  4.3 5.3 %collective-permute-start = (f32[17,8,128]{2,1,0:T(8,128)S(1)}, f32[17,8,128]{2,1,0:T(8,128)S(1)}, u32[]{:S(2)}, u32[]{:S(2)}) collective-permute-start(f32[17,8,128]{2,1,0:T(8,128)S(1)} %get-tuple-element.32.send_ref), channel_id=1, source_target_pairs={{0,1},{1,0},{2,3},{3,2},{4,5},{5,4},{6,7},{7,6},{8,9},{9,8},{10,11... | collective-permute-start | bytes 208904 | tf_op jit(solution)/shard_map/ppermute | solution.py:395
  4.4 5.1 %collective-permute-start.1 = (f32[2,8,128]{2,1,0:T(8,128)S(1)}, f32[2,8,128]{2,1,0:T(8,128)S(1)}, u32[]{:S(2)}, u32[]{:S(2)}) collective-permute-start(f32[2,8,128]{2,1,0:T(8,128)S(1)} %get-tuple-element.34.count_ref), channel_id=1, source_target_pairs={{224,0},{66,2},{68,4},{230,6},{0,32},{98,34},{100,36},{6,38},{32,6... | collective-permute-start | bytes 24584 | tf_op jit(solution)/shard_map/ppermute | solution.py:403
  9.6 5.9 %collective-permute-start.4 = (f32[17,8,128]{2,1,0:T(8,128)S(1)}, f32[17,8,128]{2,1,0:T(8,128)S(1)}, u32[]{:S(2)}, u32[]{:S(2)}) collective-permute-start(f32[17,8,128]{2,1,0:T(8,128)S(1)} %get-tuple-element.35.own_ref), channel_id=1, source_target_pairs={{0,24},{8,16},{16,8},{24,0},{1,25},{9,17},{17,9},{25,1},{2,26},{10... | collective-permute-start | bytes 208904 | tf_op jit(solution)/shard_map/ppermute | solution.py:408
  12.4 6.2 %collective-permute-start.3 = (f32[17,8,128]{2,1,0:T(8,128)S(1)}, f32[17,8,128]{2,1,0:T(8,128)S(1)}, u32[]{:S(2)}, u32[]{:S(2)}) collective-permute-start(f32[17,8,128]{2,1,0:T(8,128)S(1)} %get-tuple-element.35.own_ref), channel_id=1, source_target_pairs={{0,16},{8,24},{16,0},{24,8},{1,17},{9,25},{17,1},{25,9},{2,18},{10... | collective-permute-start | bytes 208904 | tf_op jit(solution)/shard_map/ppermute | solution.py:408
  13.2 5.4 %collective-permute-start.2 = (f32[17,8,128]{2,1,0:T(8,128)S(1)}, f32[17,8,128]{2,1,0:T(8,128)S(1)}, u32[]{:S(2)}, u32[]{:S(2)}) collective-permute-start(f32[17,8,128]{2,1,0:T(8,128)S(1)} %get-tuple-element.35.own_ref), channel_id=1, source_target_pairs={{0,8},{8,0},{16,24},{24,16},{1,9},{9,1},{17,25},{25,17},{2,10},{10... | collective-permute-start | bytes 208904 | tf_op jit(solution)/shard_map/ppermute | solution.py:408
  13.7 0.7 collective-permute-start.5
  18.6 9.2 %collective-permute-start.8 = (f32[19,8,128]{2,1,0:T(8,128)S(1)}, f32[19,8,128]{2,1,0:T(8,128)S(1)}, u32[]{:S(2)}, u32[]{:S(2)}) collective-permute-start(f32[19,8,128]{2,1,0:T(8,128)S(1)} %middle.1.own_ref), channel_id=1, source_target_pairs={{0,6},{2,4},{4,2},{6,0},{1,7},{3,5},{5,3},{7,1},{8,14},{10,12},{12... | collective-permute-start | bytes 233480 | tf_op jit(solution)/shard_map/ppermute | solution.py:408
  24.6 6.6 %collective-permute-start.7 = (f32[19,8,128]{2,1,0:T(8,128)S(1)}, f32[19,8,128]{2,1,0:T(8,128)S(1)}, u32[]{:S(2)}, u32[]{:S(2)}) collective-permute-start(f32[19,8,128]{2,1,0:T(8,128)S(1)} %middle.1.own_ref), channel_id=1, source_target_pairs={{0,4},{2,6},{4,0},{6,2},{1,5},{3,7},{5,1},{7,3},{8,12},{10,14},{12... | collective-permute-start | bytes 233480 | tf_op jit(solution)/shard_map/ppermute | solution.py:408
  27.1 4.4 %collective-permute-start.6 = (f32[19,8,128]{2,1,0:T(8,128)S(1)}, f32[19,8,128]{2,1,0:T(8,128)S(1)}, u32[]{:S(2)}, u32[]{:S(2)}) collective-permute-start(f32[19,8,128]{2,1,0:T(8,128)S(1)} %middle.1.own_ref), channel_id=1, source_target_pairs={{0,2},{2,0},{4,6},{6,4},{1,3},{3,1},{5,7},{7,5},{8,10},{10,8},{12,... | collective-permute-start | bytes 233480 | tf_op jit(solution)/shard_map/ppermute | solution.py:408
  31.6 1.3 %collective-permute-start.9 = (f32[9,8,128]{2,1,0:T(8,128)S(1)}, f32[9,8,128]{2,1,0:T(8,128)S(1)}, u32[]{:S(2)}, u32[]{:S(2)}) collective-permute-start(f32[9,8,128]{2,1,0:T(8,128)S(1)} %get-tuple-element.37.weighted_ref.own_ref), channel_id=1, source_target_pairs={{0,1},{1,0},{2,3},{3,2},{4,5},{5,4},{6,7},{7,6},{8,9},{9,8},{10,11... | collective-permute-start | bytes 110600 | tf_op jit(solution)/shard_map/ppermute | solution.py:395
  33.6 4.0 %collective-permute-start.10 = (f32[9,8,128]{2,1,0:T(8,128)S(1)}, f32[9,8,128]{2,1,0:T(8,128)S(1)}, u32[]{:S(2)}, u32[]{:S(2)}) collective-permute-start(f32[9,8,128]{2,1,0:T(8,128)S(1)} %get-tuple-element.43), channel_id=1, source_target_pairs={{0,32},{32,0},{64,96},{96,64},{128,160},{160,128},{192,224},{224,1... | collective-permute-start | bytes 110600 | tf_op jit(solution)/shard_map/ppermute | solution.py:408
  35.1 5.0 %collective-permute-start.11 = (f32[9,8,128]{2,1,0:T(8,128)S(1)}, f32[9,8,128]{2,1,0:T(8,128)S(1)}, u32[]{:S(2)}, u32[]{:S(2)}) collective-permute-start(f32[9,8,128]{2,1,0:T(8,128)S(1)} %get-tuple-element.44), channel_id=1, source_target_pairs={{0,64},{32,96},{64,0},{96,32},{128,192},{160,224},{192,128},{224,1... | collective-permute-start | bytes 110600 | tf_op jit(solution)/shard_map/ppermute | solution.py:408
  35.9 4.5 %collective-permute-start.12 = (f32[9,8,128]{2,1,0:T(8,128)S(1)}, f32[9,8,128]{2,1,0:T(8,128)S(1)}, u32[]{:S(2)}, u32[]{:S(2)}) collective-permute-start(f32[9,8,128]{2,1,0:T(8,128)S(1)} %get-tuple-element.45), channel_id=1, source_target_pairs={{0,96},{32,64},{64,32},{96,0},{128,224},{160,192},{192,160},{224,1... | collective-permute-start | bytes 110600 | tf_op jit(solution)/shard_map/ppermute | solution.py:408
  40.4 7.1 %collective-permute-start.13 = (f32[9,8,128]{2,1,0:T(8,128)S(1)}, f32[9,8,128]{2,1,0:T(8,128)S(1)}, u32[]{:S(2)}, u32[]{:S(2)}) collective-permute-start(f32[9,8,128]{2,1,0:T(8,128)S(1)} %add_half.2.refs_0_), channel_id=1, source_target_pairs={{0,224},{32,192},{64,160},{96,128},{128,96},{160,64},{192,32},{224... | collective-permute-start | bytes 110600 | tf_op jit(solution)/shard_map/ppermute | solution.py:415
  47.4 4.0 %collective-permute-start.16 = (f32[9,8,128]{2,1,0:T(8,128)S(1)}, f32[9,8,128]{2,1,0:T(8,128)S(1)}, u32[]{:S(2)}, u32[]{:S(2)}) collective-permute-start(f32[9,8,128]{2,1,0:T(8,128)S(1)} %add_tok.2.own_ref), channel_id=1, source_target_pairs={{0,96},{32,64},{64,32},{96,0},{128,224},{160,192},{192,160},{224,1... | collective-permute-start | bytes 110600 | tf_op jit(solution)/shard_map/ppermute | solution.py:408
  49.0 4.9 %collective-permute-start.15 = (f32[9,8,128]{2,1,0:T(8,128)S(1)}, f32[9,8,128]{2,1,0:T(8,128)S(1)}, u32[]{:S(2)}, u32[]{:S(2)}) collective-permute-start(f32[9,8,128]{2,1,0:T(8,128)S(1)} %add_tok.2.own_ref), channel_id=1, source_target_pairs={{0,64},{32,96},{64,0},{96,32},{128,192},{160,224},{192,128},{224,1... | collective-permute-start | bytes 110600 | tf_op jit(solution)/shard_map/ppermute | solution.py:408
  51.3 4.0 %collective-permute-start.14 = (f32[9,8,128]{2,1,0:T(8,128)S(1)}, f32[9,8,128]{2,1,0:T(8,128)S(1)}, u32[]{:S(2)}, u32[]{:S(2)}) collective-permute-start(f32[9,8,128]{2,1,0:T(8,128)S(1)} %add_tok.2.own_ref), channel_id=1, source_target_pairs={{0,32},{32,0},{64,96},{96,64},{128,160},{160,128},{192,224},{224,1... | collective-permute-start | bytes 110600 | tf_op jit(solution)/shard_map/ppermute | solution.py:408
  56.6 1.3 %collective-permute-start.17 = (f32[9,8,128]{2,1,0:T(8,128)S(1)}, f32[9,8,128]{2,1,0:T(8,128)S(1)}, u32[]{:S(2)}, u32[]{:S(2)}) collective-permute-start(f32[9,8,128]{2,1,0:T(8,128)S(1)} %get-tuple-element.48.send_ref), channel_id=1, source_target_pairs={{0,1},{1,0},{2,3},{3,2},{4,5},{5,4},{6,7},{7,6},{8,9},{9,8},{10,11... | collective-permute-start | bytes 110600 | tf_op jit(solution)/shard_map/ppermute | solution.py:395
  57.9 5.3 %collective-permute-start.20 = (f32[9,8,128]{2,1,0:T(8,128)S(1)}, f32[9,8,128]{2,1,0:T(8,128)S(1)}, u32[]{:S(2)}, u32[]{:S(2)}) collective-permute-start(f32[9,8,128]{2,1,0:T(8,128)S(1)} %add_core.1.refs_0_), channel_id=1, source_target_pairs={{0,24},{8,16},{16,8},{24,0},{1,25},{9,17},{17,9},{25,1},{2,26},{10... | collective-permute-start | bytes 110600 | tf_op jit(solution)/shard_map/ppermute | solution.py:408
  60.7 5.7 %collective-permute-start.19 = (f32[9,8,128]{2,1,0:T(8,128)S(1)}, f32[9,8,128]{2,1,0:T(8,128)S(1)}, u32[]{:S(2)}, u32[]{:S(2)}) collective-permute-start(f32[9,8,128]{2,1,0:T(8,128)S(1)} %add_core.1.refs_0_), channel_id=1, source_target_pairs={{0,16},{8,24},{16,0},{24,8},{1,17},{9,25},{17,1},{25,9},{2,18},{10... | collective-permute-start | bytes 110600 | tf_op jit(solution)/shard_map/ppermute | solution.py:408
  61.5 4.9 %collective-permute-start.18 = (f32[9,8,128]{2,1,0:T(8,128)S(1)}, f32[9,8,128]{2,1,0:T(8,128)S(1)}, u32[]{:S(2)}, u32[]{:S(2)}) collective-permute-start(f32[9,8,128]{2,1,0:T(8,128)S(1)} %add_core.1.refs_0_), channel_id=1, source_target_pairs={{0,8},{8,0},{16,24},{24,16},{1,9},{9,1},{17,25},{25,17},{2,10},{10... | collective-permute-start | bytes 110600 | tf_op jit(solution)/shard_map/ppermute | solution.py:408
  66.4 5.6 %collective-permute-start.23 = (f32[9,8,128]{2,1,0:T(8,128)S(1)}, f32[9,8,128]{2,1,0:T(8,128)S(1)}, u32[]{:S(2)}, u32[]{:S(2)}) collective-permute-start(f32[9,8,128]{2,1,0:T(8,128)S(1)} %add_x.1.refs_0_), channel_id=1, source_target_pairs={{0,6},{2,4},{4,2},{6,0},{1,7},{3,5},{5,3},{7,1},{8,14},{10,12},{12... | collective-permute-start | bytes 110600 | tf_op jit(solution)/shard_map/ppermute | solution.py:408
  68.5 5.5 %collective-permute-start.22 = (f32[9,8,128]{2,1,0:T(8,128)S(1)}, f32[9,8,128]{2,1,0:T(8,128)S(1)}, u32[]{:S(2)}, u32[]{:S(2)}) collective-permute-start(f32[9,8,128]{2,1,0:T(8,128)S(1)} %add_x.1.refs_0_), channel_id=1, source_target_pairs={{0,4},{2,6},{4,0},{6,2},{1,5},{3,7},{5,1},{7,3},{8,12},{10,14},{12... | collective-permute-start | bytes 110600 | tf_op jit(solution)/shard_map/ppermute | solution.py:408
  69.4 4.6 %collective-permute-start.21 = (f32[9,8,128]{2,1,0:T(8,128)S(1)}, f32[9,8,128]{2,1,0:T(8,128)S(1)}, u32[]{:S(2)}, u32[]{:S(2)}) collective-permute-start(f32[9,8,128]{2,1,0:T(8,128)S(1)} %add_x.1.refs_0_), channel_id=1, source_target_pairs={{0,2},{2,0},{4,6},{6,4},{1,3},{3,1},{5,7},{7,5},{8,10},{10,8},{12,... | collective-permute-start | bytes 110600 | tf_op jit(solution)/shard_map/ppermute | solution.py:408
  74.1 1.3 %collective-permute-start.24 = (f32[9,8,128]{2,1,0:T(8,128)S(1)}, f32[9,8,128]{2,1,0:T(8,128)S(1)}, u32[]{:S(2)}, u32[]{:S(2)}) collective-permute-start(f32[9,8,128]{2,1,0:T(8,128)S(1)} %get-tuple-element.52.weighted_ref.own_ref), channel_id=1, source_target_pairs={{0,1},{1,0},{2,3},{3,2},{4,5},{5,4},{6,7},{7,6},{8,9},{9,8},{10,11... | collective-permute-start | bytes 110600 | tf_op jit(solution)/shard_map/ppermute | solution.py:395
  76.1 4.1 %collective-permute-start.25 = (f32[9,8,128]{2,1,0:T(8,128)S(1)}, f32[9,8,128]{2,1,0:T(8,128)S(1)}, u32[]{:S(2)}, u32[]{:S(2)}) collective-permute-start(f32[9,8,128]{2,1,0:T(8,128)S(1)} %get-tuple-element.54), channel_id=1, source_target_pairs={{0,32},{32,0},{64,96},{96,64},{128,160},{160,128},{192,224},{224,1... | collective-permute-start | bytes 110600 | tf_op jit(solution)/shard_map/ppermute | solution.py:408
  76.9 5.0 %collective-permute-start.26 = (f32[9,8,128]{2,1,0:T(8,128)S(1)}, f32[9,8,128]{2,1,0:T(8,128)S(1)}, u32[]{:S(2)}, u32[]{:S(2)}) collective-permute-start(f32[9,8,128]{2,1,0:T(8,128)S(1)} %get-tuple-element.55), channel_id=1, source_target_pairs={{0,64},{32,96},{64,0},{96,32},{128,192},{160,224},{192,128},{224,1... | collective-permute-start | bytes 110600 | tf_op jit(solution)/shard_map/ppermute | solution.py:408
  78.9 4.2 %collective-permute-start.27 = (f32[9,8,128]{2,1,0:T(8,128)S(1)}, f32[9,8,128]{2,1,0:T(8,128)S(1)}, u32[]{:S(2)}, u32[]{:S(2)}) collective-permute-start(f32[9,8,128]{2,1,0:T(8,128)S(1)} %get-tuple-element.56), channel_id=1, source_target_pairs={{0,96},{32,64},{64,32},{96,0},{128,224},{160,192},{192,160},{224,1... | collective-permute-start | bytes 110600 | tf_op jit(solution)/shard_map/ppermute | solution.py:408
  83.1 7.2 %collective-permute-start.28 = (f32[9,8,128]{2,1,0:T(8,128)S(1)}, f32[9,8,128]{2,1,0:T(8,128)S(1)}, u32[]{:S(2)}, u32[]{:S(2)}) collective-permute-start(f32[9,8,128]{2,1,0:T(8,128)S(1)} %add_half.3.refs_0_), channel_id=1, source_target_pairs={{0,224},{32,192},{64,160},{96,128},{128,96},{160,64},{192,32},{224... | collective-permute-start | bytes 110600 | tf_op jit(solution)/shard_map/ppermute | solution.py:415
  90.3 4.0 %collective-permute-start.31 = (f32[9,8,128]{2,1,0:T(8,128)S(1)}, f32[9,8,128]{2,1,0:T(8,128)S(1)}, u32[]{:S(2)}, u32[]{:S(2)}) collective-permute-start(f32[9,8,128]{2,1,0:T(8,128)S(1)} %add_tok.3.own_ref), channel_id=1, source_target_pairs={{0,96},{32,64},{64,32},{96,0},{128,224},{160,192},{192,160},{224,1... | collective-permute-start | bytes 110600 | tf_op jit(solution)/shard_map/ppermute | solution.py:408
  91.3 4.9 %collective-permute-start.30 = (f32[9,8,128]{2,1,0:T(8,128)S(1)}, f32[9,8,128]{2,1,0:T(8,128)S(1)}, u32[]{:S(2)}, u32[]{:S(2)}) collective-permute-start(f32[9,8,128]{2,1,0:T(8,128)S(1)} %add_tok.3.own_ref), channel_id=1, source_target_pairs={{0,64},{32,96},{64,0},{96,32},{128,192},{160,224},{192,128},{224,1... | collective-permute-start | bytes 110600 | tf_op jit(solution)/shard_map/ppermute | solution.py:408
  93.3 4.0 %collective-permute-start.29 = (f32[9,8,128]{2,1,0:T(8,128)S(1)}, f32[9,8,128]{2,1,0:T(8,128)S(1)}, u32[]{:S(2)}, u32[]{:S(2)}) collective-permute-start(f32[9,8,128]{2,1,0:T(8,128)S(1)} %add_tok.3.own_ref), channel_id=1, source_target_pairs={{0,32},{32,0},{64,96},{96,64},{128,160},{160,128},{192,224},{224,1... | collective-permute-start | bytes 110600 | tf_op jit(solution)/shard_map/ppermute | solution.py:408
  (2 other events, 47.4 us)

commit v6 on v5

--- a/solution.py
+++ b/solution.py
@@ -377,7 +377,7 @@
     labels = labels.reshape(tokens // LANE, LANE)
     step = width // 4
     tok = lax.axis_index("tok").astype(jnp.int32)
-    role = jnp.minimum(tok, toks - 1 - tok)
+    role = (tok & 3) ^ (2 * (tok >> 2))
     place = (2 * role + lax.axis_index("core").astype(jnp.int32)).reshape(1)
     swap = [(0, 1), (1, 0)]
     half_product = pl.CostEstimate(
@@ -412,7 +412,7 @@
 
     def sum_over_tok(own, *rest):
         own = add("add_half", own, *from_others(list(rest), "tok"))
-        own = add("add_tok", own, lax.ppermute(own, "tok", [(i, toks - 1 - i) for i in range(toks)]))
+        own = add("add_tok", own, lax.ppermute(own, "tok", [(i, i ^ 6) for i in range(toks)]))
         return [own] + from_others(own, "tok")
 
     near, far = (-1, 2, 2, -1), (0, 1, 2, -2)

time: 98.2 us -> 99.2 us (1.010)
  starting transfers between devices: 46.2 us -> 49.4 us
  waiting for transfers between devices: 37.7 us -> 35.4 us
    ppermute x2, starting transfers between devices: 7.94 us -> 10.4 us  [sum_over_tok(): lax.ppermute(own, 'tok', [(i, i ^ 6) for i in range(toks)])]
    ppermute x2, waiting for transfers between devices: 6.27 us -> 3.88 us  [sum_over_tok(): lax.ppermute(own, 'tok', [(i, i ^ 6) for i in range(toks)])]
  transfers between devices with their start and end apart: 32 -> 32, of which waited for: 25 -> 23; matrix products, arithmetic and copies ran while one was open for 0% -> 0% of each run, Pallas kernels for 6% -> 6%
where the time goes in v6:
time: 99.2 us; the launch traced here: 99.1 us
  starting transfers between devices  49.4 us (50%)
  waiting for transfers between devices  35.4 us (36%)
  Pallas kernels  13.5 us (14%)
    ppermute x24, starting transfers between devices, from_others(): lax.ppermute(v, axis, [(i, i ^ d + 1) for i in range(count)])  36.1 us
    ppermute x24, waiting for transfers between devices, from_others(): lax.ppermute(v, axis, [(i, i ^ d + 1) for i in range(count)])  30.5 us
    ppermute x2, starting transfers between devices, sum_over_tok(): lax.ppermute(own, 'tok', [(i, i ^ 6) for i in range(toks)])  10.4 us
    ppermute x2, waiting for transfers between devices, sum_over_tok(): lax.ppermute(own, 'tok', [(i, i ^ 6) for i in range(toks)])  3.88 us
    pallas_call x1, Pallas kernels, on_device(): call(with_step(first_other_kernel), 'first_other', [SCALAR] + [IN_HBM] *...  3.62 us
    pallas_call x1, Pallas kernels, on_device(): call(with_step(first_own_kernel), 'first_own', [SCALAR, ON_CHIP, ON_CHIP,...  3.13 us
    ppermute x2, starting transfers between devices, from_tok(): return lax.ppermute(value, ('tok', 'y'), pairs)  2.65 us
  transfers between devices with their start and end apart: 32, of which 23 were waited for; matrix products, arithmetic and copies ran while one was open for 0% of the time, Pallas kernels for 6%

profile of v6, /device:TPU:32, one launch (start us, length us, event | category | flops | bytes accessed | tf_op | source)
XLA Modules:
  0.0 99.1 jit_solution(13815022523962949256)
XLA Ops:
  0.6 3.6 %first_other.1 = (f32[17,8,128]{2,1,0:T(8,128)S(1)}, f32[2,8,128]{2,1,0:T(8,128)S(1)}, bf16[64,2048]{1,0:T(8,128)(2,1)S(1)}, bf16[512,2048]{1,0:T(8,128)(2,1)S(1)}, bf16[512,2048]{1,0:T(8,128)(2,1)S(1)}) custom-call(s32[1]{0:T(128)} %bitcast.place_ref, s32[8,128]{1,0:T(8,128)} %bitcast.4, f32[16,2048]{1,0:T(8,128)} %weights_hbm.1, f32[16,2048]{1,0:T(8,128)} %right_ref.3, ...), custom_call_target="tpu_custom_call" | custom-call | tf_op jit(solution)/shard_map/first_other/pallas_call | solution.py:420
  4.4 2.0 %collective-permute-start.1 = (f32[2,8,128]{2,1,0:T(8,128)S(1)}, f32[2,8,128]{2,1,0:T(8,128)S(1)}, u32[]{:S(2)}, u32[]{:S(2)}) collective-permute-start(f32[2,8,128]{2,1,0:T(8,128)S(1)} %get-tuple-element.34.count_ref), channel_id=1, source_target_pairs={{224,0},{66,2},{68,4},{230,6},{0,32},{98,34},{100,36},{6,38},{32,6... | collective-permute-start | bytes 24584 | tf_op jit(solution)/shard_map/ppermute | solution.py:403
  6.4 3.1 %first_own.1 = (f32[17,8,128]{2,1,0:T(8,128)S(1)}, bf16[512,2048]{1,0:T(8,128)(2,1)S(1)}, bf16[512,2048]{1,0:T(8,128)(2,1)S(1)}) custom-call(s32[1]{0:T(128)} %bitcast.place_ref, bf16[64,2048]{1,0:T(8,128)(2,1)S(1)} %get-tuple-element.31.left_ref, f32[17,8,128]{2,1,0:T(8,128)S(1)} %get-tuple-element.32.send_ref, f32[1024,2048]{1,0:T(8,128)} %features_ref.3), custom_call_target="tpu_custom_call" | custom-call | flops 201326592 | bytes 4194304 | tf_op jit(solution)/shard_map/first_own/pallas_call | solution.py:437
  9.6 2.8 %collective-permute-start.4 = (f32[17,8,128]{2,1,0:T(8,128)S(1)}, f32[17,8,128]{2,1,0:T(8,128)S(1)}, u32[]{:S(2)}, u32[]{:S(2)}) collective-permute-start(f32[17,8,128]{2,1,0:T(8,128)S(1)} %get-tuple-element.35.own_ref), channel_id=1, source_target_pairs={{0,24},{8,16},{16,8},{24,0},{1,25},{9,17},{17,9},{25,1},{2,26},{10... | collective-permute-start | bytes 208904 | tf_op jit(solution)/shard_map/ppermute | solution.py:408
  15.5 3.1 %collective-permute-done.3.two_ref = f32[17,8,128]{2,1,0:T(8,128)S(1)} collective-permute-done((f32[17,8,128]{2,1,0:T(8,128)S(1)}, f32[17,8,128]{2,1,0:T(8,128)S(1)}, u32[]{:S(2)}, u32[]{:S(2)}) %collective-permute-start.3) | collective-permute-done | bytes 69664 | tf_op jit(solution)/shard_map/ppermute | solution.py:408
  18.6 6.0 %collective-permute-start.8 = (f32[19,8,128]{2,1,0:T(8,128)S(1)}, f32[19,8,128]{2,1,0:T(8,128)S(1)}, u32[]{:S(2)}, u32[]{:S(2)}) collective-permute-start(f32[19,8,128]{2,1,0:T(8,128)S(1)} %middle.1.own_ref), channel_id=1, source_target_pairs={{0,6},{2,4},{4,2},{6,0},{1,7},{3,5},{5,3},{7,1},{8,14},{10,12},{12... | collective-permute-start | bytes 233480 | tf_op jit(solution)/shard_map/ppermute | solution.py:408
  24.6 2.5 %collective-permute-start.7 = (f32[19,8,128]{2,1,0:T(8,128)S(1)}, f32[19,8,128]{2,1,0:T(8,128)S(1)}, u32[]{:S(2)}, u32[]{:S(2)}) collective-permute-start(f32[19,8,128]{2,1,0:T(8,128)S(1)} %middle.1.own_ref), channel_id=1, source_target_pairs={{0,4},{2,6},{4,0},{6,2},{1,5},{3,7},{5,1},{7,3},{8,12},{10,14},{12... | collective-permute-start | bytes 233480 | tf_op jit(solution)/shard_map/ppermute | solution.py:408
  27.8 3.4 %collective-permute-done.7.two_ref = f32[19,8,128]{2,1,0:T(8,128)S(1)} collective-permute-done((f32[19,8,128]{2,1,0:T(8,128)S(1)}, f32[19,8,128]{2,1,0:T(8,128)S(1)}, u32[]{:S(2)}, u32[]{:S(2)}) %collective-permute-start.7) | collective-permute-done | bytes 77856 | tf_op jit(solution)/shard_map/ppermute | solution.py:408
  33.6 1.5 %collective-permute-start.10 = (f32[9,8,128]{2,1,0:T(8,128)S(1)}, f32[9,8,128]{2,1,0:T(8,128)S(1)}, u32[]{:S(2)}, u32[]{:S(2)}) collective-permute-start(f32[9,8,128]{2,1,0:T(8,128)S(1)} %get-tuple-element.43), channel_id=1, source_target_pairs={{0,32},{32,0},{64,96},{96,64},{128,160},{160,128},{192,224},{224,1... | collective-permute-start | bytes 110600 | tf_op jit(solution)/shard_map/ppermute | solution.py:408
  35.9 1.2 %collective-permute-start.12 = (f32[9,8,128]{2,1,0:T(8,128)S(1)}, f32[9,8,128]{2,1,0:T(8,128)S(1)}, u32[]{:S(2)}, u32[]{:S(2)}) collective-permute-start(f32[9,8,128]{2,1,0:T(8,128)S(1)} %get-tuple-element.45), channel_id=1, source_target_pairs={{0,96},{32,64},{64,32},{96,0},{128,224},{160,192},{192,160},{224,1... | collective-permute-start | bytes 110600 | tf_op jit(solution)/shard_map/ppermute | solution.py:408
  37.6 2.5 %collective-permute-done.11.refs_2_ = f32[9,8,128]{2,1,0:T(8,128)S(1)} collective-permute-done((f32[9,8,128]{2,1,0:T(8,128)S(1)}, f32[9,8,128]{2,1,0:T(8,128)S(1)}, u32[]{:S(2)}, u32[]{:S(2)}) %collective-permute-start.11) | collective-permute-done | bytes 36896 | tf_op jit(solution)/shard_map/ppermute | solution.py:408
  40.4 5.7 %collective-permute-start.13 = (f32[9,8,128]{2,1,0:T(8,128)S(1)}, f32[9,8,128]{2,1,0:T(8,128)S(1)}, u32[]{:S(2)}, u32[]{:S(2)}) collective-permute-start(f32[9,8,128]{2,1,0:T(8,128)S(1)} %add_half.2.refs_0_), channel_id=1, source_target_pairs={{0,192},{32,224},{64,128},{96,160},{128,64},{160,96},{192,0},{224,... | collective-permute-start | bytes 110600 | tf_op jit(solution)/shard_map/ppermute | solution.py:415
  46.1 1.9 %collective-permute-done.13.refs_1_ = f32[9,8,128]{2,1,0:T(8,128)S(1)} collective-permute-done((f32[9,8,128]{2,1,0:T(8,128)S(1)}, f32[9,8,128]{2,1,0:T(8,128)S(1)}, u32[]{:S(2)}, u32[]{:S(2)}) %collective-permute-start.13) | collective-permute-done | bytes 36896 | tf_op jit(solution)/shard_map/ppermute | solution.py:415
  48.7 3.5 %collective-permute-start.15 = (f32[9,8,128]{2,1,0:T(8,128)S(1)}, f32[9,8,128]{2,1,0:T(8,128)S(1)}, u32[]{:S(2)}, u32[]{:S(2)}) collective-permute-start(f32[9,8,128]{2,1,0:T(8,128)S(1)} %add_tok.2.own_ref), channel_id=1, source_target_pairs={{0,64},{32,96},{64,0},{96,32},{128,192},{160,224},{192,128},{224,1... | collective-permute-start | bytes 110600 | tf_op jit(solution)/shard_map/ppermute | solution.py:408
  52.2 2.3 %collective-permute-done.15.two_ref = f32[9,8,128]{2,1,0:T(8,128)S(1)} collective-permute-done((f32[9,8,128]{2,1,0:T(8,128)S(1)}, f32[9,8,128]{2,1,0:T(8,128)S(1)}, u32[]{:S(2)}, u32[]{:S(2)}) %collective-permute-start.15) | collective-permute-done | bytes 36896 | tf_op jit(solution)/shard_map/ppermute | solution.py:408
  54.5 1.6 %collective-permute-done.14.one_ref = f32[9,8,128]{2,1,0:T(8,128)S(1)} collective-permute-done((f32[9,8,128]{2,1,0:T(8,128)S(1)}, f32[9,8,128]{2,1,0:T(8,128)S(1)}, u32[]{:S(2)}, u32[]{:S(2)}) %collective-permute-start.14) | collective-permute-done | bytes 36896 | tf_op jit(solution)/shard_map/ppermute | solution.py:408
  56.1 1.4 %residual_other.1 = (f32[9,8,128]{2,1,0:T(8,128)S(1)}, f32[16,2048]{1,0:T(8,128)S(1)}, f32[8,128]{1,0:T(8,128)S(1)}, bf16[32,2048]{1,0:T(8,128)(2,1)S(1)}) custom-call(s32[1]{0:T(128)} %bitcast.place_ref, f32[9,8,128]{2,1,0:T(8,128)S(1)} %add_tok.2.own_ref, f32[9,8,128]{2,1,0:T(8,128)S(1)} %collective-permute-done.14.one_ref, ...), custom_call_target="tpu_custom_call" | custom-call | tf_op jit(solution)/shard_map/residual_other/pallas_call | solution.py:476
  57.5 1.3 %residual_own.1.refs_0_ = f32[9,8,128]{2,1,0:T(8,128)S(1)} custom-call(bf16[32,2048]{1,0:T(8,128)(2,1)S(1)} %get-tuple-element.47.left_ref, bf16[512,2048]{1,0:T(8,128)(2,1)S(1)} %get-tuple-element.40.high_ref, bf16[512,2048]{1,0:T(8,128)(2,1)S(1)} %get-tuple-element.41.low_ref, f32[9,8,128]{2,1,0:T(8,128)S(1)} %get-tuple-element.48.send_ref), custom_call_target="tpu_custom_call" | custom-call | flops 201326592 | bytes 4194304 | tf_op jit(solution)/shard_map/residual_own/pallas_call | solution.py:483
  58.8 2.8 %collective-permute-start.20 = (f32[9,8,128]{2,1,0:T(8,128)S(1)}, f32[9,8,128]{2,1,0:T(8,128)S(1)}, u32[]{:S(2)}, u32[]{:S(2)}) collective-permute-start(f32[9,8,128]{2,1,0:T(8,128)S(1)} %add_core.1.refs_0_), channel_id=1, source_target_pairs={{0,24},{8,16},{16,8},{24,0},{1,25},{9,17},{17,9},{25,1},{2,26},{10... | collective-permute-start | bytes 110600 | tf_op jit(solution)/shard_map/ppermute | solution.py:408
  64.0 3.2 %collective-permute-done.19.refs_2_ = f32[9,8,128]{2,1,0:T(8,128)S(1)} collective-permute-done((f32[9,8,128]{2,1,0:T(8,128)S(1)}, f32[9,8,128]{2,1,0:T(8,128)S(1)}, u32[]{:S(2)}, u32[]{:S(2)}) %collective-permute-start.19) | collective-permute-done | bytes 36896 | tf_op jit(solution)/shard_map/ppermute | solution.py:408
  67.3 2.1 %collective-permute-start.23 = (f32[9,8,128]{2,1,0:T(8,128)S(1)}, f32[9,8,128]{2,1,0:T(8,128)S(1)}, u32[]{:S(2)}, u32[]{:S(2)}) collective-permute-start(f32[9,8,128]{2,1,0:T(8,128)S(1)} %add_x.1.refs_0_), channel_id=1, source_target_pairs={{0,6},{2,4},{4,2},{6,0},{1,7},{3,5},{5,3},{7,1},{8,14},{10,12},{12... | collective-permute-start | bytes 110600 | tf_op jit(solution)/shard_map/ppermute | solution.py:408
  70.3 1.2 %collective-permute-start.21 = (f32[9,8,128]{2,1,0:T(8,128)S(1)}, f32[9,8,128]{2,1,0:T(8,128)S(1)}, u32[]{:S(2)}, u32[]{:S(2)}) collective-permute-start(f32[9,8,128]{2,1,0:T(8,128)S(1)} %add_x.1.refs_0_), channel_id=1, source_target_pairs={{0,2},{2,0},{4,6},{6,4},{1,3},{3,1},{5,7},{7,5},{8,10},{10,8},{12,... | collective-permute-start | bytes 110600 | tf_op jit(solution)/shard_map/ppermute | solution.py:408
  71.5 1.4 %collective-permute-done.23.refs_3_ = f32[9,8,128]{2,1,0:T(8,128)S(1)} collective-permute-done((f32[9,8,128]{2,1,0:T(8,128)S(1)}, f32[9,8,128]{2,1,0:T(8,128)S(1)}, u32[]{:S(2)}, u32[]{:S(2)}) %collective-permute-start.23) | collective-permute-done | bytes 36896 | tf_op jit(solution)/shard_map/ppermute | solution.py:408
  72.9 2.0 %collective-permute-done.22.refs_2_ = f32[9,8,128]{2,1,0:T(8,128)S(1)} collective-permute-done((f32[9,8,128]{2,1,0:T(8,128)S(1)}, f32[9,8,128]{2,1,0:T(8,128)S(1)}, u32[]{:S(2)}, u32[]{:S(2)}) %collective-permute-start.22) | collective-permute-done | bytes 36896 | tf_op jit(solution)/shard_map/ppermute | solution.py:408
  77.4 1.9 %collective-permute-start.26 = (f32[9,8,128]{2,1,0:T(8,128)S(1)}, f32[9,8,128]{2,1,0:T(8,128)S(1)}, u32[]{:S(2)}, u32[]{:S(2)}) collective-permute-start(f32[9,8,128]{2,1,0:T(8,128)S(1)} %get-tuple-element.55), channel_id=1, source_target_pairs={{0,64},{32,96},{64,0},{96,32},{128,192},{160,224},{192,128},{224,1... | collective-permute-start | bytes 110600 | tf_op jit(solution)/shard_map/ppermute | solution.py:408
  79.3 1.2 %collective-permute-start.27 = (f32[9,8,128]{2,1,0:T(8,128)S(1)}, f32[9,8,128]{2,1,0:T(8,128)S(1)}, u32[]{:S(2)}, u32[]{:S(2)}) collective-permute-start(f32[9,8,128]{2,1,0:T(8,128)S(1)} %get-tuple-element.56), channel_id=1, source_target_pairs={{0,96},{32,64},{64,32},{96,0},{128,224},{160,192},{192,160},{224,1... | collective-permute-start | bytes 110600 | tf_op jit(solution)/shard_map/ppermute | solution.py:408
  82.4 1.2 %collective-permute-done.27.refs_3_ = f32[9,8,128]{2,1,0:T(8,128)S(1)} collective-permute-done((f32[9,8,128]{2,1,0:T(8,128)S(1)}, f32[9,8,128]{2,1,0:T(8,128)S(1)}, u32[]{:S(2)}, u32[]{:S(2)}) %collective-permute-start.27) | collective-permute-done | bytes 36896 | tf_op jit(solution)/shard_map/ppermute | solution.py:408
  83.7 4.7 %collective-permute-start.28 = (f32[9,8,128]{2,1,0:T(8,128)S(1)}, f32[9,8,128]{2,1,0:T(8,128)S(1)}, u32[]{:S(2)}, u32[]{:S(2)}) collective-permute-start(f32[9,8,128]{2,1,0:T(8,128)S(1)} %add_half.3.refs_0_), channel_id=1, source_target_pairs={{0,192},{32,224},{64,128},{96,160},{128,64},{160,96},{192,0},{224,... | collective-permute-start | bytes 110600 | tf_op jit(solution)/shard_map/ppermute | solution.py:415
  88.3 1.9 %collective-permute-done.28.refs_1_ = f32[9,8,128]{2,1,0:T(8,128)S(1)} collective-permute-done((f32[9,8,128]{2,1,0:T(8,128)S(1)}, f32[9,8,128]{2,1,0:T(8,128)S(1)}, u32[]{:S(2)}, u32[]{:S(2)}) %collective-permute-start.28) | collective-permute-done | bytes 36896 | tf_op jit(solution)/shard_map/ppermute | solution.py:415
  91.4 2.9 %collective-permute-start.30 = (f32[9,8,128]{2,1,0:T(8,128)S(1)}, f32[9,8,128]{2,1,0:T(8,128)S(1)}, u32[]{:S(2)}, u32[]{:S(2)}) collective-permute-start(f32[9,8,128]{2,1,0:T(8,128)S(1)} %add_tok.3.own_ref), channel_id=1, source_target_pairs={{0,64},{32,96},{64,0},{96,32},{128,192},{160,224},{192,128},{224,1... | collective-permute-start | bytes 110600 | tf_op jit(solution)/shard_map/ppermute | solution.py:408
  94.3 2.3 %collective-permute-done.30.two_ref = f32[9,8,128]{2,1,0:T(8,128)S(1)} collective-permute-done((f32[9,8,128]{2,1,0:T(8,128)S(1)}, f32[9,8,128]{2,1,0:T(8,128)S(1)}, u32[]{:S(2)}, u32[]{:S(2)}) %collective-permute-start.30) | collective-permute-done | bytes 36896 | tf_op jit(solution)/shard_map/ppermute | solution.py:408
  96.6 1.6 %collective-permute-done.29.one_ref = f32[9,8,128]{2,1,0:T(8,128)S(1)} collective-permute-done((f32[9,8,128]{2,1,0:T(8,128)S(1)}, f32[9,8,128]{2,1,0:T(8,128)S(1)}, u32[]{:S(2)}, u32[]{:S(2)}) %collective-permute-start.29) | collective-permute-done | bytes 36896 | tf_op jit(solution)/shard_map/ppermute | solution.py:408
  (56 shorter events, 18.5 us)
Async XLA Ops:
  4.3 5.3 %collective-permute-start = (f32[17,8,128]{2,1,0:T(8,128)S(1)}, f32[17,8,128]{2,1,0:T(8,128)S(1)}, u32[]{:S(2)}, u32[]{:S(2)}) collective-permute-start(f32[17,8,128]{2,1,0:T(8,128)S(1)} %get-tuple-element.32.send_ref), channel_id=1, source_target_pairs={{0,1},{1,0},{2,3},{3,2},{4,5},{5,4},{6,7},{7,6},{8,9},{9,8},{10,11... | collective-permute-start | bytes 208904 | tf_op jit(solution)/shard_map/ppermute | solution.py:395
  4.4 5.1 %collective-permute-start.1 = (f32[2,8,128]{2,1,0:T(8,128)S(1)}, f32[2,8,128]{2,1,0:T(8,128)S(1)}, u32[]{:S(2)}, u32[]{:S(2)}) collective-permute-start(f32[2,8,128]{2,1,0:T(8,128)S(1)} %get-tuple-element.34.count_ref), channel_id=1, source_target_pairs={{224,0},{66,2},{68,4},{230,6},{0,32},{98,34},{100,36},{6,38},{32,6... | collective-permute-start | bytes 24584 | tf_op jit(solution)/shard_map/ppermute | solution.py:403
  9.6 5.9 %collective-permute-start.4 = (f32[17,8,128]{2,1,0:T(8,128)S(1)}, f32[17,8,128]{2,1,0:T(8,128)S(1)}, u32[]{:S(2)}, u32[]{:S(2)}) collective-permute-start(f32[17,8,128]{2,1,0:T(8,128)S(1)} %get-tuple-element.35.own_ref), channel_id=1, source_target_pairs={{0,24},{8,16},{16,8},{24,0},{1,25},{9,17},{17,9},{25,1},{2,26},{10... | collective-permute-start | bytes 208904 | tf_op jit(solution)/shard_map/ppermute | solution.py:408
  12.4 6.2 %collective-permute-start.3 = (f32[17,8,128]{2,1,0:T(8,128)S(1)}, f32[17,8,128]{2,1,0:T(8,128)S(1)}, u32[]{:S(2)}, u32[]{:S(2)}) collective-permute-start(f32[17,8,128]{2,1,0:T(8,128)S(1)} %get-tuple-element.35.own_ref), channel_id=1, source_target_pairs={{0,16},{8,24},{16,0},{24,8},{1,17},{9,25},{17,1},{25,9},{2,18},{10... | collective-permute-start | bytes 208904 | tf_op jit(solution)/shard_map/ppermute | solution.py:408
  13.2 5.4 %collective-permute-start.2 = (f32[17,8,128]{2,1,0:T(8,128)S(1)}, f32[17,8,128]{2,1,0:T(8,128)S(1)}, u32[]{:S(2)}, u32[]{:S(2)}) collective-permute-start(f32[17,8,128]{2,1,0:T(8,128)S(1)} %get-tuple-element.35.own_ref), channel_id=1, source_target_pairs={{0,8},{8,0},{16,24},{24,16},{1,9},{9,1},{17,25},{25,17},{2,10},{10... | collective-permute-start | bytes 208904 | tf_op jit(solution)/shard_map/ppermute | solution.py:408
  13.7 0.7 collective-permute-start.5
  18.6 9.2 %collective-permute-start.8 = (f32[19,8,128]{2,1,0:T(8,128)S(1)}, f32[19,8,128]{2,1,0:T(8,128)S(1)}, u32[]{:S(2)}, u32[]{:S(2)}) collective-permute-start(f32[19,8,128]{2,1,0:T(8,128)S(1)} %middle.1.own_ref), channel_id=1, source_target_pairs={{0,6},{2,4},{4,2},{6,0},{1,7},{3,5},{5,3},{7,1},{8,14},{10,12},{12... | collective-permute-start | bytes 233480 | tf_op jit(solution)/shard_map/ppermute | solution.py:408
  24.6 6.6 %collective-permute-start.7 = (f32[19,8,128]{2,1,0:T(8,128)S(1)}, f32[19,8,128]{2,1,0:T(8,128)S(1)}, u32[]{:S(2)}, u32[]{:S(2)}) collective-permute-start(f32[19,8,128]{2,1,0:T(8,128)S(1)} %middle.1.own_ref), channel_id=1, source_target_pairs={{0,4},{2,6},{4,0},{6,2},{1,5},{3,7},{5,1},{7,3},{8,12},{10,14},{12... | collective-permute-start | bytes 233480 | tf_op jit(solution)/shard_map/ppermute | solution.py:408
  27.1 4.4 %collective-permute-start.6 = (f32[19,8,128]{2,1,0:T(8,128)S(1)}, f32[19,8,128]{2,1,0:T(8,128)S(1)}, u32[]{:S(2)}, u32[]{:S(2)}) collective-permute-start(f32[19,8,128]{2,1,0:T(8,128)S(1)} %middle.1.own_ref), channel_id=1, source_target_pairs={{0,2},{2,0},{4,6},{6,4},{1,3},{3,1},{5,7},{7,5},{8,10},{10,8},{12,... | collective-permute-start | bytes 233480 | tf_op jit(solution)/shard_map/ppermute | solution.py:408
  31.6 1.3 %collective-permute-start.9 = (f32[9,8,128]{2,1,0:T(8,128)S(1)}, f32[9,8,128]{2,1,0:T(8,128)S(1)}, u32[]{:S(2)}, u32[]{:S(2)}) collective-permute-start(f32[9,8,128]{2,1,0:T(8,128)S(1)} %get-tuple-element.37.weighted_ref.own_ref), channel_id=1, source_target_pairs={{0,1},{1,0},{2,3},{3,2},{4,5},{5,4},{6,7},{7,6},{8,9},{9,8},{10,11... | collective-permute-start | bytes 110600 | tf_op jit(solution)/shard_map/ppermute | solution.py:395
  33.6 4.0 %collective-permute-start.10 = (f32[9,8,128]{2,1,0:T(8,128)S(1)}, f32[9,8,128]{2,1,0:T(8,128)S(1)}, u32[]{:S(2)}, u32[]{:S(2)}) collective-permute-start(f32[9,8,128]{2,1,0:T(8,128)S(1)} %get-tuple-element.43), channel_id=1, source_target_pairs={{0,32},{32,0},{64,96},{96,64},{128,160},{160,128},{192,224},{224,1... | collective-permute-start | bytes 110600 | tf_op jit(solution)/shard_map/ppermute | solution.py:408
  35.1 5.0 %collective-permute-start.11 = (f32[9,8,128]{2,1,0:T(8,128)S(1)}, f32[9,8,128]{2,1,0:T(8,128)S(1)}, u32[]{:S(2)}, u32[]{:S(2)}) collective-permute-start(f32[9,8,128]{2,1,0:T(8,128)S(1)} %get-tuple-element.44), channel_id=1, source_target_pairs={{0,64},{32,96},{64,0},{96,32},{128,192},{160,224},{192,128},{224,1... | collective-permute-start | bytes 110600 | tf_op jit(solution)/shard_map/ppermute | solution.py:408
  35.9 4.5 %collective-permute-start.12 = (f32[9,8,128]{2,1,0:T(8,128)S(1)}, f32[9,8,128]{2,1,0:T(8,128)S(1)}, u32[]{:S(2)}, u32[]{:S(2)}) collective-permute-start(f32[9,8,128]{2,1,0:T(8,128)S(1)} %get-tuple-element.45), channel_id=1, source_target_pairs={{0,96},{32,64},{64,32},{96,0},{128,224},{160,192},{192,160},{224,1... | collective-permute-start | bytes 110600 | tf_op jit(solution)/shard_map/ppermute | solution.py:408
  40.4 7.6 %collective-permute-start.13 = (f32[9,8,128]{2,1,0:T(8,128)S(1)}, f32[9,8,128]{2,1,0:T(8,128)S(1)}, u32[]{:S(2)}, u32[]{:S(2)}) collective-permute-start(f32[9,8,128]{2,1,0:T(8,128)S(1)} %add_half.2.refs_0_), channel_id=1, source_target_pairs={{0,192},{32,224},{64,128},{96,160},{128,64},{160,96},{192,0},{224,... | collective-permute-start | bytes 110600 | tf_op jit(solution)/shard_map/ppermute | solution.py:415
  48.0 4.2 %collective-permute-start.16 = (f32[9,8,128]{2,1,0:T(8,128)S(1)}, f32[9,8,128]{2,1,0:T(8,128)S(1)}, u32[]{:S(2)}, u32[]{:S(2)}) collective-permute-start(f32[9,8,128]{2,1,0:T(8,128)S(1)} %add_tok.2.own_ref), channel_id=1, source_target_pairs={{0,96},{32,64},{64,32},{96,0},{128,224},{160,192},{192,160},{224,1... | collective-permute-start | bytes 110600 | tf_op jit(solution)/shard_map/ppermute | solution.py:408
  48.7 5.8 %collective-permute-start.15 = (f32[9,8,128]{2,1,0:T(8,128)S(1)}, f32[9,8,128]{2,1,0:T(8,128)S(1)}, u32[]{:S(2)}, u32[]{:S(2)}) collective-permute-start(f32[9,8,128]{2,1,0:T(8,128)S(1)} %add_tok.2.own_ref), channel_id=1, source_target_pairs={{0,64},{32,96},{64,0},{96,32},{128,192},{160,224},{192,128},{224,1... | collective-permute-start | bytes 110600 | tf_op jit(solution)/shard_map/ppermute | solution.py:408
  52.2 4.0 %collective-permute-start.14 = (f32[9,8,128]{2,1,0:T(8,128)S(1)}, f32[9,8,128]{2,1,0:T(8,128)S(1)}, u32[]{:S(2)}, u32[]{:S(2)}) collective-permute-start(f32[9,8,128]{2,1,0:T(8,128)S(1)} %add_tok.2.own_ref), channel_id=1, source_target_pairs={{0,32},{32,0},{64,96},{96,64},{128,160},{160,128},{192,224},{224,1... | collective-permute-start | bytes 110600 | tf_op jit(solution)/shard_map/ppermute | solution.py:408
  57.5 1.3 %collective-permute-start.17 = (f32[9,8,128]{2,1,0:T(8,128)S(1)}, f32[9,8,128]{2,1,0:T(8,128)S(1)}, u32[]{:S(2)}, u32[]{:S(2)}) collective-permute-start(f32[9,8,128]{2,1,0:T(8,128)S(1)} %get-tuple-element.48.send_ref), channel_id=1, source_target_pairs={{0,1},{1,0},{2,3},{3,2},{4,5},{5,4},{6,7},{7,6},{8,9},{9,8},{10,11... | collective-permute-start | bytes 110600 | tf_op jit(solution)/shard_map/ppermute | solution.py:395
  58.8 5.3 %collective-permute-start.20 = (f32[9,8,128]{2,1,0:T(8,128)S(1)}, f32[9,8,128]{2,1,0:T(8,128)S(1)}, u32[]{:S(2)}, u32[]{:S(2)}) collective-permute-start(f32[9,8,128]{2,1,0:T(8,128)S(1)} %add_core.1.refs_0_), channel_id=1, source_target_pairs={{0,24},{8,16},{16,8},{24,0},{1,25},{9,17},{17,9},{25,1},{2,26},{10... | collective-permute-start | bytes 110600 | tf_op jit(solution)/shard_map/ppermute | solution.py:408
  61.6 5.7 %collective-permute-start.19 = (f32[9,8,128]{2,1,0:T(8,128)S(1)}, f32[9,8,128]{2,1,0:T(8,128)S(1)}, u32[]{:S(2)}, u32[]{:S(2)}) collective-permute-start(f32[9,8,128]{2,1,0:T(8,128)S(1)} %add_core.1.refs_0_), channel_id=1, source_target_pairs={{0,16},{8,24},{16,0},{24,8},{1,17},{9,25},{17,1},{25,9},{2,18},{10... | collective-permute-start | bytes 110600 | tf_op jit(solution)/shard_map/ppermute | solution.py:408
  62.4 4.9 %collective-permute-start.18 = (f32[9,8,128]{2,1,0:T(8,128)S(1)}, f32[9,8,128]{2,1,0:T(8,128)S(1)}, u32[]{:S(2)}, u32[]{:S(2)}) collective-permute-start(f32[9,8,128]{2,1,0:T(8,128)S(1)} %add_core.1.refs_0_), channel_id=1, source_target_pairs={{0,8},{8,0},{16,24},{24,16},{1,9},{9,1},{17,25},{25,17},{2,10},{10... | collective-permute-start | bytes 110600 | tf_op jit(solution)/shard_map/ppermute | solution.py:408
  67.3 5.6 %collective-permute-start.23 = (f32[9,8,128]{2,1,0:T(8,128)S(1)}, f32[9,8,128]{2,1,0:T(8,128)S(1)}, u32[]{:S(2)}, u32[]{:S(2)}) collective-permute-start(f32[9,8,128]{2,1,0:T(8,128)S(1)} %add_x.1.refs_0_), channel_id=1, source_target_pairs={{0,6},{2,4},{4,2},{6,0},{1,7},{3,5},{5,3},{7,1},{8,14},{10,12},{12... | collective-permute-start | bytes 110600 | tf_op jit(solution)/shard_map/ppermute | solution.py:408
  69.4 5.5 %collective-permute-start.22 = (f32[9,8,128]{2,1,0:T(8,128)S(1)}, f32[9,8,128]{2,1,0:T(8,128)S(1)}, u32[]{:S(2)}, u32[]{:S(2)}) collective-permute-start(f32[9,8,128]{2,1,0:T(8,128)S(1)} %add_x.1.refs_0_), channel_id=1, source_target_pairs={{0,4},{2,6},{4,0},{6,2},{1,5},{3,7},{5,1},{7,3},{8,12},{10,14},{12... | collective-permute-start | bytes 110600 | tf_op jit(solution)/shard_map/ppermute | solution.py:408
  70.3 4.6 %collective-permute-start.21 = (f32[9,8,128]{2,1,0:T(8,128)S(1)}, f32[9,8,128]{2,1,0:T(8,128)S(1)}, u32[]{:S(2)}, u32[]{:S(2)}) collective-permute-start(f32[9,8,128]{2,1,0:T(8,128)S(1)} %add_x.1.refs_0_), channel_id=1, source_target_pairs={{0,2},{2,0},{4,6},{6,4},{1,3},{3,1},{5,7},{7,5},{8,10},{10,8},{12,... | collective-permute-start | bytes 110600 | tf_op jit(solution)/shard_map/ppermute | solution.py:408
  75.0 1.3 %collective-permute-start.24 = (f32[9,8,128]{2,1,0:T(8,128)S(1)}, f32[9,8,128]{2,1,0:T(8,128)S(1)}, u32[]{:S(2)}, u32[]{:S(2)}) collective-permute-start(f32[9,8,128]{2,1,0:T(8,128)S(1)} %get-tuple-element.52.weighted_ref.own_ref), channel_id=1, source_target_pairs={{0,1},{1,0},{2,3},{3,2},{4,5},{5,4},{6,7},{7,6},{8,9},{9,8},{10,11... | collective-permute-start | bytes 110600 | tf_op jit(solution)/shard_map/ppermute | solution.py:395
  77.0 4.2 %collective-permute-start.25 = (f32[9,8,128]{2,1,0:T(8,128)S(1)}, f32[9,8,128]{2,1,0:T(8,128)S(1)}, u32[]{:S(2)}, u32[]{:S(2)}) collective-permute-start(f32[9,8,128]{2,1,0:T(8,128)S(1)} %get-tuple-element.54), channel_id=1, source_target_pairs={{0,32},{32,0},{64,96},{96,64},{128,160},{160,128},{192,224},{224,1... | collective-permute-start | bytes 110600 | tf_op jit(solution)/shard_map/ppermute | solution.py:408
  77.4 5.0 %collective-permute-start.26 = (f32[9,8,128]{2,1,0:T(8,128)S(1)}, f32[9,8,128]{2,1,0:T(8,128)S(1)}, u32[]{:S(2)}, u32[]{:S(2)}) collective-permute-start(f32[9,8,128]{2,1,0:T(8,128)S(1)} %get-tuple-element.55), channel_id=1, source_target_pairs={{0,64},{32,96},{64,0},{96,32},{128,192},{160,224},{192,128},{224,1... | collective-permute-start | bytes 110600 | tf_op jit(solution)/shard_map/ppermute | solution.py:408
  79.3 4.3 %collective-permute-start.27 = (f32[9,8,128]{2,1,0:T(8,128)S(1)}, f32[9,8,128]{2,1,0:T(8,128)S(1)}, u32[]{:S(2)}, u32[]{:S(2)}) collective-permute-start(f32[9,8,128]{2,1,0:T(8,128)S(1)} %get-tuple-element.56), channel_id=1, source_target_pairs={{0,96},{32,64},{64,32},{96,0},{128,224},{160,192},{192,160},{224,1... | collective-permute-start | bytes 110600 | tf_op jit(solution)/shard_map/ppermute | solution.py:408
  83.7 6.6 %collective-permute-start.28 = (f32[9,8,128]{2,1,0:T(8,128)S(1)}, f32[9,8,128]{2,1,0:T(8,128)S(1)}, u32[]{:S(2)}, u32[]{:S(2)}) collective-permute-start(f32[9,8,128]{2,1,0:T(8,128)S(1)} %add_half.3.refs_0_), channel_id=1, source_target_pairs={{0,192},{32,224},{64,128},{96,160},{128,64},{160,96},{192,0},{224,... | collective-permute-start | bytes 110600 | tf_op jit(solution)/shard_map/ppermute | solution.py:415
  90.3 4.0 %collective-permute-start.31 = (f32[9,8,128]{2,1,0:T(8,128)S(1)}, f32[9,8,128]{2,1,0:T(8,128)S(1)}, u32[]{:S(2)}, u32[]{:S(2)}) collective-permute-start(f32[9,8,128]{2,1,0:T(8,128)S(1)} %add_tok.3.own_ref), channel_id=1, source_target_pairs={{0,96},{32,64},{64,32},{96,0},{128,224},{160,192},{192,160},{224,1... | collective-permute-start | bytes 110600 | tf_op jit(solution)/shard_map/ppermute | solution.py:408
  91.4 5.2 %collective-permute-start.30 = (f32[9,8,128]{2,1,0:T(8,128)S(1)}, f32[9,8,128]{2,1,0:T(8,128)S(1)}, u32[]{:S(2)}, u32[]{:S(2)}) collective-permute-start(f32[9,8,128]{2,1,0:T(8,128)S(1)} %add_tok.3.own_ref), channel_id=1, source_target_pairs={{0,64},{32,96},{64,0},{96,32},{128,192},{160,224},{192,128},{224,1... | collective-permute-start | bytes 110600 | tf_op jit(solution)/shard_map/ppermute | solution.py:408
  94.3 4.0 %collective-permute-start.29 = (f32[9,8,128]{2,1,0:T(8,128)S(1)}, f32[9,8,128]{2,1,0:T(8,128)S(1)}, u32[]{:S(2)}, u32[]{:S(2)}) collective-permute-start(f32[9,8,128]{2,1,0:T(8,128)S(1)} %add_tok.3.own_ref), channel_id=1, source_target_pairs={{0,32},{32,0},{64,96},{96,64},{128,160},{160,128},{192,224},{224,1... | collective-permute-start | bytes 110600 | tf_op jit(solution)/shard_map/ppermute | solution.py:408
  (2 other events, 48.3 us)

commit v7 on v5

--- a/solution.py
+++ b/solution.py
@@ -291,79 +291,115 @@
     return jnp.concatenate(rows, axis=0)
 
 
-def project_kept(left_ref, high_ref, low_ref):
-    classes = left_ref.shape[0] // 2
+def project_block(left, at, high_ref, low_ref):
+    classes = left.shape[0] // 2
+    both = lax.dot_general(left, high_ref[:, at], ROWS_WITH_ROWS, preferred_element_type=f32)
+    rest = lax.dot_general(left[:classes], low_ref[:, at], ROWS_WITH_ROWS, preferred_element_type=f32)
+    return both[:classes] + both[classes:] + rest
+
+
+def block_at(step, place_ref, d):
+    return pl.ds(pl.multiple_of(((place_ref[0] >> 1) ^ d) * step, step), step)
+
+
+def residual_block(at, piece_ref, rate, right_ref, residual_ref, left_ref):
+    classes = right_ref.shape[0]
+    right = right_ref[:, at]
+    residual = right - rate * (columns_of(piece_ref, classes) + ridge_strength * right)
+    residual_ref[:, at] = residual
+    high, low = parts(residual)
+    left_ref[:classes, at] = high
+    left_ref[classes:, at] = low
+
+
+def residual_start_kernel(
+    step,
+    place_ref,
+    own_ref,
+    norm_ref,
+    right_ref,
+    high_own_ref,
+    low_own_ref,
+    high_other_ref,
+    low_other_ref,
+    rate_ref,
+    residual_ref,
+    share_own_ref,
+    share_other_ref,
+    left_ref,
+):
+    norm_now = norm_ref[0:1, 0:1]
+    curve = total(own_ref[own_ref.shape[0] - 1])
+    rate = norm_now / (curve + ridge_strength * norm_now)
+    rate_ref[...] = jnp.broadcast_to(rate, (SUB, LANE))
+    at = block_at(step, place_ref, 0)
+    classes = right_ref.shape[0]
+    right = right_ref[:, at]
+    residual = right - rate * (columns_of(own_ref, classes) + ridge_strength * right)
+    residual_ref[...] = residual
+    high, low = parts(residual)
+    left_ref[:classes] = high
+    left_ref[classes:] = low
     left = left_ref[...]
-    both = lax.dot_general(left, high_ref[...], ROWS_WITH_ROWS, preferred_element_type=f32)
-    rest = lax.dot_general(left[:classes], low_ref[...], ROWS_WITH_ROWS, preferred_element_type=f32)
-    return both[:classes] + both[classes:] + rest
+    share_own_ref[...] = project_block(left, at, high_own_ref, low_own_ref)
+    share_other_ref[...] = project_block(left, at, high_other_ref, low_other_ref)
 
 
 def residual_other_kernel(
     step,
     place_ref,
-    own_ref,
     one_ref,
     two_ref,
     three_ref,
-    norm_ref,
+    rate_ref,
+    start_ref,
+    share_ref,
     right_ref,
     high_ref,
     low_ref,
     send_ref,
     residual_ref,
-    rate_ref,
     left_ref,
 ):
-    classes = right_ref.shape[0]
-    norm_now = norm_ref[0:1, 0:1]
-    curve = total(own_ref[own_ref.shape[0] - 1])
-    rate = norm_now / (curve + ridge_strength * norm_now)
-    rate_ref[...] = jnp.broadcast_to(rate, (SUB, LANE))
-    for d, piece_ref in enumerate((own_ref, one_ref, two_ref, three_ref)):
-        at = pl.ds(pl.multiple_of(((place_ref[0] >> 1) ^ d) * step, step), step)
-        right = right_ref[:, at]
-        residual = right - rate * (columns_of(piece_ref, classes) + ridge_strength * right)
-        residual_ref[:, at] = residual
-        high, low = parts(residual)
-        left_ref[:classes, at] = high
-        left_ref[classes:, at] = low
+    rate = rate_ref[0:1, 0:1]
+    residual_ref[:, block_at(step, place_ref, 0)] = start_ref[...]
+    for d, piece_ref in enumerate((one_ref, two_ref, three_ref)):
+        residual_block(block_at(step, place_ref, d + 1), piece_ref, rate, right_ref, residual_ref, left_ref)
     right, residual = right_ref[...], residual_ref[...]
     norm, cross = fold(residual * residual), fold(residual * right)
     sums = jnp.concatenate([norm[:4] + norm[4:], cross[:4] + cross[4:]])
-    store_tiles(send_ref, project_kept(left_ref, high_ref, low_ref), sums)
-
-
-def residual_own_kernel(left_ref, high_ref, low_ref, send_ref, keep_ref):
-    store_tiles(keep_ref, project_kept(left_ref, high_ref, low_ref), send_ref[send_ref.shape[0] - 1])
-
-
-def last_kernel(
-    step,
-    place_ref,
-    own_ref,
-    one_ref,
-    two_ref,
-    three_ref,
-    numbers_ref,
-    rate_ref,
-    right_ref,
-    old_ref,
-    solution_ref,
-    residual_ref,
-):
-    classes = right_ref.shape[0]
+    value = share_ref[...]
+    for d in range(1, 4):
+        at = block_at(step, place_ref, d)
+        value += project_block(left_ref[:, at], at, high_ref, low_ref)
+    store_tiles(send_ref, value, sums)
+
+
+def residual_own_kernel(step, place_ref, left_ref, share_ref, high_ref, low_ref, send_ref, keep_ref):
+    value = share_ref[...]
+    for d in range(1, 4):
+        at = block_at(step, place_ref, d)
+        value += project_block(left_ref[:, at], at, high_ref, low_ref)
+    store_tiles(keep_ref, value, send_ref[send_ref.shape[0] - 1])
+
+
+def finish_kernel(own_ref, numbers_ref, rate_ref, right_ref, old_ref, solution_ref, base_ref, last_rate_ref):
     norm_next, ratio, norm_direction = [numbers_ref[i, 0:1, 0:1] for i in range(3)]
     curve = total(own_ref[own_ref.shape[0] - 1])
     rate = norm_next / (curve + ridge_strength * norm_direction)
-    rate_first = rate_ref[0:1, 0:1]
+    right, old = right_ref[...], old_ref[...]
+    direction = old + ratio * right
+    solution_ref[...] = rate_ref[0:1, 0:1] * right + rate * direction
+    base_ref[...] = old - rate * (ridge_strength * direction)
+    last_rate_ref[...] = jnp.broadcast_to(rate, (SUB, LANE))
+
+
+def last_kernel(step, place_ref, own_ref, one_ref, two_ref, three_ref, base_ref, rate_ref, residual_ref):
+    classes = base_ref.shape[0]
+    rate = rate_ref[0:1, 0:1]
     for d, piece_ref in enumerate((own_ref, one_ref, two_ref, three_ref)):
         at = pl.ds(pl.multiple_of(((place_ref[0] >> 1) ^ d) * step, step), step)
-        right, old = right_ref[:, at], old_ref[:, at]
-        direction = old + ratio * right
-        image = columns_of(piece_ref, classes) + ridge_strength * direction
-        solution_ref[:, at] = rate_first * right + rate * direction
-        residual_ref[:, at] = old - rate * image
+        residual_ref[:, at] = base_ref[:, at] - rate * columns_of(piece_ref, classes)
 
 
 def on_device(features, labels, weights, right_side):
@@ -473,16 +509,25 @@
     pieces = sum_over_tok(*image(weighted))
 
     kept = groups * across + 1
-    send, residual, rate, left = call(
+    share = pltpu.VMEM((classes, half), f32)
+    rate, start, share_own, share_other = call(
+        with_step(residual_start_kernel),
+        "residual_start",
+        [SCALAR] + [ON_CHIP] * 7,
+        [tiles(), pltpu.VMEM((classes, step), f32), share, share],
+        [pltpu.VMEM((2 * classes, step), bf16)],
+        cost=half_product,
+    )(place, pieces[0], norm_now, right_side, high_own, low_own, high_other, low_other)
+    send, residual, left = call(
         with_step(residual_other_kernel),
         "residual_other",
-        [SCALAR] + [ON_CHIP] * 8,
-        [tiles(kept), pltpu.VMEM((classes, width), f32), tiles(), pltpu.VMEM((2 * classes, width), bf16)],
-    )(place, *pieces, norm_now, right_side, high_other, low_other)
+        [SCALAR] + [ON_CHIP] * 9,
+        [tiles(kept), pltpu.VMEM((classes, width), f32), pltpu.VMEM((2 * classes, width), bf16)],
+    )(place, *pieces[1:], rate, start, share_other, right_side, high_other, low_other)
     got = swapped(send)
-    keep = call(residual_own_kernel, "residual_own", [ON_CHIP] * 4, tiles(kept), cost=half_product)(
-        left, high_own, low_own, send
-    )
+    keep = call(
+        with_step(residual_own_kernel), "residual_own", [SCALAR] + [ON_CHIP] * 5, tiles(kept), cost=half_product
+    )(place, left, share_own, high_own, low_own, send)
     own = add("add_core", keep, got)
     own = add("add_x", own, *from_others(own, "x"))
     own = add("add_y", own, *from_others(own, "y"))
@@ -491,11 +536,15 @@
     )
     pieces = sum_over_tok(*image(weighted))
     out = jax.ShapeDtypeStruct((classes, width), f32)
-    return tuple(
-        call(with_step(last_kernel), "last", [SCALAR] + [ON_CHIP] * 8, [out, out])(
-            place, *pieces, numbers, rate, right_side, residual
-        )
-    )
+    solution, base, rate = call(
+        finish_kernel,
+        "finish",
+        [ON_CHIP] * 5,
+        [out, pltpu.VMEM((classes, width), f32), tiles()],
+        cost=half_product,
+    )(pieces[0], numbers, rate, right_side, residual)
+    residual = call(with_step(last_kernel), "last", [SCALAR] + [ON_CHIP] * 6, out)(place, *pieces, base, rate)
+    return solution, residual
 
 
 def solution(mesh):

time: 98.2 us -> 97.4 us (level)
  waiting for transfers between devices: 37.7 us -> 36.2 us
    ppermute x24, waiting for transfers between devices: 30.4 us -> 28.7 us  [from_others(): lax.ppermute(v, axis, [(i, i ^ d + 1) for i in range(count)])]
    pallas_call x2 -> x4, Pallas kernels: 2.13 us -> 3.27 us  [the longest x1 0.98 us: on_device(): call(with_step(residual_own_kernel), 'residual_own', [SCALAR] + [ON_CHIP]...]
  transfers between devices with their start and end apart: 32 -> 32, of which waited for: 25 -> 24; matrix products, arithmetic and copies ran while one was open for 0% -> 0% of each run, Pallas kernels for 6% -> 7%
where the time goes in v7:
time: 97.4 us; the launch traced here: 97.3 us
  starting transfers between devices  46.1 us (47%)
  waiting for transfers between devices  36.2 us (37%)
  Pallas kernels  14.2 us (15%)
    ppermute x24, starting transfers between devices, from_others(): lax.ppermute(v, axis, [(i, i ^ d + 1) for i in range(count)])  35.2 us
    ppermute x24, waiting for transfers between devices, from_others(): lax.ppermute(v, axis, [(i, i ^ d + 1) for i in range(count)])  28.7 us
    ppermute x2, starting transfers between devices, sum_over_tok(): lax.ppermute(own, 'tok', [(i, toks - 1 - i) for i in range(toks)])  7.94 us
    ppermute x2, waiting for transfers between devices, sum_over_tok(): lax.ppermute(own, 'tok', [(i, toks - 1 - i) for i in range(toks)])  6.27 us
    pallas_call x1, Pallas kernels, on_device(): call(with_step(first_other_kernel), 'first_other', [SCALAR] + [IN_HBM] *...  3.62 us
    pallas_call x1, Pallas kernels, on_device(): call(with_step(first_own_kernel), 'first_own', [SCALAR, ON_CHIP, ON_CHIP,...  3.13 us
    ppermute x2, starting transfers between devices, from_tok(): return lax.ppermute(value, ('tok', 'y'), pairs)  2.65 us
  transfers between devices with their start and end apart: 32, of which 24 were waited for; matrix products, arithmetic and copies ran while one was open for 0% of the time, Pallas kernels for 7%

profile of v7, /device:TPU:32, one launch (start us, length us, event | category | flops | bytes accessed | tf_op | source)
XLA Modules:
  0.0 97.3 jit_solution(9732420764499464959)
XLA Ops:
  0.6 3.6 %first_other.1 = (f32[17,8,128]{2,1,0:T(8,128)S(1)}, f32[2,8,128]{2,1,0:T(8,128)S(1)}, bf16[64,2048]{1,0:T(8,128)(2,1)S(1)}, bf16[512,2048]{1,0:T(8,128)(2,1)S(1)}, bf16[512,2048]{1,0:T(8,128)(2,1)S(1)}) custom-call(s32[1]{0:T(128)} %bitcast.place_ref, s32[8,128]{1,0:T(8,128)} %bitcast.4, f32[16,2048]{1,0:T(8,128)} %weights_hbm.1, f32[16,2048]{1,0:T(8,128)} %right_ref.5, ...), custom_call_target="tpu_custom_call" | custom-call | tf_op jit(solution)/shard_map/first_other/pallas_call | solution.py:456
  4.4 2.0 %collective-permute-start.1 = (f32[2,8,128]{2,1,0:T(8,128)S(1)}, f32[2,8,128]{2,1,0:T(8,128)S(1)}, u32[]{:S(2)}, u32[]{:S(2)}) collective-permute-start(f32[2,8,128]{2,1,0:T(8,128)S(1)} %get-tuple-element.40.count_ref), channel_id=1, source_target_pairs={{224,0},{66,2},{68,4},{230,6},{0,32},{98,34},{100,36},{6,38},{32,6... | collective-permute-start | bytes 24584 | tf_op jit(solution)/shard_map/ppermute | solution.py:439
  6.4 3.1 %first_own.1 = (f32[17,8,128]{2,1,0:T(8,128)S(1)}, bf16[512,2048]{1,0:T(8,128)(2,1)S(1)}, bf16[512,2048]{1,0:T(8,128)(2,1)S(1)}) custom-call(s32[1]{0:T(128)} %bitcast.place_ref, bf16[64,2048]{1,0:T(8,128)(2,1)S(1)} %get-tuple-element.37.left_ref, f32[17,8,128]{2,1,0:T(8,128)S(1)} %get-tuple-element.38.send_ref, f32[1024,2048]{1,0:T(8,128)} %features_ref.3), custom_call_target="tpu_custom_call" | custom-call | flops 201326592 | bytes 4194304 | tf_op jit(solution)/shard_map/first_own/pallas_call | solution.py:473
  9.6 2.8 %collective-permute-start.4 = (f32[17,8,128]{2,1,0:T(8,128)S(1)}, f32[17,8,128]{2,1,0:T(8,128)S(1)}, u32[]{:S(2)}, u32[]{:S(2)}) collective-permute-start(f32[17,8,128]{2,1,0:T(8,128)S(1)} %get-tuple-element.41.own_ref), channel_id=1, source_target_pairs={{0,24},{8,16},{16,8},{24,0},{1,25},{9,17},{17,9},{25,1},{2,26},{10... | collective-permute-start | bytes 208904 | tf_op jit(solution)/shard_map/ppermute | solution.py:444
  14.4 1.1 %collective-permute-done.4.three_ref = f32[17,8,128]{2,1,0:T(8,128)S(1)} collective-permute-done((f32[17,8,128]{2,1,0:T(8,128)S(1)}, f32[17,8,128]{2,1,0:T(8,128)S(1)}, u32[]{:S(2)}, u32[]{:S(2)}) %collective-permute-start.4) | collective-permute-done | bytes 69664 | tf_op jit(solution)/shard_map/ppermute | solution.py:444
  15.5 3.1 %collective-permute-done.3.two_ref = f32[17,8,128]{2,1,0:T(8,128)S(1)} collective-permute-done((f32[17,8,128]{2,1,0:T(8,128)S(1)}, f32[17,8,128]{2,1,0:T(8,128)S(1)}, u32[]{:S(2)}, u32[]{:S(2)}) %collective-permute-start.3) | collective-permute-done | bytes 69664 | tf_op jit(solution)/shard_map/ppermute | solution.py:444
  18.6 6.0 %collective-permute-start.8 = (f32[19,8,128]{2,1,0:T(8,128)S(1)}, f32[19,8,128]{2,1,0:T(8,128)S(1)}, u32[]{:S(2)}, u32[]{:S(2)}) collective-permute-start(f32[19,8,128]{2,1,0:T(8,128)S(1)} %middle.1.own_ref), channel_id=1, source_target_pairs={{0,6},{2,4},{4,2},{6,0},{1,7},{3,5},{5,3},{7,1},{8,14},{10,12},{12... | collective-permute-start | bytes 233480 | tf_op jit(solution)/shard_map/ppermute | solution.py:444
  24.6 2.5 %collective-permute-start.7 = (f32[19,8,128]{2,1,0:T(8,128)S(1)}, f32[19,8,128]{2,1,0:T(8,128)S(1)}, u32[]{:S(2)}, u32[]{:S(2)}) collective-permute-start(f32[19,8,128]{2,1,0:T(8,128)S(1)} %middle.1.own_ref), channel_id=1, source_target_pairs={{0,4},{2,6},{4,0},{6,2},{1,5},{3,7},{5,1},{7,3},{8,12},{10,14},{12... | collective-permute-start | bytes 233480 | tf_op jit(solution)/shard_map/ppermute | solution.py:444
  27.8 3.4 %collective-permute-done.7.two_ref = f32[19,8,128]{2,1,0:T(8,128)S(1)} collective-permute-done((f32[19,8,128]{2,1,0:T(8,128)S(1)}, f32[19,8,128]{2,1,0:T(8,128)S(1)}, u32[]{:S(2)}, u32[]{:S(2)}) %collective-permute-start.7) | collective-permute-done | bytes 77856 | tf_op jit(solution)/shard_map/ppermute | solution.py:444
  33.6 1.5 %collective-permute-start.10 = (f32[9,8,128]{2,1,0:T(8,128)S(1)}, f32[9,8,128]{2,1,0:T(8,128)S(1)}, u32[]{:S(2)}, u32[]{:S(2)}) collective-permute-start(f32[9,8,128]{2,1,0:T(8,128)S(1)} %get-tuple-element.49), channel_id=1, source_target_pairs={{0,32},{32,0},{64,96},{96,64},{128,160},{160,128},{192,224},{224,1... | collective-permute-start | bytes 110600 | tf_op jit(solution)/shard_map/ppermute | solution.py:444
  35.9 1.2 %collective-permute-start.12 = (f32[9,8,128]{2,1,0:T(8,128)S(1)}, f32[9,8,128]{2,1,0:T(8,128)S(1)}, u32[]{:S(2)}, u32[]{:S(2)}) collective-permute-start(f32[9,8,128]{2,1,0:T(8,128)S(1)} %get-tuple-element.51), channel_id=1, source_target_pairs={{0,96},{32,64},{64,32},{96,0},{128,224},{160,192},{192,160},{224,1... | collective-permute-start | bytes 110600 | tf_op jit(solution)/shard_map/ppermute | solution.py:444
  37.6 2.5 %collective-permute-done.11.refs_2_ = f32[9,8,128]{2,1,0:T(8,128)S(1)} collective-permute-done((f32[9,8,128]{2,1,0:T(8,128)S(1)}, f32[9,8,128]{2,1,0:T(8,128)S(1)}, u32[]{:S(2)}, u32[]{:S(2)}) %collective-permute-start.11) | collective-permute-done | bytes 36896 | tf_op jit(solution)/shard_map/ppermute | solution.py:444
  40.4 3.9 %collective-permute-start.13 = (f32[9,8,128]{2,1,0:T(8,128)S(1)}, f32[9,8,128]{2,1,0:T(8,128)S(1)}, u32[]{:S(2)}, u32[]{:S(2)}) collective-permute-start(f32[9,8,128]{2,1,0:T(8,128)S(1)} %add_half.2.refs_0_), channel_id=1, source_target_pairs={{0,224},{32,192},{64,160},{96,128},{128,96},{160,64},{192,32},{224... | collective-permute-start | bytes 110600 | tf_op jit(solution)/shard_map/ppermute | solution.py:451
  44.3 3.2 %collective-permute-done.13.refs_1_ = f32[9,8,128]{2,1,0:T(8,128)S(1)} collective-permute-done((f32[9,8,128]{2,1,0:T(8,128)S(1)}, f32[9,8,128]{2,1,0:T(8,128)S(1)}, u32[]{:S(2)}, u32[]{:S(2)}) %collective-permute-start.13) | collective-permute-done | bytes 36896 | tf_op jit(solution)/shard_map/ppermute | solution.py:451
  47.4 1.5 %collective-permute-start.16 = (f32[9,8,128]{2,1,0:T(8,128)S(1)}, f32[9,8,128]{2,1,0:T(8,128)S(1)}, u32[]{:S(2)}, u32[]{:S(2)}) collective-permute-start(f32[9,8,128]{2,1,0:T(8,128)S(1)} %add_tok.2.own_ref), channel_id=1, source_target_pairs={{0,96},{32,64},{64,32},{96,0},{128,224},{160,192},{192,160},{224,1... | collective-permute-start | bytes 110600 | tf_op jit(solution)/shard_map/ppermute | solution.py:444
  49.0 2.3 %collective-permute-start.15 = (f32[9,8,128]{2,1,0:T(8,128)S(1)}, f32[9,8,128]{2,1,0:T(8,128)S(1)}, u32[]{:S(2)}, u32[]{:S(2)}) collective-permute-start(f32[9,8,128]{2,1,0:T(8,128)S(1)} %add_tok.2.own_ref), channel_id=1, source_target_pairs={{0,64},{32,96},{64,0},{96,32},{128,192},{160,224},{192,128},{224,1... | collective-permute-start | bytes 110600 | tf_op jit(solution)/shard_map/ppermute | solution.py:444
  52.0 1.8 %collective-permute-done.15.two_ref = f32[9,8,128]{2,1,0:T(8,128)S(1)} collective-permute-done((f32[9,8,128]{2,1,0:T(8,128)S(1)}, f32[9,8,128]{2,1,0:T(8,128)S(1)}, u32[]{:S(2)}, u32[]{:S(2)}) %collective-permute-start.15) | collective-permute-done | bytes 36896 | tf_op jit(solution)/shard_map/ppermute | solution.py:444
  53.8 1.4 %collective-permute-done.14.one_ref = f32[9,8,128]{2,1,0:T(8,128)S(1)} collective-permute-done((f32[9,8,128]{2,1,0:T(8,128)S(1)}, f32[9,8,128]{2,1,0:T(8,128)S(1)}, u32[]{:S(2)}, u32[]{:S(2)}) %collective-permute-start.14) | collective-permute-done | bytes 36896 | tf_op jit(solution)/shard_map/ppermute | solution.py:444
  57.4 2.8 %collective-permute-start.20 = (f32[9,8,128]{2,1,0:T(8,128)S(1)}, f32[9,8,128]{2,1,0:T(8,128)S(1)}, u32[]{:S(2)}, u32[]{:S(2)}) collective-permute-start(f32[9,8,128]{2,1,0:T(8,128)S(1)} %add_core.1.refs_0_), channel_id=1, source_target_pairs={{0,24},{8,16},{16,8},{24,0},{1,25},{9,17},{17,9},{25,1},{2,26},{10... | collective-permute-start | bytes 110600 | tf_op jit(solution)/shard_map/ppermute | solution.py:444
  61.6 1.1 %collective-permute-done.20.refs_3_ = f32[9,8,128]{2,1,0:T(8,128)S(1)} collective-permute-done((f32[9,8,128]{2,1,0:T(8,128)S(1)}, f32[9,8,128]{2,1,0:T(8,128)S(1)}, u32[]{:S(2)}, u32[]{:S(2)}) %collective-permute-start.20) | collective-permute-done | bytes 36896 | tf_op jit(solution)/shard_map/ppermute | solution.py:444
  62.6 3.1 %collective-permute-done.19.refs_2_ = f32[9,8,128]{2,1,0:T(8,128)S(1)} collective-permute-done((f32[9,8,128]{2,1,0:T(8,128)S(1)}, f32[9,8,128]{2,1,0:T(8,128)S(1)}, u32[]{:S(2)}, u32[]{:S(2)}) %collective-permute-start.19) | collective-permute-done | bytes 36896 | tf_op jit(solution)/shard_map/ppermute | solution.py:444
  65.7 2.1 %collective-permute-start.23 = (f32[9,8,128]{2,1,0:T(8,128)S(1)}, f32[9,8,128]{2,1,0:T(8,128)S(1)}, u32[]{:S(2)}, u32[]{:S(2)}) collective-permute-start(f32[9,8,128]{2,1,0:T(8,128)S(1)} %add_x.1.refs_0_), channel_id=1, source_target_pairs={{0,6},{2,4},{4,2},{6,0},{1,7},{3,5},{5,3},{7,1},{8,14},{10,12},{12... | collective-permute-start | bytes 110600 | tf_op jit(solution)/shard_map/ppermute | solution.py:444
  68.7 1.2 %collective-permute-start.21 = (f32[9,8,128]{2,1,0:T(8,128)S(1)}, f32[9,8,128]{2,1,0:T(8,128)S(1)}, u32[]{:S(2)}, u32[]{:S(2)}) collective-permute-start(f32[9,8,128]{2,1,0:T(8,128)S(1)} %add_x.1.refs_0_), channel_id=1, source_target_pairs={{0,2},{2,0},{4,6},{6,4},{1,3},{3,1},{5,7},{7,5},{8,10},{10,8},{12,... | collective-permute-start | bytes 110600 | tf_op jit(solution)/shard_map/ppermute | solution.py:444
  69.9 1.4 %collective-permute-done.23.refs_3_ = f32[9,8,128]{2,1,0:T(8,128)S(1)} collective-permute-done((f32[9,8,128]{2,1,0:T(8,128)S(1)}, f32[9,8,128]{2,1,0:T(8,128)S(1)}, u32[]{:S(2)}, u32[]{:S(2)}) %collective-permute-start.23) | collective-permute-done | bytes 36896 | tf_op jit(solution)/shard_map/ppermute | solution.py:444
  71.3 2.0 %collective-permute-done.22.refs_2_ = f32[9,8,128]{2,1,0:T(8,128)S(1)} collective-permute-done((f32[9,8,128]{2,1,0:T(8,128)S(1)}, f32[9,8,128]{2,1,0:T(8,128)S(1)}, u32[]{:S(2)}, u32[]{:S(2)}) %collective-permute-start.22) | collective-permute-done | bytes 36896 | tf_op jit(solution)/shard_map/ppermute | solution.py:444
  76.2 2.0 %collective-permute-start.26 = (f32[9,8,128]{2,1,0:T(8,128)S(1)}, f32[9,8,128]{2,1,0:T(8,128)S(1)}, u32[]{:S(2)}, u32[]{:S(2)}) collective-permute-start(f32[9,8,128]{2,1,0:T(8,128)S(1)} %get-tuple-element.65), channel_id=1, source_target_pairs={{0,64},{32,96},{64,0},{96,32},{128,192},{160,224},{192,128},{224,1... | collective-permute-start | bytes 110600 | tf_op jit(solution)/shard_map/ppermute | solution.py:444
  79.6 1.6 %collective-permute-done.26.refs_2_ = f32[9,8,128]{2,1,0:T(8,128)S(1)} collective-permute-done((f32[9,8,128]{2,1,0:T(8,128)S(1)}, f32[9,8,128]{2,1,0:T(8,128)S(1)}, u32[]{:S(2)}, u32[]{:S(2)}) %collective-permute-start.26) | collective-permute-done | bytes 36896 | tf_op jit(solution)/shard_map/ppermute | solution.py:444
  81.2 1.2 %collective-permute-done.27.refs_3_ = f32[9,8,128]{2,1,0:T(8,128)S(1)} collective-permute-done((f32[9,8,128]{2,1,0:T(8,128)S(1)}, f32[9,8,128]{2,1,0:T(8,128)S(1)}, u32[]{:S(2)}, u32[]{:S(2)}) %collective-permute-start.27) | collective-permute-done | bytes 36896 | tf_op jit(solution)/shard_map/ppermute | solution.py:444
  82.4 4.0 %collective-permute-start.28 = (f32[9,8,128]{2,1,0:T(8,128)S(1)}, f32[9,8,128]{2,1,0:T(8,128)S(1)}, u32[]{:S(2)}, u32[]{:S(2)}) collective-permute-start(f32[9,8,128]{2,1,0:T(8,128)S(1)} %add_half.3.refs_0_), channel_id=1, source_target_pairs={{0,224},{32,192},{64,160},{96,128},{128,96},{160,64},{192,32},{224... | collective-permute-start | bytes 110600 | tf_op jit(solution)/shard_map/ppermute | solution.py:451
  86.5 3.1 %collective-permute-done.28.refs_1_ = f32[9,8,128]{2,1,0:T(8,128)S(1)} collective-permute-done((f32[9,8,128]{2,1,0:T(8,128)S(1)}, f32[9,8,128]{2,1,0:T(8,128)S(1)}, u32[]{:S(2)}, u32[]{:S(2)}) %collective-permute-start.28) | collective-permute-done | bytes 36896 | tf_op jit(solution)/shard_map/ppermute | solution.py:451
  90.7 2.0 %collective-permute-start.30 = (f32[9,8,128]{2,1,0:T(8,128)S(1)}, f32[9,8,128]{2,1,0:T(8,128)S(1)}, u32[]{:S(2)}, u32[]{:S(2)}) collective-permute-start(f32[9,8,128]{2,1,0:T(8,128)S(1)} %add_tok.3.own_ref), channel_id=1, source_target_pairs={{0,64},{32,96},{64,0},{96,32},{128,192},{160,224},{192,128},{224,1... | collective-permute-start | bytes 110600 | tf_op jit(solution)/shard_map/ppermute | solution.py:444
  93.9 1.6 %collective-permute-done.30.two_ref = f32[9,8,128]{2,1,0:T(8,128)S(1)} collective-permute-done((f32[9,8,128]{2,1,0:T(8,128)S(1)}, f32[9,8,128]{2,1,0:T(8,128)S(1)}, u32[]{:S(2)}, u32[]{:S(2)}) %collective-permute-start.30) | collective-permute-done | bytes 36896 | tf_op jit(solution)/shard_map/ppermute | solution.py:444
  (58 shorter events, 20.6 us)
Async XLA Ops:
  4.3 5.3 %collective-permute-start = (f32[17,8,128]{2,1,0:T(8,128)S(1)}, f32[17,8,128]{2,1,0:T(8,128)S(1)}, u32[]{:S(2)}, u32[]{:S(2)}) collective-permute-start(f32[17,8,128]{2,1,0:T(8,128)S(1)} %get-tuple-element.38.send_ref), channel_id=1, source_target_pairs={{0,1},{1,0},{2,3},{3,2},{4,5},{5,4},{6,7},{7,6},{8,9},{9,8},{10,11... | collective-permute-start | bytes 208904 | tf_op jit(solution)/shard_map/ppermute | solution.py:431
  4.4 5.1 %collective-permute-start.1 = (f32[2,8,128]{2,1,0:T(8,128)S(1)}, f32[2,8,128]{2,1,0:T(8,128)S(1)}, u32[]{:S(2)}, u32[]{:S(2)}) collective-permute-start(f32[2,8,128]{2,1,0:T(8,128)S(1)} %get-tuple-element.40.count_ref), channel_id=1, source_target_pairs={{224,0},{66,2},{68,4},{230,6},{0,32},{98,34},{100,36},{6,38},{32,6... | collective-permute-start | bytes 24584 | tf_op jit(solution)/shard_map/ppermute | solution.py:439
  9.6 5.9 %collective-permute-start.4 = (f32[17,8,128]{2,1,0:T(8,128)S(1)}, f32[17,8,128]{2,1,0:T(8,128)S(1)}, u32[]{:S(2)}, u32[]{:S(2)}) collective-permute-start(f32[17,8,128]{2,1,0:T(8,128)S(1)} %get-tuple-element.41.own_ref), channel_id=1, source_target_pairs={{0,24},{8,16},{16,8},{24,0},{1,25},{9,17},{17,9},{25,1},{2,26},{10... | collective-permute-start | bytes 208904 | tf_op jit(solution)/shard_map/ppermute | solution.py:444
  12.4 6.2 %collective-permute-start.3 = (f32[17,8,128]{2,1,0:T(8,128)S(1)}, f32[17,8,128]{2,1,0:T(8,128)S(1)}, u32[]{:S(2)}, u32[]{:S(2)}) collective-permute-start(f32[17,8,128]{2,1,0:T(8,128)S(1)} %get-tuple-element.41.own_ref), channel_id=1, source_target_pairs={{0,16},{8,24},{16,0},{24,8},{1,17},{9,25},{17,1},{25,9},{2,18},{10... | collective-permute-start | bytes 208904 | tf_op jit(solution)/shard_map/ppermute | solution.py:444
  13.2 5.4 %collective-permute-start.2 = (f32[17,8,128]{2,1,0:T(8,128)S(1)}, f32[17,8,128]{2,1,0:T(8,128)S(1)}, u32[]{:S(2)}, u32[]{:S(2)}) collective-permute-start(f32[17,8,128]{2,1,0:T(8,128)S(1)} %get-tuple-element.41.own_ref), channel_id=1, source_target_pairs={{0,8},{8,0},{16,24},{24,16},{1,9},{9,1},{17,25},{25,17},{2,10},{10... | collective-permute-start | bytes 208904 | tf_op jit(solution)/shard_map/ppermute | solution.py:444
  13.7 0.7 collective-permute-start.5
  18.6 9.2 %collective-permute-start.8 = (f32[19,8,128]{2,1,0:T(8,128)S(1)}, f32[19,8,128]{2,1,0:T(8,128)S(1)}, u32[]{:S(2)}, u32[]{:S(2)}) collective-permute-start(f32[19,8,128]{2,1,0:T(8,128)S(1)} %middle.1.own_ref), channel_id=1, source_target_pairs={{0,6},{2,4},{4,2},{6,0},{1,7},{3,5},{5,3},{7,1},{8,14},{10,12},{12... | collective-permute-start | bytes 233480 | tf_op jit(solution)/shard_map/ppermute | solution.py:444
  24.6 6.6 %collective-permute-start.7 = (f32[19,8,128]{2,1,0:T(8,128)S(1)}, f32[19,8,128]{2,1,0:T(8,128)S(1)}, u32[]{:S(2)}, u32[]{:S(2)}) collective-permute-start(f32[19,8,128]{2,1,0:T(8,128)S(1)} %middle.1.own_ref), channel_id=1, source_target_pairs={{0,4},{2,6},{4,0},{6,2},{1,5},{3,7},{5,1},{7,3},{8,12},{10,14},{12... | collective-permute-start | bytes 233480 | tf_op jit(solution)/shard_map/ppermute | solution.py:444
  27.1 4.4 %collective-permute-start.6 = (f32[19,8,128]{2,1,0:T(8,128)S(1)}, f32[19,8,128]{2,1,0:T(8,128)S(1)}, u32[]{:S(2)}, u32[]{:S(2)}) collective-permute-start(f32[19,8,128]{2,1,0:T(8,128)S(1)} %middle.1.own_ref), channel_id=1, source_target_pairs={{0,2},{2,0},{4,6},{6,4},{1,3},{3,1},{5,7},{7,5},{8,10},{10,8},{12,... | collective-permute-start | bytes 233480 | tf_op jit(solution)/shard_map/ppermute | solution.py:444
  31.6 1.3 %collective-permute-start.9 = (f32[9,8,128]{2,1,0:T(8,128)S(1)}, f32[9,8,128]{2,1,0:T(8,128)S(1)}, u32[]{:S(2)}, u32[]{:S(2)}) collective-permute-start(f32[9,8,128]{2,1,0:T(8,128)S(1)} %get-tuple-element.43.weighted_ref.own_ref), channel_id=1, source_target_pairs={{0,1},{1,0},{2,3},{3,2},{4,5},{5,4},{6,7},{7,6},{8,9},{9,8},{10,11... | collective-permute-start | bytes 110600 | tf_op jit(solution)/shard_map/ppermute | solution.py:431
  33.6 4.0 %collective-permute-start.10 = (f32[9,8,128]{2,1,0:T(8,128)S(1)}, f32[9,8,128]{2,1,0:T(8,128)S(1)}, u32[]{:S(2)}, u32[]{:S(2)}) collective-permute-start(f32[9,8,128]{2,1,0:T(8,128)S(1)} %get-tuple-element.49), channel_id=1, source_target_pairs={{0,32},{32,0},{64,96},{96,64},{128,160},{160,128},{192,224},{224,1... | collective-permute-start | bytes 110600 | tf_op jit(solution)/shard_map/ppermute | solution.py:444
  35.1 5.0 %collective-permute-start.11 = (f32[9,8,128]{2,1,0:T(8,128)S(1)}, f32[9,8,128]{2,1,0:T(8,128)S(1)}, u32[]{:S(2)}, u32[]{:S(2)}) collective-permute-start(f32[9,8,128]{2,1,0:T(8,128)S(1)} %get-tuple-element.50), channel_id=1, source_target_pairs={{0,64},{32,96},{64,0},{96,32},{128,192},{160,224},{192,128},{224,1... | collective-permute-start | bytes 110600 | tf_op jit(solution)/shard_map/ppermute | solution.py:444
  35.9 4.5 %collective-permute-start.12 = (f32[9,8,128]{2,1,0:T(8,128)S(1)}, f32[9,8,128]{2,1,0:T(8,128)S(1)}, u32[]{:S(2)}, u32[]{:S(2)}) collective-permute-start(f32[9,8,128]{2,1,0:T(8,128)S(1)} %get-tuple-element.51), channel_id=1, source_target_pairs={{0,96},{32,64},{64,32},{96,0},{128,224},{160,192},{192,160},{224,1... | collective-permute-start | bytes 110600 | tf_op jit(solution)/shard_map/ppermute | solution.py:444
  40.4 7.1 %collective-permute-start.13 = (f32[9,8,128]{2,1,0:T(8,128)S(1)}, f32[9,8,128]{2,1,0:T(8,128)S(1)}, u32[]{:S(2)}, u32[]{:S(2)}) collective-permute-start(f32[9,8,128]{2,1,0:T(8,128)S(1)} %add_half.2.refs_0_), channel_id=1, source_target_pairs={{0,224},{32,192},{64,160},{96,128},{128,96},{160,64},{192,32},{224... | collective-permute-start | bytes 110600 | tf_op jit(solution)/shard_map/ppermute | solution.py:451
  47.4 4.6 %collective-permute-start.16 = (f32[9,8,128]{2,1,0:T(8,128)S(1)}, f32[9,8,128]{2,1,0:T(8,128)S(1)}, u32[]{:S(2)}, u32[]{:S(2)}) collective-permute-start(f32[9,8,128]{2,1,0:T(8,128)S(1)} %add_tok.2.own_ref), channel_id=1, source_target_pairs={{0,96},{32,64},{64,32},{96,0},{128,224},{160,192},{192,160},{224,1... | collective-permute-start | bytes 110600 | tf_op jit(solution)/shard_map/ppermute | solution.py:444
  49.0 4.9 %collective-permute-start.15 = (f32[9,8,128]{2,1,0:T(8,128)S(1)}, f32[9,8,128]{2,1,0:T(8,128)S(1)}, u32[]{:S(2)}, u32[]{:S(2)}) collective-permute-start(f32[9,8,128]{2,1,0:T(8,128)S(1)} %add_tok.2.own_ref), channel_id=1, source_target_pairs={{0,64},{32,96},{64,0},{96,32},{128,192},{160,224},{192,128},{224,1... | collective-permute-start | bytes 110600 | tf_op jit(solution)/shard_map/ppermute | solution.py:444
  51.3 4.0 %collective-permute-start.14 = (f32[9,8,128]{2,1,0:T(8,128)S(1)}, f32[9,8,128]{2,1,0:T(8,128)S(1)}, u32[]{:S(2)}, u32[]{:S(2)}) collective-permute-start(f32[9,8,128]{2,1,0:T(8,128)S(1)} %add_tok.2.own_ref), channel_id=1, source_target_pairs={{0,32},{32,0},{64,96},{96,64},{128,160},{160,128},{192,224},{224,1... | collective-permute-start | bytes 110600 | tf_op jit(solution)/shard_map/ppermute | solution.py:444
  56.2 1.2 %collective-permute-start.17 = (f32[9,8,128]{2,1,0:T(8,128)S(1)}, f32[9,8,128]{2,1,0:T(8,128)S(1)}, u32[]{:S(2)}, u32[]{:S(2)}) collective-permute-start(f32[9,8,128]{2,1,0:T(8,128)S(1)} %get-tuple-element.58.send_ref), channel_id=1, source_target_pairs={{0,1},{1,0},{2,3},{3,2},{4,5},{5,4},{6,7},{7,6},{8,9},{9,8},{10,11... | collective-permute-start | bytes 110600 | tf_op jit(solution)/shard_map/ppermute | solution.py:431
  57.4 5.2 %collective-permute-start.20 = (f32[9,8,128]{2,1,0:T(8,128)S(1)}, f32[9,8,128]{2,1,0:T(8,128)S(1)}, u32[]{:S(2)}, u32[]{:S(2)}) collective-permute-start(f32[9,8,128]{2,1,0:T(8,128)S(1)} %add_core.1.refs_0_), channel_id=1, source_target_pairs={{0,24},{8,16},{16,8},{24,0},{1,25},{9,17},{17,9},{25,1},{2,26},{10... | collective-permute-start | bytes 110600 | tf_op jit(solution)/shard_map/ppermute | solution.py:444
  60.2 5.5 %collective-permute-start.19 = (f32[9,8,128]{2,1,0:T(8,128)S(1)}, f32[9,8,128]{2,1,0:T(8,128)S(1)}, u32[]{:S(2)}, u32[]{:S(2)}) collective-permute-start(f32[9,8,128]{2,1,0:T(8,128)S(1)} %add_core.1.refs_0_), channel_id=1, source_target_pairs={{0,16},{8,24},{16,0},{24,8},{1,17},{9,25},{17,1},{25,9},{2,18},{10... | collective-permute-start | bytes 110600 | tf_op jit(solution)/shard_map/ppermute | solution.py:444
  61.0 4.7 %collective-permute-start.18 = (f32[9,8,128]{2,1,0:T(8,128)S(1)}, f32[9,8,128]{2,1,0:T(8,128)S(1)}, u32[]{:S(2)}, u32[]{:S(2)}) collective-permute-start(f32[9,8,128]{2,1,0:T(8,128)S(1)} %add_core.1.refs_0_), channel_id=1, source_target_pairs={{0,8},{8,0},{16,24},{24,16},{1,9},{9,1},{17,25},{25,17},{2,10},{10... | collective-permute-start | bytes 110600 | tf_op jit(solution)/shard_map/ppermute | solution.py:444
  65.7 5.6 %collective-permute-start.23 = (f32[9,8,128]{2,1,0:T(8,128)S(1)}, f32[9,8,128]{2,1,0:T(8,128)S(1)}, u32[]{:S(2)}, u32[]{:S(2)}) collective-permute-start(f32[9,8,128]{2,1,0:T(8,128)S(1)} %add_x.1.refs_0_), channel_id=1, source_target_pairs={{0,6},{2,4},{4,2},{6,0},{1,7},{3,5},{5,3},{7,1},{8,14},{10,12},{12... | collective-permute-start | bytes 110600 | tf_op jit(solution)/shard_map/ppermute | solution.py:444
  67.8 5.5 %collective-permute-start.22 = (f32[9,8,128]{2,1,0:T(8,128)S(1)}, f32[9,8,128]{2,1,0:T(8,128)S(1)}, u32[]{:S(2)}, u32[]{:S(2)}) collective-permute-start(f32[9,8,128]{2,1,0:T(8,128)S(1)} %add_x.1.refs_0_), channel_id=1, source_target_pairs={{0,4},{2,6},{4,0},{6,2},{1,5},{3,7},{5,1},{7,3},{8,12},{10,14},{12... | collective-permute-start | bytes 110600 | tf_op jit(solution)/shard_map/ppermute | solution.py:444
  68.7 4.6 %collective-permute-start.21 = (f32[9,8,128]{2,1,0:T(8,128)S(1)}, f32[9,8,128]{2,1,0:T(8,128)S(1)}, u32[]{:S(2)}, u32[]{:S(2)}) collective-permute-start(f32[9,8,128]{2,1,0:T(8,128)S(1)} %add_x.1.refs_0_), channel_id=1, source_target_pairs={{0,2},{2,0},{4,6},{6,4},{1,3},{3,1},{5,7},{7,5},{8,10},{10,8},{12,... | collective-permute-start | bytes 110600 | tf_op jit(solution)/shard_map/ppermute | solution.py:444
  73.5 1.3 %collective-permute-start.24 = (f32[9,8,128]{2,1,0:T(8,128)S(1)}, f32[9,8,128]{2,1,0:T(8,128)S(1)}, u32[]{:S(2)}, u32[]{:S(2)}) collective-permute-start(f32[9,8,128]{2,1,0:T(8,128)S(1)} %get-tuple-element.62.weighted_ref.own_ref), channel_id=1, source_target_pairs={{0,1},{1,0},{2,3},{3,2},{4,5},{5,4},{6,7},{7,6},{8,9},{9,8},{10,11... | collective-permute-start | bytes 110600 | tf_op jit(solution)/shard_map/ppermute | solution.py:431
  75.5 4.2 %collective-permute-start.25 = (f32[9,8,128]{2,1,0:T(8,128)S(1)}, f32[9,8,128]{2,1,0:T(8,128)S(1)}, u32[]{:S(2)}, u32[]{:S(2)}) collective-permute-start(f32[9,8,128]{2,1,0:T(8,128)S(1)} %get-tuple-element.64), channel_id=1, source_target_pairs={{0,32},{32,0},{64,96},{96,64},{128,160},{160,128},{192,224},{224,1... | collective-permute-start | bytes 110600 | tf_op jit(solution)/shard_map/ppermute | solution.py:444
  76.2 5.0 %collective-permute-start.26 = (f32[9,8,128]{2,1,0:T(8,128)S(1)}, f32[9,8,128]{2,1,0:T(8,128)S(1)}, u32[]{:S(2)}, u32[]{:S(2)}) collective-permute-start(f32[9,8,128]{2,1,0:T(8,128)S(1)} %get-tuple-element.65), channel_id=1, source_target_pairs={{0,64},{32,96},{64,0},{96,32},{128,192},{160,224},{192,128},{224,1... | collective-permute-start | bytes 110600 | tf_op jit(solution)/shard_map/ppermute | solution.py:444
  78.2 4.2 %collective-permute-start.27 = (f32[9,8,128]{2,1,0:T(8,128)S(1)}, f32[9,8,128]{2,1,0:T(8,128)S(1)}, u32[]{:S(2)}, u32[]{:S(2)}) collective-permute-start(f32[9,8,128]{2,1,0:T(8,128)S(1)} %get-tuple-element.66), channel_id=1, source_target_pairs={{0,96},{32,64},{64,32},{96,0},{128,224},{160,192},{192,160},{224,1... | collective-permute-start | bytes 110600 | tf_op jit(solution)/shard_map/ppermute | solution.py:444
  82.4 7.2 %collective-permute-start.28 = (f32[9,8,128]{2,1,0:T(8,128)S(1)}, f32[9,8,128]{2,1,0:T(8,128)S(1)}, u32[]{:S(2)}, u32[]{:S(2)}) collective-permute-start(f32[9,8,128]{2,1,0:T(8,128)S(1)} %add_half.3.refs_0_), channel_id=1, source_target_pairs={{0,224},{32,192},{64,160},{96,128},{128,96},{160,64},{192,32},{224... | collective-permute-start | bytes 110600 | tf_op jit(solution)/shard_map/ppermute | solution.py:451
  89.6 4.3 %collective-permute-start.31 = (f32[9,8,128]{2,1,0:T(8,128)S(1)}, f32[9,8,128]{2,1,0:T(8,128)S(1)}, u32[]{:S(2)}, u32[]{:S(2)}) collective-permute-start(f32[9,8,128]{2,1,0:T(8,128)S(1)} %add_tok.3.own_ref), channel_id=1, source_target_pairs={{0,96},{32,64},{64,32},{96,0},{128,224},{160,192},{192,160},{224,1... | collective-permute-start | bytes 110600 | tf_op jit(solution)/shard_map/ppermute | solution.py:444
  90.7 4.9 %collective-permute-start.30 = (f32[9,8,128]{2,1,0:T(8,128)S(1)}, f32[9,8,128]{2,1,0:T(8,128)S(1)}, u32[]{:S(2)}, u32[]{:S(2)}) collective-permute-start(f32[9,8,128]{2,1,0:T(8,128)S(1)} %add_tok.3.own_ref), channel_id=1, source_target_pairs={{0,64},{32,96},{64,0},{96,32},{128,192},{160,224},{192,128},{224,1... | collective-permute-start | bytes 110600 | tf_op jit(solution)/shard_map/ppermute | solution.py:444
  92.6 4.0 %collective-permute-start.29 = (f32[9,8,128]{2,1,0:T(8,128)S(1)}, f32[9,8,128]{2,1,0:T(8,128)S(1)}, u32[]{:S(2)}, u32[]{:S(2)}) collective-permute-start(f32[9,8,128]{2,1,0:T(8,128)S(1)} %add_tok.3.own_ref), channel_id=1, source_target_pairs={{0,32},{32,0},{64,96},{96,64},{128,160},{160,128},{192,224},{224,1... | collective-permute-start | bytes 110600 | tf_op jit(solution)/shard_map/ppermute | solution.py:444
  (2 other events, 43.5 us)

commit v8 on v7

--- a/solution.py
+++ b/solution.py
@@ -271,13 +271,13 @@
 
 
 def image_other_kernel(
-    step, place_ref, other_ref, own_ref, high_ref, low_ref, before_ref, *piece_refs_and_left
+    step, wanted, place_ref, other_ref, own_ref, high_ref, low_ref, before_ref, *piece_refs_and_left
 ):
     *piece_refs, left_ref = piece_refs_and_left
     last = own_ref.shape[0] - 1
     curve = own_ref[last] + other_ref[last]
     left = put_together(other_ref, left_ref)
-    for d, piece_ref in enumerate(piece_refs):
+    for d, piece_ref in zip(wanted, piece_refs, strict=True):
         block = (place_ref[0] >> 1) ^ d
         at = pl.multiple_of(block * step, step)
         store_tiles(piece_ref, before_ref[block] + image_columns(at, step, left, high_ref, low_ref), curve)
@@ -502,9 +502,19 @@
             [put],
             cost=half_product,
         )(weighted, high_own, low_own)
-        return call(
-            with_step(image_other_kernel), "image_other", [SCALAR] + [ON_CHIP] * 5, [piece] * 4, [put]
-        )(place, other, weighted, high_other, low_other, before)
+
+        def image_pieces(wanted, name, cost=None):
+            return call(
+                functools.partial(image_other_kernel, step, wanted),
+                name,
+                [SCALAR] + [ON_CHIP] * 5,
+                [piece] * len(wanted),
+                [put],
+                cost=cost,
+            )(place, other, weighted, high_other, low_other, before)
+
+        pieces = image_pieces((1, 2, 3), "image_send")
+        return image_pieces((0,), "image_keep", half_product) + pieces
 
     pieces = sum_over_tok(*image(weighted))
 

time: 97.4 us -> 97.1 us (level)
  transfers between devices with their start and end apart: 32 -> 32, of which waited for: 24 -> 24; matrix products, arithmetic and copies ran while one was open for 0% -> 0% of each run, Pallas kernels for 7% -> 8%
where the time goes in v8:
time: 97.1 us; the launch traced here: 97 us
  starting transfers between devices  46.1 us (47%)
  waiting for transfers between devices  35.7 us (37%)
  Pallas kernels  14.4 us (15%)
    ppermute x24, starting transfers between devices, from_others(): lax.ppermute(v, axis, [(i, i ^ d + 1) for i in range(count)])  35.2 us
    ppermute x24, waiting for transfers between devices, from_others(): lax.ppermute(v, axis, [(i, i ^ d + 1) for i in range(count)])  28.1 us
    ppermute x2, starting transfers between devices, sum_over_tok(): lax.ppermute(own, 'tok', [(i, toks - 1 - i) for i in range(toks)])  7.94 us
    ppermute x2, waiting for transfers between devices, sum_over_tok(): lax.ppermute(own, 'tok', [(i, toks - 1 - i) for i in range(toks)])  6.27 us
    pallas_call x1, Pallas kernels, on_device(): call(with_step(first_other_kernel), 'first_other', [SCALAR] + [IN_HBM] *...  3.62 us
    pallas_call x1, Pallas kernels, on_device(): call(with_step(first_own_kernel), 'first_own', [SCALAR, ON_CHIP, ON_CHIP,...  3.13 us
    ppermute x2, starting transfers between devices, from_tok(): return lax.ppermute(value, ('tok', 'y'), pairs)  2.65 us
  transfers between devices with their start and end apart: 32, of which 24 were waited for; matrix products, arithmetic and copies ran while one was open for 0% of the time, Pallas kernels for 8%

profile of v8, /device:TPU:32, one launch (start us, length us, event | category | flops | bytes accessed | tf_op | source)
XLA Modules:
  0.0 97.0 jit_solution(587973005084418851)
XLA Ops:
  0.6 3.6 %first_other.1 = (f32[17,8,128]{2,1,0:T(8,128)S(1)}, f32[2,8,128]{2,1,0:T(8,128)S(1)}, bf16[64,2048]{1,0:T(8,128)(2,1)S(1)}, bf16[512,2048]{1,0:T(8,128)(2,1)S(1)}, bf16[512,2048]{1,0:T(8,128)(2,1)S(1)}) custom-call(s32[1]{0:T(128)} %bitcast.place_ref, s32[8,128]{1,0:T(8,128)} %bitcast.4, f32[16,2048]{1,0:T(8,128)} %weights_hbm.1, f32[16,2048]{1,0:T(8,128)} %right_ref.5, ...), custom_call_target="tpu_custom_call" | custom-call | tf_op jit(solution)/shard_map/first_other/pallas_call | solution.py:456
  4.4 2.0 %collective-permute-start.1 = (f32[2,8,128]{2,1,0:T(8,128)S(1)}, f32[2,8,128]{2,1,0:T(8,128)S(1)}, u32[]{:S(2)}, u32[]{:S(2)}) collective-permute-start(f32[2,8,128]{2,1,0:T(8,128)S(1)} %get-tuple-element.38.count_ref), channel_id=1, source_target_pairs={{224,0},{66,2},{68,4},{230,6},{0,32},{98,34},{100,36},{6,38},{32,6... | collective-permute-start | bytes 24584 | tf_op jit(solution)/shard_map/ppermute | solution.py:439
  6.4 3.1 %first_own.1 = (f32[17,8,128]{2,1,0:T(8,128)S(1)}, bf16[512,2048]{1,0:T(8,128)(2,1)S(1)}, bf16[512,2048]{1,0:T(8,128)(2,1)S(1)}) custom-call(s32[1]{0:T(128)} %bitcast.place_ref, bf16[64,2048]{1,0:T(8,128)(2,1)S(1)} %get-tuple-element.35.left_ref, f32[17,8,128]{2,1,0:T(8,128)S(1)} %get-tuple-element.36.send_ref, f32[1024,2048]{1,0:T(8,128)} %features_ref.3), custom_call_target="tpu_custom_call" | custom-call | flops 201326592 | bytes 4194304 | tf_op jit(solution)/shard_map/first_own/pallas_call | solution.py:473
  9.6 2.8 %collective-permute-start.4 = (f32[17,8,128]{2,1,0:T(8,128)S(1)}, f32[17,8,128]{2,1,0:T(8,128)S(1)}, u32[]{:S(2)}, u32[]{:S(2)}) collective-permute-start(f32[17,8,128]{2,1,0:T(8,128)S(1)} %get-tuple-element.39.own_ref), channel_id=1, source_target_pairs={{0,24},{8,16},{16,8},{24,0},{1,25},{9,17},{17,9},{25,1},{2,26},{10... | collective-permute-start | bytes 208904 | tf_op jit(solution)/shard_map/ppermute | solution.py:444
  14.4 1.1 %collective-permute-done.4.three_ref = f32[17,8,128]{2,1,0:T(8,128)S(1)} collective-permute-done((f32[17,8,128]{2,1,0:T(8,128)S(1)}, f32[17,8,128]{2,1,0:T(8,128)S(1)}, u32[]{:S(2)}, u32[]{:S(2)}) %collective-permute-start.4) | collective-permute-done | bytes 69664 | tf_op jit(solution)/shard_map/ppermute | solution.py:444
  15.5 3.1 %collective-permute-done.3.two_ref = f32[17,8,128]{2,1,0:T(8,128)S(1)} collective-permute-done((f32[17,8,128]{2,1,0:T(8,128)S(1)}, f32[17,8,128]{2,1,0:T(8,128)S(1)}, u32[]{:S(2)}, u32[]{:S(2)}) %collective-permute-start.3) | collective-permute-done | bytes 69664 | tf_op jit(solution)/shard_map/ppermute | solution.py:444
  18.6 6.0 %collective-permute-start.8 = (f32[19,8,128]{2,1,0:T(8,128)S(1)}, f32[19,8,128]{2,1,0:T(8,128)S(1)}, u32[]{:S(2)}, u32[]{:S(2)}) collective-permute-start(f32[19,8,128]{2,1,0:T(8,128)S(1)} %middle.1.own_ref), channel_id=1, source_target_pairs={{0,6},{2,4},{4,2},{6,0},{1,7},{3,5},{5,3},{7,1},{8,14},{10,12},{12... | collective-permute-start | bytes 233480 | tf_op jit(solution)/shard_map/ppermute | solution.py:444
  24.6 2.5 %collective-permute-start.7 = (f32[19,8,128]{2,1,0:T(8,128)S(1)}, f32[19,8,128]{2,1,0:T(8,128)S(1)}, u32[]{:S(2)}, u32[]{:S(2)}) collective-permute-start(f32[19,8,128]{2,1,0:T(8,128)S(1)} %middle.1.own_ref), channel_id=1, source_target_pairs={{0,4},{2,6},{4,0},{6,2},{1,5},{3,7},{5,1},{7,3},{8,12},{10,14},{12... | collective-permute-start | bytes 233480 | tf_op jit(solution)/shard_map/ppermute | solution.py:444
  27.8 3.4 %collective-permute-done.7.two_ref = f32[19,8,128]{2,1,0:T(8,128)S(1)} collective-permute-done((f32[19,8,128]{2,1,0:T(8,128)S(1)}, f32[19,8,128]{2,1,0:T(8,128)S(1)}, u32[]{:S(2)}, u32[]{:S(2)}) %collective-permute-start.7) | collective-permute-done | bytes 77856 | tf_op jit(solution)/shard_map/ppermute | solution.py:444
  33.5 1.5 %collective-permute-start.10 = (f32[9,8,128]{2,1,0:T(8,128)S(1)}, f32[9,8,128]{2,1,0:T(8,128)S(1)}, u32[]{:S(2)}, u32[]{:S(2)}) collective-permute-start(f32[9,8,128]{2,1,0:T(8,128)S(1)} %get-tuple-element.46), channel_id=1, source_target_pairs={{0,32},{32,0},{64,96},{96,64},{128,160},{160,128},{192,224},{224,1... | collective-permute-start | bytes 110600 | tf_op jit(solution)/shard_map/ppermute | solution.py:444
  35.8 1.2 %collective-permute-start.12 = (f32[9,8,128]{2,1,0:T(8,128)S(1)}, f32[9,8,128]{2,1,0:T(8,128)S(1)}, u32[]{:S(2)}, u32[]{:S(2)}) collective-permute-start(f32[9,8,128]{2,1,0:T(8,128)S(1)} %get-tuple-element.48), channel_id=1, source_target_pairs={{0,96},{32,64},{64,32},{96,0},{128,224},{160,192},{192,160},{224,1... | collective-permute-start | bytes 110600 | tf_op jit(solution)/shard_map/ppermute | solution.py:444
  37.4 2.5 %collective-permute-done.11.refs_2_ = f32[9,8,128]{2,1,0:T(8,128)S(1)} collective-permute-done((f32[9,8,128]{2,1,0:T(8,128)S(1)}, f32[9,8,128]{2,1,0:T(8,128)S(1)}, u32[]{:S(2)}, u32[]{:S(2)}) %collective-permute-start.11) | collective-permute-done | bytes 36896 | tf_op jit(solution)/shard_map/ppermute | solution.py:444
  40.2 3.9 %collective-permute-start.13 = (f32[9,8,128]{2,1,0:T(8,128)S(1)}, f32[9,8,128]{2,1,0:T(8,128)S(1)}, u32[]{:S(2)}, u32[]{:S(2)}) collective-permute-start(f32[9,8,128]{2,1,0:T(8,128)S(1)} %add_half.2.refs_0_), channel_id=1, source_target_pairs={{0,224},{32,192},{64,160},{96,128},{128,96},{160,64},{192,32},{224... | collective-permute-start | bytes 110600 | tf_op jit(solution)/shard_map/ppermute | solution.py:451
  44.1 3.2 %collective-permute-done.13.refs_1_ = f32[9,8,128]{2,1,0:T(8,128)S(1)} collective-permute-done((f32[9,8,128]{2,1,0:T(8,128)S(1)}, f32[9,8,128]{2,1,0:T(8,128)S(1)}, u32[]{:S(2)}, u32[]{:S(2)}) %collective-permute-start.13) | collective-permute-done | bytes 36896 | tf_op jit(solution)/shard_map/ppermute | solution.py:451
  47.3 1.5 %collective-permute-start.16 = (f32[9,8,128]{2,1,0:T(8,128)S(1)}, f32[9,8,128]{2,1,0:T(8,128)S(1)}, u32[]{:S(2)}, u32[]{:S(2)}) collective-permute-start(f32[9,8,128]{2,1,0:T(8,128)S(1)} %add_tok.2.own_ref), channel_id=1, source_target_pairs={{0,96},{32,64},{64,32},{96,0},{128,224},{160,192},{192,160},{224,1... | collective-permute-start | bytes 110600 | tf_op jit(solution)/shard_map/ppermute | solution.py:444
  48.8 2.3 %collective-permute-start.15 = (f32[9,8,128]{2,1,0:T(8,128)S(1)}, f32[9,8,128]{2,1,0:T(8,128)S(1)}, u32[]{:S(2)}, u32[]{:S(2)}) collective-permute-start(f32[9,8,128]{2,1,0:T(8,128)S(1)} %add_tok.2.own_ref), channel_id=1, source_target_pairs={{0,64},{32,96},{64,0},{96,32},{128,192},{160,224},{192,128},{224,1... | collective-permute-start | bytes 110600 | tf_op jit(solution)/shard_map/ppermute | solution.py:444
  51.9 1.8 %collective-permute-done.15.two_ref = f32[9,8,128]{2,1,0:T(8,128)S(1)} collective-permute-done((f32[9,8,128]{2,1,0:T(8,128)S(1)}, f32[9,8,128]{2,1,0:T(8,128)S(1)}, u32[]{:S(2)}, u32[]{:S(2)}) %collective-permute-start.15) | collective-permute-done | bytes 36896 | tf_op jit(solution)/shard_map/ppermute | solution.py:444
  53.7 1.4 %collective-permute-done.14.one_ref = f32[9,8,128]{2,1,0:T(8,128)S(1)} collective-permute-done((f32[9,8,128]{2,1,0:T(8,128)S(1)}, f32[9,8,128]{2,1,0:T(8,128)S(1)}, u32[]{:S(2)}, u32[]{:S(2)}) %collective-permute-start.14) | collective-permute-done | bytes 36896 | tf_op jit(solution)/shard_map/ppermute | solution.py:444
  57.3 2.8 %collective-permute-start.20 = (f32[9,8,128]{2,1,0:T(8,128)S(1)}, f32[9,8,128]{2,1,0:T(8,128)S(1)}, u32[]{:S(2)}, u32[]{:S(2)}) collective-permute-start(f32[9,8,128]{2,1,0:T(8,128)S(1)} %add_core.1.refs_0_), channel_id=1, source_target_pairs={{0,24},{8,16},{16,8},{24,0},{1,25},{9,17},{17,9},{25,1},{2,26},{10... | collective-permute-start | bytes 110600 | tf_op jit(solution)/shard_map/ppermute | solution.py:444
  61.4 1.1 %collective-permute-done.20.refs_3_ = f32[9,8,128]{2,1,0:T(8,128)S(1)} collective-permute-done((f32[9,8,128]{2,1,0:T(8,128)S(1)}, f32[9,8,128]{2,1,0:T(8,128)S(1)}, u32[]{:S(2)}, u32[]{:S(2)}) %collective-permute-start.20) | collective-permute-done | bytes 36896 | tf_op jit(solution)/shard_map/ppermute | solution.py:444
  62.5 3.1 %collective-permute-done.19.refs_2_ = f32[9,8,128]{2,1,0:T(8,128)S(1)} collective-permute-done((f32[9,8,128]{2,1,0:T(8,128)S(1)}, f32[9,8,128]{2,1,0:T(8,128)S(1)}, u32[]{:S(2)}, u32[]{:S(2)}) %collective-permute-start.19) | collective-permute-done | bytes 36896 | tf_op jit(solution)/shard_map/ppermute | solution.py:444
  65.6 2.1 %collective-permute-start.23 = (f32[9,8,128]{2,1,0:T(8,128)S(1)}, f32[9,8,128]{2,1,0:T(8,128)S(1)}, u32[]{:S(2)}, u32[]{:S(2)}) collective-permute-start(f32[9,8,128]{2,1,0:T(8,128)S(1)} %add_x.1.refs_0_), channel_id=1, source_target_pairs={{0,6},{2,4},{4,2},{6,0},{1,7},{3,5},{5,3},{7,1},{8,14},{10,12},{12... | collective-permute-start | bytes 110600 | tf_op jit(solution)/shard_map/ppermute | solution.py:444
  68.6 1.2 %collective-permute-start.21 = (f32[9,8,128]{2,1,0:T(8,128)S(1)}, f32[9,8,128]{2,1,0:T(8,128)S(1)}, u32[]{:S(2)}, u32[]{:S(2)}) collective-permute-start(f32[9,8,128]{2,1,0:T(8,128)S(1)} %add_x.1.refs_0_), channel_id=1, source_target_pairs={{0,2},{2,0},{4,6},{6,4},{1,3},{3,1},{5,7},{7,5},{8,10},{10,8},{12,... | collective-permute-start | bytes 110600 | tf_op jit(solution)/shard_map/ppermute | solution.py:444
  69.8 1.4 %collective-permute-done.23.refs_3_ = f32[9,8,128]{2,1,0:T(8,128)S(1)} collective-permute-done((f32[9,8,128]{2,1,0:T(8,128)S(1)}, f32[9,8,128]{2,1,0:T(8,128)S(1)}, u32[]{:S(2)}, u32[]{:S(2)}) %collective-permute-start.23) | collective-permute-done | bytes 36896 | tf_op jit(solution)/shard_map/ppermute | solution.py:444
  71.1 2.0 %collective-permute-done.22.refs_2_ = f32[9,8,128]{2,1,0:T(8,128)S(1)} collective-permute-done((f32[9,8,128]{2,1,0:T(8,128)S(1)}, f32[9,8,128]{2,1,0:T(8,128)S(1)}, u32[]{:S(2)}, u32[]{:S(2)}) %collective-permute-start.22) | collective-permute-done | bytes 36896 | tf_op jit(solution)/shard_map/ppermute | solution.py:444
  75.9 2.0 %collective-permute-start.26 = (f32[9,8,128]{2,1,0:T(8,128)S(1)}, f32[9,8,128]{2,1,0:T(8,128)S(1)}, u32[]{:S(2)}, u32[]{:S(2)}) collective-permute-start(f32[9,8,128]{2,1,0:T(8,128)S(1)} %get-tuple-element.61), channel_id=1, source_target_pairs={{0,64},{32,96},{64,0},{96,32},{128,192},{160,224},{192,128},{224,1... | collective-permute-start | bytes 110600 | tf_op jit(solution)/shard_map/ppermute | solution.py:444
  79.3 1.6 %collective-permute-done.26.refs_2_ = f32[9,8,128]{2,1,0:T(8,128)S(1)} collective-permute-done((f32[9,8,128]{2,1,0:T(8,128)S(1)}, f32[9,8,128]{2,1,0:T(8,128)S(1)}, u32[]{:S(2)}, u32[]{:S(2)}) %collective-permute-start.26) | collective-permute-done | bytes 36896 | tf_op jit(solution)/shard_map/ppermute | solution.py:444
  80.9 1.2 %collective-permute-done.27.refs_3_ = f32[9,8,128]{2,1,0:T(8,128)S(1)} collective-permute-done((f32[9,8,128]{2,1,0:T(8,128)S(1)}, f32[9,8,128]{2,1,0:T(8,128)S(1)}, u32[]{:S(2)}, u32[]{:S(2)}) %collective-permute-start.27) | collective-permute-done | bytes 36896 | tf_op jit(solution)/shard_map/ppermute | solution.py:444
  82.1 4.0 %collective-permute-start.28 = (f32[9,8,128]{2,1,0:T(8,128)S(1)}, f32[9,8,128]{2,1,0:T(8,128)S(1)}, u32[]{:S(2)}, u32[]{:S(2)}) collective-permute-start(f32[9,8,128]{2,1,0:T(8,128)S(1)} %add_half.3.refs_0_), channel_id=1, source_target_pairs={{0,224},{32,192},{64,160},{96,128},{128,96},{160,64},{192,32},{224... | collective-permute-start | bytes 110600 | tf_op jit(solution)/shard_map/ppermute | solution.py:451
  86.2 3.1 %collective-permute-done.28.refs_1_ = f32[9,8,128]{2,1,0:T(8,128)S(1)} collective-permute-done((f32[9,8,128]{2,1,0:T(8,128)S(1)}, f32[9,8,128]{2,1,0:T(8,128)S(1)}, u32[]{:S(2)}, u32[]{:S(2)}) %collective-permute-start.28) | collective-permute-done | bytes 36896 | tf_op jit(solution)/shard_map/ppermute | solution.py:451
  90.4 2.0 %collective-permute-start.30 = (f32[9,8,128]{2,1,0:T(8,128)S(1)}, f32[9,8,128]{2,1,0:T(8,128)S(1)}, u32[]{:S(2)}, u32[]{:S(2)}) collective-permute-start(f32[9,8,128]{2,1,0:T(8,128)S(1)} %add_tok.3.own_ref), channel_id=1, source_target_pairs={{0,64},{32,96},{64,0},{96,32},{128,192},{160,224},{192,128},{224,1... | collective-permute-start | bytes 110600 | tf_op jit(solution)/shard_map/ppermute | solution.py:444
  93.6 1.6 %collective-permute-done.30.two_ref = f32[9,8,128]{2,1,0:T(8,128)S(1)} collective-permute-done((f32[9,8,128]{2,1,0:T(8,128)S(1)}, f32[9,8,128]{2,1,0:T(8,128)S(1)}, u32[]{:S(2)}, u32[]{:S(2)}) %collective-permute-start.30) | collective-permute-done | bytes 36896 | tf_op jit(solution)/shard_map/ppermute | solution.py:444
  (60 shorter events, 20.3 us)
Async XLA Ops:
  4.3 5.3 %collective-permute-start = (f32[17,8,128]{2,1,0:T(8,128)S(1)}, f32[17,8,128]{2,1,0:T(8,128)S(1)}, u32[]{:S(2)}, u32[]{:S(2)}) collective-permute-start(f32[17,8,128]{2,1,0:T(8,128)S(1)} %get-tuple-element.36.send_ref), channel_id=1, source_target_pairs={{0,1},{1,0},{2,3},{3,2},{4,5},{5,4},{6,7},{7,6},{8,9},{9,8},{10,11... | collective-permute-start | bytes 208904 | tf_op jit(solution)/shard_map/ppermute | solution.py:431
  4.4 5.1 %collective-permute-start.1 = (f32[2,8,128]{2,1,0:T(8,128)S(1)}, f32[2,8,128]{2,1,0:T(8,128)S(1)}, u32[]{:S(2)}, u32[]{:S(2)}) collective-permute-start(f32[2,8,128]{2,1,0:T(8,128)S(1)} %get-tuple-element.38.count_ref), channel_id=1, source_target_pairs={{224,0},{66,2},{68,4},{230,6},{0,32},{98,34},{100,36},{6,38},{32,6... | collective-permute-start | bytes 24584 | tf_op jit(solution)/shard_map/ppermute | solution.py:439
  9.6 5.9 %collective-permute-start.4 = (f32[17,8,128]{2,1,0:T(8,128)S(1)}, f32[17,8,128]{2,1,0:T(8,128)S(1)}, u32[]{:S(2)}, u32[]{:S(2)}) collective-permute-start(f32[17,8,128]{2,1,0:T(8,128)S(1)} %get-tuple-element.39.own_ref), channel_id=1, source_target_pairs={{0,24},{8,16},{16,8},{24,0},{1,25},{9,17},{17,9},{25,1},{2,26},{10... | collective-permute-start | bytes 208904 | tf_op jit(solution)/shard_map/ppermute | solution.py:444
  12.4 6.2 %collective-permute-start.3 = (f32[17,8,128]{2,1,0:T(8,128)S(1)}, f32[17,8,128]{2,1,0:T(8,128)S(1)}, u32[]{:S(2)}, u32[]{:S(2)}) collective-permute-start(f32[17,8,128]{2,1,0:T(8,128)S(1)} %get-tuple-element.39.own_ref), channel_id=1, source_target_pairs={{0,16},{8,24},{16,0},{24,8},{1,17},{9,25},{17,1},{25,9},{2,18},{10... | collective-permute-start | bytes 208904 | tf_op jit(solution)/shard_map/ppermute | solution.py:444
  13.2 5.4 %collective-permute-start.2 = (f32[17,8,128]{2,1,0:T(8,128)S(1)}, f32[17,8,128]{2,1,0:T(8,128)S(1)}, u32[]{:S(2)}, u32[]{:S(2)}) collective-permute-start(f32[17,8,128]{2,1,0:T(8,128)S(1)} %get-tuple-element.39.own_ref), channel_id=1, source_target_pairs={{0,8},{8,0},{16,24},{24,16},{1,9},{9,1},{17,25},{25,17},{2,10},{10... | collective-permute-start | bytes 208904 | tf_op jit(solution)/shard_map/ppermute | solution.py:444
  13.7 0.7 collective-permute-start.5
  18.6 9.2 %collective-permute-start.8 = (f32[19,8,128]{2,1,0:T(8,128)S(1)}, f32[19,8,128]{2,1,0:T(8,128)S(1)}, u32[]{:S(2)}, u32[]{:S(2)}) collective-permute-start(f32[19,8,128]{2,1,0:T(8,128)S(1)} %middle.1.own_ref), channel_id=1, source_target_pairs={{0,6},{2,4},{4,2},{6,0},{1,7},{3,5},{5,3},{7,1},{8,14},{10,12},{12... | collective-permute-start | bytes 233480 | tf_op jit(solution)/shard_map/ppermute | solution.py:444
  24.6 6.6 %collective-permute-start.7 = (f32[19,8,128]{2,1,0:T(8,128)S(1)}, f32[19,8,128]{2,1,0:T(8,128)S(1)}, u32[]{:S(2)}, u32[]{:S(2)}) collective-permute-start(f32[19,8,128]{2,1,0:T(8,128)S(1)} %middle.1.own_ref), channel_id=1, source_target_pairs={{0,4},{2,6},{4,0},{6,2},{1,5},{3,7},{5,1},{7,3},{8,12},{10,14},{12... | collective-permute-start | bytes 233480 | tf_op jit(solution)/shard_map/ppermute | solution.py:444
  27.1 4.4 %collective-permute-start.6 = (f32[19,8,128]{2,1,0:T(8,128)S(1)}, f32[19,8,128]{2,1,0:T(8,128)S(1)}, u32[]{:S(2)}, u32[]{:S(2)}) collective-permute-start(f32[19,8,128]{2,1,0:T(8,128)S(1)} %middle.1.own_ref), channel_id=1, source_target_pairs={{0,2},{2,0},{4,6},{6,4},{1,3},{3,1},{5,7},{7,5},{8,10},{10,8},{12,... | collective-permute-start | bytes 233480 | tf_op jit(solution)/shard_map/ppermute | solution.py:444
  31.6 1.3 %collective-permute-start.9 = (f32[9,8,128]{2,1,0:T(8,128)S(1)}, f32[9,8,128]{2,1,0:T(8,128)S(1)}, u32[]{:S(2)}, u32[]{:S(2)}) collective-permute-start(f32[9,8,128]{2,1,0:T(8,128)S(1)} %get-tuple-element.41.weighted_ref.own_ref), channel_id=1, source_target_pairs={{0,1},{1,0},{2,3},{3,2},{4,5},{5,4},{6,7},{7,6},{8,9},{9,8},{10,11... | collective-permute-start | bytes 110600 | tf_op jit(solution)/shard_map/ppermute | solution.py:431
  33.5 4.0 %collective-permute-start.10 = (f32[9,8,128]{2,1,0:T(8,128)S(1)}, f32[9,8,128]{2,1,0:T(8,128)S(1)}, u32[]{:S(2)}, u32[]{:S(2)}) collective-permute-start(f32[9,8,128]{2,1,0:T(8,128)S(1)} %get-tuple-element.46), channel_id=1, source_target_pairs={{0,32},{32,0},{64,96},{96,64},{128,160},{160,128},{192,224},{224,1... | collective-permute-start | bytes 110600 | tf_op jit(solution)/shard_map/ppermute | solution.py:444
  34.9 5.0 %collective-permute-start.11 = (f32[9,8,128]{2,1,0:T(8,128)S(1)}, f32[9,8,128]{2,1,0:T(8,128)S(1)}, u32[]{:S(2)}, u32[]{:S(2)}) collective-permute-start(f32[9,8,128]{2,1,0:T(8,128)S(1)} %get-tuple-element.47), channel_id=1, source_target_pairs={{0,64},{32,96},{64,0},{96,32},{128,192},{160,224},{192,128},{224,1... | collective-permute-start | bytes 110600 | tf_op jit(solution)/shard_map/ppermute | solution.py:444
  35.8 4.4 %collective-permute-start.12 = (f32[9,8,128]{2,1,0:T(8,128)S(1)}, f32[9,8,128]{2,1,0:T(8,128)S(1)}, u32[]{:S(2)}, u32[]{:S(2)}) collective-permute-start(f32[9,8,128]{2,1,0:T(8,128)S(1)} %get-tuple-element.48), channel_id=1, source_target_pairs={{0,96},{32,64},{64,32},{96,0},{128,224},{160,192},{192,160},{224,1... | collective-permute-start | bytes 110600 | tf_op jit(solution)/shard_map/ppermute | solution.py:444
  40.2 7.1 %collective-permute-start.13 = (f32[9,8,128]{2,1,0:T(8,128)S(1)}, f32[9,8,128]{2,1,0:T(8,128)S(1)}, u32[]{:S(2)}, u32[]{:S(2)}) collective-permute-start(f32[9,8,128]{2,1,0:T(8,128)S(1)} %add_half.2.refs_0_), channel_id=1, source_target_pairs={{0,224},{32,192},{64,160},{96,128},{128,96},{160,64},{192,32},{224... | collective-permute-start | bytes 110600 | tf_op jit(solution)/shard_map/ppermute | solution.py:451
  47.3 4.6 %collective-permute-start.16 = (f32[9,8,128]{2,1,0:T(8,128)S(1)}, f32[9,8,128]{2,1,0:T(8,128)S(1)}, u32[]{:S(2)}, u32[]{:S(2)}) collective-permute-start(f32[9,8,128]{2,1,0:T(8,128)S(1)} %add_tok.2.own_ref), channel_id=1, source_target_pairs={{0,96},{32,64},{64,32},{96,0},{128,224},{160,192},{192,160},{224,1... | collective-permute-start | bytes 110600 | tf_op jit(solution)/shard_map/ppermute | solution.py:444
  48.8 4.9 %collective-permute-start.15 = (f32[9,8,128]{2,1,0:T(8,128)S(1)}, f32[9,8,128]{2,1,0:T(8,128)S(1)}, u32[]{:S(2)}, u32[]{:S(2)}) collective-permute-start(f32[9,8,128]{2,1,0:T(8,128)S(1)} %add_tok.2.own_ref), channel_id=1, source_target_pairs={{0,64},{32,96},{64,0},{96,32},{128,192},{160,224},{192,128},{224,1... | collective-permute-start | bytes 110600 | tf_op jit(solution)/shard_map/ppermute | solution.py:444
  51.1 4.0 %collective-permute-start.14 = (f32[9,8,128]{2,1,0:T(8,128)S(1)}, f32[9,8,128]{2,1,0:T(8,128)S(1)}, u32[]{:S(2)}, u32[]{:S(2)}) collective-permute-start(f32[9,8,128]{2,1,0:T(8,128)S(1)} %add_tok.2.own_ref), channel_id=1, source_target_pairs={{0,32},{32,0},{64,96},{96,64},{128,160},{160,128},{192,224},{224,1... | collective-permute-start | bytes 110600 | tf_op jit(solution)/shard_map/ppermute | solution.py:444
  56.1 1.2 %collective-permute-start.17 = (f32[9,8,128]{2,1,0:T(8,128)S(1)}, f32[9,8,128]{2,1,0:T(8,128)S(1)}, u32[]{:S(2)}, u32[]{:S(2)}) collective-permute-start(f32[9,8,128]{2,1,0:T(8,128)S(1)} %get-tuple-element.55.send_ref), channel_id=1, source_target_pairs={{0,1},{1,0},{2,3},{3,2},{4,5},{5,4},{6,7},{7,6},{8,9},{9,8},{10,11... | collective-permute-start | bytes 110600 | tf_op jit(solution)/shard_map/ppermute | solution.py:431
  57.3 5.2 %collective-permute-start.20 = (f32[9,8,128]{2,1,0:T(8,128)S(1)}, f32[9,8,128]{2,1,0:T(8,128)S(1)}, u32[]{:S(2)}, u32[]{:S(2)}) collective-permute-start(f32[9,8,128]{2,1,0:T(8,128)S(1)} %add_core.1.refs_0_), channel_id=1, source_target_pairs={{0,24},{8,16},{16,8},{24,0},{1,25},{9,17},{17,9},{25,1},{2,26},{10... | collective-permute-start | bytes 110600 | tf_op jit(solution)/shard_map/ppermute | solution.py:444
  60.1 5.5 %collective-permute-start.19 = (f32[9,8,128]{2,1,0:T(8,128)S(1)}, f32[9,8,128]{2,1,0:T(8,128)S(1)}, u32[]{:S(2)}, u32[]{:S(2)}) collective-permute-start(f32[9,8,128]{2,1,0:T(8,128)S(1)} %add_core.1.refs_0_), channel_id=1, source_target_pairs={{0,16},{8,24},{16,0},{24,8},{1,17},{9,25},{17,1},{25,9},{2,18},{10... | collective-permute-start | bytes 110600 | tf_op jit(solution)/shard_map/ppermute | solution.py:444
  60.9 4.7 %collective-permute-start.18 = (f32[9,8,128]{2,1,0:T(8,128)S(1)}, f32[9,8,128]{2,1,0:T(8,128)S(1)}, u32[]{:S(2)}, u32[]{:S(2)}) collective-permute-start(f32[9,8,128]{2,1,0:T(8,128)S(1)} %add_core.1.refs_0_), channel_id=1, source_target_pairs={{0,8},{8,0},{16,24},{24,16},{1,9},{9,1},{17,25},{25,17},{2,10},{10... | collective-permute-start | bytes 110600 | tf_op jit(solution)/shard_map/ppermute | solution.py:444
  65.6 5.6 %collective-permute-start.23 = (f32[9,8,128]{2,1,0:T(8,128)S(1)}, f32[9,8,128]{2,1,0:T(8,128)S(1)}, u32[]{:S(2)}, u32[]{:S(2)}) collective-permute-start(f32[9,8,128]{2,1,0:T(8,128)S(1)} %add_x.1.refs_0_), channel_id=1, source_target_pairs={{0,6},{2,4},{4,2},{6,0},{1,7},{3,5},{5,3},{7,1},{8,14},{10,12},{12... | collective-permute-start | bytes 110600 | tf_op jit(solution)/shard_map/ppermute | solution.py:444
  67.7 5.5 %collective-permute-start.22 = (f32[9,8,128]{2,1,0:T(8,128)S(1)}, f32[9,8,128]{2,1,0:T(8,128)S(1)}, u32[]{:S(2)}, u32[]{:S(2)}) collective-permute-start(f32[9,8,128]{2,1,0:T(8,128)S(1)} %add_x.1.refs_0_), channel_id=1, source_target_pairs={{0,4},{2,6},{4,0},{6,2},{1,5},{3,7},{5,1},{7,3},{8,12},{10,14},{12... | collective-permute-start | bytes 110600 | tf_op jit(solution)/shard_map/ppermute | solution.py:444
  68.6 4.6 %collective-permute-start.21 = (f32[9,8,128]{2,1,0:T(8,128)S(1)}, f32[9,8,128]{2,1,0:T(8,128)S(1)}, u32[]{:S(2)}, u32[]{:S(2)}) collective-permute-start(f32[9,8,128]{2,1,0:T(8,128)S(1)} %add_x.1.refs_0_), channel_id=1, source_target_pairs={{0,2},{2,0},{4,6},{6,4},{1,3},{3,1},{5,7},{7,5},{8,10},{10,8},{12,... | collective-permute-start | bytes 110600 | tf_op jit(solution)/shard_map/ppermute | solution.py:444
  73.3 1.3 %collective-permute-start.24 = (f32[9,8,128]{2,1,0:T(8,128)S(1)}, f32[9,8,128]{2,1,0:T(8,128)S(1)}, u32[]{:S(2)}, u32[]{:S(2)}) collective-permute-start(f32[9,8,128]{2,1,0:T(8,128)S(1)} %get-tuple-element.59.weighted_ref.own_ref), channel_id=1, source_target_pairs={{0,1},{1,0},{2,3},{3,2},{4,5},{5,4},{6,7},{7,6},{8,9},{9,8},{10,11... | collective-permute-start | bytes 110600 | tf_op jit(solution)/shard_map/ppermute | solution.py:431
  75.2 4.2 %collective-permute-start.25 = (f32[9,8,128]{2,1,0:T(8,128)S(1)}, f32[9,8,128]{2,1,0:T(8,128)S(1)}, u32[]{:S(2)}, u32[]{:S(2)}) collective-permute-start(f32[9,8,128]{2,1,0:T(8,128)S(1)} %get-tuple-element.60), channel_id=1, source_target_pairs={{0,32},{32,0},{64,96},{96,64},{128,160},{160,128},{192,224},{224,1... | collective-permute-start | bytes 110600 | tf_op jit(solution)/shard_map/ppermute | solution.py:444
  75.9 5.0 %collective-permute-start.26 = (f32[9,8,128]{2,1,0:T(8,128)S(1)}, f32[9,8,128]{2,1,0:T(8,128)S(1)}, u32[]{:S(2)}, u32[]{:S(2)}) collective-permute-start(f32[9,8,128]{2,1,0:T(8,128)S(1)} %get-tuple-element.61), channel_id=1, source_target_pairs={{0,64},{32,96},{64,0},{96,32},{128,192},{160,224},{192,128},{224,1... | collective-permute-start | bytes 110600 | tf_op jit(solution)/shard_map/ppermute | solution.py:444
  77.9 4.2 %collective-permute-start.27 = (f32[9,8,128]{2,1,0:T(8,128)S(1)}, f32[9,8,128]{2,1,0:T(8,128)S(1)}, u32[]{:S(2)}, u32[]{:S(2)}) collective-permute-start(f32[9,8,128]{2,1,0:T(8,128)S(1)} %get-tuple-element.62), channel_id=1, source_target_pairs={{0,96},{32,64},{64,32},{96,0},{128,224},{160,192},{192,160},{224,1... | collective-permute-start | bytes 110600 | tf_op jit(solution)/shard_map/ppermute | solution.py:444
  82.1 7.2 %collective-permute-start.28 = (f32[9,8,128]{2,1,0:T(8,128)S(1)}, f32[9,8,128]{2,1,0:T(8,128)S(1)}, u32[]{:S(2)}, u32[]{:S(2)}) collective-permute-start(f32[9,8,128]{2,1,0:T(8,128)S(1)} %add_half.3.refs_0_), channel_id=1, source_target_pairs={{0,224},{32,192},{64,160},{96,128},{128,96},{160,64},{192,32},{224... | collective-permute-start | bytes 110600 | tf_op jit(solution)/shard_map/ppermute | solution.py:451
  89.3 4.3 %collective-permute-start.31 = (f32[9,8,128]{2,1,0:T(8,128)S(1)}, f32[9,8,128]{2,1,0:T(8,128)S(1)}, u32[]{:S(2)}, u32[]{:S(2)}) collective-permute-start(f32[9,8,128]{2,1,0:T(8,128)S(1)} %add_tok.3.own_ref), channel_id=1, source_target_pairs={{0,96},{32,64},{64,32},{96,0},{128,224},{160,192},{192,160},{224,1... | collective-permute-start | bytes 110600 | tf_op jit(solution)/shard_map/ppermute | solution.py:444
  90.4 4.9 %collective-permute-start.30 = (f32[9,8,128]{2,1,0:T(8,128)S(1)}, f32[9,8,128]{2,1,0:T(8,128)S(1)}, u32[]{:S(2)}, u32[]{:S(2)}) collective-permute-start(f32[9,8,128]{2,1,0:T(8,128)S(1)} %add_tok.3.own_ref), channel_id=1, source_target_pairs={{0,64},{32,96},{64,0},{96,32},{128,192},{160,224},{192,128},{224,1... | collective-permute-start | bytes 110600 | tf_op jit(solution)/shard_map/ppermute | solution.py:444
  92.3 4.0 %collective-permute-start.29 = (f32[9,8,128]{2,1,0:T(8,128)S(1)}, f32[9,8,128]{2,1,0:T(8,128)S(1)}, u32[]{:S(2)}, u32[]{:S(2)}) collective-permute-start(f32[9,8,128]{2,1,0:T(8,128)S(1)} %add_tok.3.own_ref), channel_id=1, source_target_pairs={{0,32},{32,0},{64,96},{96,64},{128,160},{160,128},{192,224},{224,1... | collective-permute-start | bytes 110600 | tf_op jit(solution)/shard_map/ppermute | solution.py:444
  (2 other events, 40.5 us)
